TPU v7x, 128 devices: a whole 4x4x4 slice. The times are simulated.
128 devices in a mesh: ulysses: 8 (over y_hi, x), blk: 16 (over z, y_lo, core).
Axes of the slice: x: 4, y: 4 (y_hi: 2, y_lo: 2; y = y_hi * 2 + y_lo), z: 4, core: 2. Of those that a mesh axis runs over, the one named last changes fastest.
Arguments:
- tokens: bfloat16 [16384, 2048], P(('ulysses', 'blk')), may hold values from -6 to 6
- cotangent: bfloat16 [16384, 2048], P(('ulysses', 'blk')), may hold values from -6 to 6
- doc_ids: int32 [128], replicated, may hold values from 0 to 20, never falling along the last dimension, each value on 1 to 16 neighbouring positions
- ln1_gain: bfloat16 [2048], P('blk'), may hold values from 0.099609375 to 1.8984375
- ln1_shift: bfloat16 [2048], P('blk'), may hold values from -1.75 to 1.75
- w_qkv: bfloat16 [2048, 3, 2048], P('blk', None, 'ulysses'), may hold values from -0.125 to 0.125
- b_qkv: bfloat16 [3, 2048], P(None, ('ulysses', 'blk')), may hold values from -0.625 to 0.625
- w_out: bfloat16 [2048, 2048], P('ulysses', 'blk'), may hold values from -0.5 to 0.5
- ln2_gain: bfloat16 [2048], P('blk'), may hold values from 0.099609375 to 1.8984375
- ln2_shift: bfloat16 [2048], P('blk'), may hold values from -1.75 to 1.75
- w_gate: bfloat16 [2048, 5632], P('blk', 'ulysses'), may hold values from -0.125 to 0.125
- w_up: bfloat16 [2048, 5632], P('blk', 'ulysses'), may hold values from -0.125 to 0.125
- w_down: bfloat16 [5632, 2048], P('ulysses', 'blk'), may hold values from -0.15625 to 0.15625
Outputs:
- mixed: bfloat16 [16384, 2048], P(('ulysses', 'blk'))
- input_grad: float32 [16384, 2048], P(('ulysses', 'blk'))
- ln1_gain_grad: float32 [2048], P(('ulysses', 'blk'))
- ln1_shift_grad: float32 [2048], P(('ulysses', 'blk'))
- w_qkv_grad: float32 [2048, 3, 2048], P('blk', None, 'ulysses')
- b_qkv_grad: float32 [3, 2048], P(None, ('ulysses', 'blk'))
- w_out_grad: float32 [2048, 2048], P('ulysses', 'blk')
- ln2_gain_grad: float32 [2048], P(('ulysses', 'blk'))
- ln2_shift_grad: float32 [2048], P(('ulysses', 'blk'))
- w_gate_grad: float32 [2048, 5632], P('blk', 'ulysses')
- w_up_grad: float32 [2048, 5632], P('blk', 'ulysses')
- w_down_grad: float32 [5632, 2048], P('ulysses', 'blk')
Inputs may be any that keep to these rules, and one draw needn't show every extreme that they name: `doc_ids`: document numbers never fall along the blocks; each of the 21 documents covers 1 to 16 consecutive blocks, one exactly 16.
All inputs are finite; a program needn't handle non-finite values.
Results may differ from a plain program's by a relative error of at most 0.035.
Values may be sent and summed in bfloat16 or wider, within the bound.
No kernel may reach another device: no remote copies, remote signals or barrier semaphores. Data moves between devices by JAX's collectives and lax.ppermute only.
A program may use at most 128 MiB of HBM per device.

v0:
```python
import jax
import jax.numpy as jnp
from jax import lax
from jax.sharding import PartitionSpec as P

D = 2048
HEADS = 32
HEAD_DIM = 64
ROT = 16
BLK_TOK = 128


eps = 1e-05
rope_base = 10000.0
masked_score = -1e30
contract_cols = (((1,), (1,)), ((), ()))
contract_rows = (((0,), (0,)), ((), ()))


def from_behind(block, axis, distance):
    devices = range(lax.axis_size(axis))
    route = [((i - distance) % len(devices), i) for i in devices]
    return lax.ppermute(block, axis, route)


def rotary_tables(positions):
    halfway = ROT // 2
    counter = jnp.arange(halfway, dtype=jnp.float32)
    frequency = rope_base ** (-2.0 * counter / ROT)
    angles = positions.astype(jnp.float32)[:, None] * frequency[None, :]
    return (jnp.concatenate([jnp.cos(angles)] * 2, -1), jnp.concatenate([jnp.sin(angles)] * 2, -1))


def rotate(values, cosine, sine):
    halfway = ROT // 2
    turning = values[..., :ROT]
    turned = jnp.concatenate([-turning[..., halfway:], turning[..., :halfway]], -1)
    rotated = turning * cosine[:, None, :] + turned * sine[:, None, :]
    return jnp.concatenate([rotated, values[..., ROT:]], -1)


def layer_stats(values):
    centred = values - jnp.mean(values, -1, keepdims=True)
    inverse = lax.rsqrt(jnp.mean(centred * centred, -1, keepdims=True) + eps)
    return (centred * inverse, inverse)


def norm_back(grad_normed, unit, inverse, gain):
    grad_unit = grad_normed * gain
    centred_grad = (
        grad_unit
        - jnp.mean(grad_unit, -1, keepdims=True)
        - unit * jnp.mean(grad_unit * unit, -1, keepdims=True)
    )
    return (inverse * centred_grad, jnp.sum(grad_normed * unit, 0), jnp.sum(grad_normed, 0))


def stream_tables(doc_ids, group_size, cycle_size, local_rows):
    blocks = doc_ids.shape[0]
    first_block = jnp.sum((doc_ids[None, :] < doc_ids[:, None]).astype(jnp.int32), axis=1)
    layout = (group_size, cycle_size, local_rows)
    token_doc = jnp.broadcast_to(doc_ids[:, None], (blocks, BLK_TOK)).reshape(layout)
    block_start = jnp.broadcast_to((first_block * BLK_TOK)[:, None], (blocks, BLK_TOK)).reshape(
        layout
    )
    token_index = jnp.arange(blocks * BLK_TOK, dtype=jnp.int32).reshape(layout)
    return (token_doc, token_index, token_index - block_start)


def pick_slot(table, source):
    return lax.dynamic_index_in_dim(table, source, 1, keepdims=False)


def band(values, offset, bands, fill):
    depth = bands + 1
    padded = jnp.concatenate([jnp.full((depth,) + values.shape[1:], fill, values.dtype), values], 0)
    pieces = lax.dynamic_slice_in_dim(padded, depth - offset - 0, values.shape[0], 0)
    return pieces


def unband(grads, offset, bands):
    rows_each = grads.shape[1] // bands
    depth = bands + 1
    total = jnp.zeros((grads.shape[0], rows_each) + grads.shape[2:], grads.dtype)
    piece = grads[:, 0 * rows_each : 1 * rows_each]
    padded = jnp.concatenate([piece, jnp.zeros((depth,) + piece.shape[1:], piece.dtype)], 0)
    total = total + lax.dynamic_slice_in_dim(padded, offset + 0, grads.shape[0], 0)
    return total


def local(
    tokens,
    cotangent,
    doc_ids,
    ln1_gain,
    ln1_shift,
    w_qkv,
    b_qkv,
    w_out,
    ln2_gain,
    ln2_shift,
    w_gate,
    w_up,
    w_down,
):
    group_size = lax.axis_size("ulysses")
    cycle_size = lax.axis_size("blk")
    cycle_slot = lax.axis_index("blk")
    local_rows = tokens.shape[0]
    group_rows = group_size * local_rows
    head_count = HEADS // group_size
    head_width = head_count * HEAD_DIM
    score_scale = HEAD_DIM ** (-0.5)
    reach = (cycle_size * local_rows - 1 + local_rows - BLK_TOK) // local_rows
    local_bands = reach // cycle_size + 1
    cycle_bands = (reach - 1) // cycle_size + 1
    spanned = (group_size, local_rows, head_width)
    heads_shape = (group_rows, head_count, HEAD_DIM)
    fetched = (
        lax.all_gather(ln1_gain, "blk", axis=0, tiled=True),
        lax.all_gather(ln1_shift, "blk", axis=0, tiled=True),
        lax.all_gather(ln2_gain, "blk", axis=0, tiled=True),
        lax.all_gather(ln2_shift, "blk", axis=0, tiled=True),
        lax.all_gather(w_qkv, "blk", axis=0, tiled=True),
        lax.all_gather(b_qkv, "blk", axis=1, tiled=True),
        lax.all_gather(w_out, "blk", axis=1, tiled=True),
        lax.all_gather(w_gate, "blk", axis=0, tiled=True),
        lax.all_gather(w_up, "blk", axis=0, tiled=True),
        lax.all_gather(w_down, "blk", axis=1, tiled=True),
    )
    gain_one = fetched[0].astype(jnp.float32)
    shift_one = fetched[1].astype(jnp.float32)
    gain_two = fetched[2].astype(jnp.float32)
    shift_two = fetched[3].astype(jnp.float32)
    qkv_full = fetched[4].reshape(D, 3 * head_width)
    bias_full = fetched[5].reshape(3 * head_width).astype(jnp.float32)
    out_full = fetched[6]
    gate_full = fetched[7]
    up_full = fetched[8]
    down_full = fetched[9]
    token_doc, token_index, token_pos = stream_tables(doc_ids, group_size, cycle_size, local_rows)
    query_doc = pick_slot(token_doc, cycle_slot)
    query_index = pick_slot(token_index, cycle_slot)
    cosine, sine = rotary_tables(pick_slot(token_pos, cycle_slot).reshape(group_rows))
    inputs = tokens.astype(jnp.float32)
    unit_one, inverse_one = layer_stats(inputs)
    normed_one = (unit_one * gain_one + shift_one).astype(jnp.bfloat16)
    group_normed, group_cot = (
        lax.all_gather(normed_one, "ulysses", axis=0, tiled=True),
        lax.all_gather(cotangent, "ulysses", axis=0, tiled=True),
    )
    joint = jnp.dot(group_normed, qkv_full, preferred_element_type=jnp.float32) + bias_full
    joint = joint.reshape(group_rows, 3, head_count, HEAD_DIM)
    query_all = rotate(joint[:, 0], cosine, sine).astype(jnp.bfloat16).reshape(spanned)
    key_all = rotate(joint[:, 1], cosine, sine).astype(jnp.bfloat16).reshape(spanned)
    value_all = joint[:, 2].astype(jnp.bfloat16).reshape(spanned)

    def block_mask(source, offset, bands):
        key_doc = band(pick_slot(token_doc, source), offset, bands, -1)
        key_index = band(pick_slot(token_index, source), offset, bands, 0)
        return (query_doc[:, :, None] == key_doc[:, None, :]) & (
            key_index[:, None, :] <= query_index[:, :, None]
        )

    def head_scores(keys_band, head_num, allowed):
        columns = slice(head_num * HEAD_DIM, (head_num + 1) * HEAD_DIM)
        scores = (
            jnp.einsum(
                "cqd,ckd->cqk",
                query_all[..., columns],
                keys_band[..., columns],
                preferred_element_type=jnp.float32,
            )
            * score_scale
        )
        return jnp.where(allowed, scores, masked_score)

    def attend_block(state, keys, values, source, offset, bands):
        maxima, totals, sums = state
        allowed = block_mask(source, offset, bands)
        keys_band = band(keys, offset, bands, 0)
        values_band = band(values, offset, bands, 0)
        new_maxima, new_totals, new_sums = ([], [], [])
        for head_num in range(head_count):
            columns = slice(head_num * HEAD_DIM, (head_num + 1) * HEAD_DIM)
            scores = head_scores(keys_band, head_num, allowed)
            top_score = jnp.maximum(maxima[head_num], jnp.max(scores, -1))
            weights_e = jnp.where(allowed, jnp.exp(scores - top_score[..., None]), 0.0)
            rescale = jnp.exp(maxima[head_num] - top_score)
            new_maxima.append(top_score)
            new_totals.append(totals[head_num] * rescale + jnp.sum(weights_e, -1))
            carried = jnp.einsum(
                "cqk,ckd->cqd",
                weights_e.astype(jnp.bfloat16),
                values_band[..., columns],
                preferred_element_type=jnp.float32,
            )
            new_sums.append(sums[head_num] * rescale[..., None] + carried)
        return (jnp.stack(new_maxima), jnp.stack(new_totals), jnp.stack(new_sums))

    empty_state = (
        jnp.full((head_count, group_size, local_rows), masked_score, jnp.float32),
        jnp.zeros((head_count, group_size, local_rows), jnp.float32),
        jnp.zeros((head_count, group_size, local_rows, HEAD_DIM), jnp.float32),
    )
    state = attend_block(empty_state, key_all, value_all, cycle_slot, 0, local_bands)

    def cycle_step(step_num, keys, values, inner):
        keys, values = from_behind((keys, values), "blk", 1)
        source = (cycle_slot - step_num) % cycle_size
        offset = (source > cycle_slot).astype(jnp.int32)
        return (keys, values, attend_block(inner, keys, values, source, offset, cycle_bands))

    def cycle_forward(step_num, carry):
        keys, values, inner = carry
        return cycle_step(step_num, keys, values, inner)

    state = lax.fori_loop(1, cycle_size, cycle_forward, (key_all, value_all, state))[2]
    maxima, totals, sums = state
    attended = (sums / totals[..., None]).transpose(1, 2, 0, 3).reshape(group_rows, head_width)
    attended_low = attended.astype(jnp.bfloat16)
    log_total = maxima + jnp.log(totals)
    middle = inputs + lax.psum_scatter(
        jnp.dot(attended_low, out_full, preferred_element_type=jnp.float32).astype(jnp.bfloat16),
        "ulysses",
        scatter_dimension=0,
        tiled=True,
    ).astype(jnp.float32)
    unit_two, inverse_two = layer_stats(middle)
    normed_two = (unit_two * gain_two + shift_two).astype(jnp.bfloat16)
    group_two = lax.all_gather(normed_two, "ulysses", axis=0, tiled=True)
    gate_pre = jnp.dot(group_two, gate_full, preferred_element_type=jnp.float32)
    up_pre = jnp.dot(group_two, up_full, preferred_element_type=jnp.float32)
    sigmoid_g = jax.nn.sigmoid(gate_pre)
    silu_g = gate_pre * sigmoid_g
    active = (silu_g * up_pre).astype(jnp.bfloat16)
    mixed = (
        middle
        + lax.psum_scatter(
            jnp.dot(active, down_full, preferred_element_type=jnp.float32).astype(jnp.bfloat16),
            "ulysses",
            scatter_dimension=0,
            tiled=True,
        ).astype(jnp.float32)
    ).astype(jnp.bfloat16)
    again = (
        lax.all_gather(ln1_gain, "blk", axis=0, tiled=True),
        lax.all_gather(ln2_gain, "blk", axis=0, tiled=True),
        lax.all_gather(w_qkv, "blk", axis=0, tiled=True),
        lax.all_gather(w_out, "blk", axis=1, tiled=True),
        lax.all_gather(w_gate, "blk", axis=0, tiled=True),
        lax.all_gather(w_up, "blk", axis=0, tiled=True),
        lax.all_gather(w_down, "blk", axis=1, tiled=True),
    )
    gain_one = again[0].astype(jnp.float32)
    gain_two = again[1].astype(jnp.float32)
    qkv_full = again[2].reshape(D, 3 * head_width)
    out_full = again[3]
    gate_full = again[4]
    up_full = again[5]
    down_full = again[6]
    grad_active = lax.dot_general(
        group_cot, down_full, contract_cols, preferred_element_type=jnp.float32
    )
    grad_down = lax.dot_general(
        active, group_cot, contract_rows, preferred_element_type=jnp.float32
    )
    grad_gate = (grad_active * up_pre * (sigmoid_g + silu_g * (1.0 - sigmoid_g))).astype(
        jnp.bfloat16
    )
    grad_up = (grad_active * silu_g).astype(jnp.bfloat16)
    grad_gate_w = lax.dot_general(
        group_two, grad_gate, contract_rows, preferred_element_type=jnp.float32
    )
    grad_up_w = lax.dot_general(
        group_two, grad_up, contract_rows, preferred_element_type=jnp.float32
    )
    grad_normed_two = lax.psum_scatter(
        (
            lax.dot_general(grad_gate, gate_full, contract_cols, preferred_element_type=jnp.float32)
            + lax.dot_general(grad_up, up_full, contract_cols, preferred_element_type=jnp.float32)
        ).astype(jnp.bfloat16),
        "ulysses",
        scatter_dimension=0,
        tiled=True,
    ).astype(jnp.float32)
    grad_middle, grad_gain_two, grad_shift_two = norm_back(
        grad_normed_two, unit_two, inverse_two, gain_two
    )
    grad_middle = grad_middle + cotangent.astype(jnp.float32)
    group_grad = lax.all_gather(grad_middle.astype(jnp.bfloat16), "ulysses", axis=0, tiled=True)
    grad_attended = lax.dot_general(
        group_grad, out_full, contract_cols, preferred_element_type=jnp.float32
    ).astype(jnp.bfloat16)
    grad_out_w = lax.dot_general(
        attended_low, group_grad, contract_rows, preferred_element_type=jnp.float32
    )
    grad_spans = grad_attended.reshape(spanned)
    delta = jnp.sum(
        (grad_attended.astype(jnp.float32) * attended).reshape(
            group_size, local_rows, head_count, HEAD_DIM
        ),
        -1,
    ).transpose(2, 0, 1)

    def back_block(grads, keys, values, source, offset, bands):
        grad_query, grad_key, grad_value = grads
        allowed = block_mask(source, offset, bands)
        keys_band = band(keys, offset, bands, 0)
        values_band = band(values, offset, bands, 0)
        query_parts, key_parts, value_parts = ([], [], [])
        for head_num in range(head_count):
            columns = slice(head_num * HEAD_DIM, (head_num + 1) * HEAD_DIM)
            scores = head_scores(keys_band, head_num, allowed)
            weights_e = jnp.where(allowed, jnp.exp(scores - log_total[head_num][..., None]), 0.0)
            grad_weights = jnp.einsum(
                "cqd,ckd->cqk",
                grad_spans[..., columns],
                values_band[..., columns],
                preferred_element_type=jnp.float32,
            )
            grad_scores = (weights_e * (grad_weights - delta[head_num][..., None])).astype(
                jnp.bfloat16
            )
            query_parts.append(
                jnp.einsum(
                    "cqk,ckd->cqd",
                    grad_scores,
                    keys_band[..., columns],
                    preferred_element_type=jnp.float32,
                )
                * score_scale
            )
            key_parts.append(
                jnp.einsum(
                    "cqk,cqd->ckd",
                    grad_scores,
                    query_all[..., columns],
                    preferred_element_type=jnp.float32,
                )
                * score_scale
            )
            value_parts.append(
                jnp.einsum(
                    "cqk,cqd->ckd",
                    weights_e.astype(jnp.bfloat16),
                    grad_spans[..., columns],
                    preferred_element_type=jnp.float32,
                )
            )
        grad_query = grad_query + jnp.concatenate(query_parts, -1)
        grad_key = grad_key + unband(jnp.concatenate(key_parts, -1), offset, bands)
        grad_value = grad_value + unband(jnp.concatenate(value_parts, -1), offset, bands)
        return (grad_query, grad_key, grad_value)

    def pass_grads(grad_key, grad_value):
        return (
            from_behind(grad_key.astype(jnp.bfloat16), "blk", 1).astype(grad_key.dtype),
            from_behind(grad_value.astype(jnp.bfloat16), "blk", 1).astype(grad_value.dtype),
        )

    zero_spans = jnp.zeros(spanned, jnp.float32)
    grads = back_block(
        (zero_spans, zero_spans, zero_spans), key_all, value_all, cycle_slot, 0, local_bands
    )

    def back_step(step_num, keys, values, grad_query, grad_key, grad_value):
        grad_key, grad_value = pass_grads(grad_key, grad_value)
        source = (cycle_slot - step_num) % cycle_size
        offset = (source > cycle_slot).astype(jnp.int32)
        return back_block(
            (grad_query, grad_key, grad_value), keys, values, source, offset, cycle_bands
        )

    def cycle_backward(step_num, carry):
        keys, values, grad_query, grad_key, grad_value = carry
        keys, values = from_behind((keys, values), "blk", 1)
        grad_query, grad_key, grad_value = back_step(
            step_num, keys, values, grad_query, grad_key, grad_value
        )
        return (keys, values, grad_query, grad_key, grad_value)

    looped = lax.fori_loop(1, cycle_size, cycle_backward, (key_all, value_all) + grads)[2:]
    grad_key, grad_value = pass_grads(looped[1], looped[2])
    grad_joint = jnp.stack(
        [
            rotate(looped[0].reshape(heads_shape), cosine, -sine),
            rotate(grad_key.reshape(heads_shape), cosine, -sine),
            grad_value.reshape(heads_shape),
        ],
        1,
    )
    grad_joint = grad_joint.reshape(group_rows, 3 * head_width).astype(jnp.bfloat16)
    grad_bias = jnp.sum(grad_joint.astype(jnp.float32), 0).reshape(3, head_width)
    grad_qkv_w = lax.dot_general(
        group_normed, grad_joint, contract_rows, preferred_element_type=jnp.float32
    ).reshape(D, 3, head_width)
    grad_normed_one = lax.psum_scatter(
        lax.dot_general(
            grad_joint, qkv_full, contract_cols, preferred_element_type=jnp.float32
        ).astype(jnp.bfloat16),
        "ulysses",
        scatter_dimension=0,
        tiled=True,
    ).astype(jnp.float32)
    grad_inputs, grad_gain_one, grad_shift_one = norm_back(
        grad_normed_one, unit_one, inverse_one, gain_one
    )
    input_grad = grad_middle + grad_inputs
    weight_sums = (
        lax.psum_scatter(
            grad_qkv_w.astype(jnp.bfloat16), "blk", scatter_dimension=0, tiled=True
        ).astype(jnp.float32),
        lax.psum_scatter(
            grad_bias.astype(jnp.bfloat16), "blk", scatter_dimension=1, tiled=True
        ).astype(jnp.float32),
        lax.psum_scatter(
            grad_out_w.astype(jnp.bfloat16), "blk", scatter_dimension=1, tiled=True
        ).astype(jnp.float32),
        lax.psum_scatter(
            grad_gate_w.astype(jnp.bfloat16), "blk", scatter_dimension=0, tiled=True
        ).astype(jnp.float32),
        lax.psum_scatter(
            grad_up_w.astype(jnp.bfloat16), "blk", scatter_dimension=0, tiled=True
        ).astype(jnp.float32),
        lax.psum_scatter(
            grad_down.astype(jnp.bfloat16), "blk", scatter_dimension=1, tiled=True
        ).astype(jnp.float32),
    )
    norm_sums = (
        lax.psum_scatter(grad_gain_one, ("ulysses", "blk"), scatter_dimension=0, tiled=True),
        lax.psum_scatter(grad_shift_one, ("ulysses", "blk"), scatter_dimension=0, tiled=True),
        lax.psum_scatter(grad_gain_two, ("ulysses", "blk"), scatter_dimension=0, tiled=True),
        lax.psum_scatter(grad_shift_two, ("ulysses", "blk"), scatter_dimension=0, tiled=True),
    )
    return (
        mixed,
        input_grad,
        norm_sums[0],
        norm_sums[1],
        weight_sums[0],
        weight_sums[1],
        weight_sums[2],
        norm_sums[2],
        norm_sums[3],
        weight_sums[3],
        weight_sums[4],
        weight_sums[5],
    )


def solution(mesh):
    placed = (
        P(("ulysses", "blk"), None),
        P(("ulysses", "blk"), None),
        P(),
        P("blk"),
        P("blk"),
        P("blk", None, "ulysses"),
        P(None, ("ulysses", "blk")),
        P("ulysses", "blk"),
        P("blk"),
        P("blk"),
        P("blk", "ulysses"),
        P("blk", "ulysses"),
        P("ulysses", "blk"),
    )
    return jax.shard_map(
        local,
        mesh=mesh,
        in_specs=placed,
        out_specs=(
            P(("ulysses", "blk"), None),
            P(("ulysses", "blk"), None),
            P(("ulysses", "blk")),
            P(("ulysses", "blk")),
            P("blk", None, "ulysses"),
            P(None, ("ulysses", "blk")),
            P("ulysses", "blk"),
            P(("ulysses", "blk")),
            P(("ulysses", "blk")),
            P("blk", "ulysses"),
            P("blk", "ulysses"),
            P("ulysses", "blk"),
        ),
        check_vma=False,
    )
```

profile of v0, /device:TPU:0, one launch (start us, length us, event | category | flops | bytes accessed | tf_op | source)
XLA Modules:
  0.0 2141.5 jit_solution(14179579689005862599)
XLA Ops:
  9.1 21.1 all-gather
  30.2 16.3 all-gather.1
  52.9 17.6 all-gather.2
  71.6 57.0 %all-gather.15.cloned.1.call-done = bf16[1024,2048]{1,0:T(8,128)(2,1)} async-done(((bf16[128,2048]{1,0:T(8,128)(2,1)}), bf16[1024,2048]{1,0:T(8,128)(2,1)}) %all-gather.15.cloned.1.call-update) | async-done | bytes 4194320 | tf_op jit(solution)/shard_map/all_gather | solution.py:149
  146.9 326.8 %while.48 = (s32[]{:T(128)}, bf16[8,128,256]{1,2,0:T(8,128)(2,1)S(1)}, bf16[8,128,256]{1,2,0:T(8,128)(2,1)}, f32[4,8,128]{2,1,0:T(8,128)S(1)}, f32[4,8,128]{2,1,...) while((s32[]{:T(128)}, ...), condition=%wide.region_20.21_spmd.clone, body=%wide.region_11.20_spmd.clone.sunk | while | flops 143826976 | bytes 21953260 | solution.py:218
  147.8 11.4 collective-permute-done
  170.6 10.5 collective-permute-done
  192.3 10.5 collective-permute-done
  214.0 10.5 collective-permute-done
  235.6 10.5 collective-permute-done
  257.3 10.5 collective-permute-done
  279.0 10.5 collective-permute-done
  300.6 10.5 collective-permute-done
  409.0 10.5 collective-permute-done
  430.6 10.5 collective-permute-done
  452.3 10.5 collective-permute-done
  480.1 15.9 all-gather.3
  496.0 17.8 all-gather.4
  513.8 45.7 %reduce-scatter.21.cloned.1.call-done = bf16[128,2048]{1,0:T(8,128)(2,1)} async-done(((bf16[1024,2048]{1,0:T(8,128)(2,1)}), bf16[128,2048]{1,0:T(8,128)(2,1)}) %reduce-scatter.21.cloned.1.call-update) | async-done | bytes 524304 | tf_op jit(solution)/shard_map/reduce_scatter | solution.py:223
  567.1 33.0 %all-gather.25.cloned.1.call-done = bf16[2048,704]{0,1:T(8,128)(2,1)} async-done(((bf16[128,704]{0,1:T(8,128)(2,1)}), bf16[2048,704]{0,1:T(8,128)(2,1)}) %all-gather.25.cloned.1.call-update) | async-done | bytes 2883600 | tf_op jit(solution)/shard_map/all_gather | solution.py:128
  600.1 73.9 %all-gather.21.cloned.1.call-done = bf16[1024,2048]{1,0:T(8,128)(2,1)} async-done(((bf16[128,2048]{1,0:T(8,128)(2,1)}), bf16[1024,2048]{1,0:T(8,128)(2,1)}) %all-gather.21.cloned.1.call-update) | async-done | bytes 4194320 | tf_op jit(solution)/shard_map/all_gather | solution.py:231
  681.9 32.0 %all-gather.23.cloned.1.call-done = bf16[2048,704]{0,1:T(8,128)(2,1)} async-done(((bf16[128,704]{0,1:T(8,128)(2,1)}), bf16[2048,704]{0,1:T(8,128)(2,1)}) %all-gather.23.cloned.1.call-update) | async-done | bytes 2883600 | tf_op jit(solution)/shard_map/all_gather | solution.py:127
  721.7 34.2 %all-gather.27.cloned.1.call-done = bf16[704,2048]{1,0:T(8,128)(2,1)} async-done(((bf16[704,128]{1,0:T(8,128)(2,1)}), bf16[704,2048]{1,0:T(8,128)(2,1)}) %all-gather.27.cloned.1.call-update) | async-done | bytes 2883600 | tf_op jit(solution)/shard_map/all_gather | solution.py:129
  755.9 74.1 %all-gather.29.cloned.1.call-done = bf16[1024,2048]{1,0:T(8,128)(2,1)} async-done(((bf16[128,2048]{1,0:T(8,128)(2,1)}), bf16[1024,2048]{1,0:T(8,128)(2,1)}) %all-gather.29.cloned.1.call-update) | async-done | bytes 4194320 | tf_op jit(solution)/shard_map/all_gather | solution.py:150
  849.1 82.9 %reduce-scatter.25.cloned.1.call-done = bf16[128,2048]{1,0:T(8,128)(2,1)} async-done(((bf16[1024,2048]{1,0:T(8,128)(2,1)}), bf16[128,2048]{1,0:T(8,128)(2,1)}) %reduce-scatter.25.cloned.1.call-update) | async-done | bytes 524304 | tf_op jit(solution)/shard_map/reduce_scatter | solution.py:278
  974.2 33.1 %all-gather.31.cloned.1.call-done = bf16[1024,2048]{1,0:T(8,128)(2,1)} async-done(((bf16[128,2048]{1,0:T(8,128)(2,1)}), bf16[1024,2048]{1,0:T(8,128)(2,1)}) %all-gather.31.cloned.1.call-update) | async-done | bytes 4194320 | tf_op jit(solution)/shard_map/all_gather | solution.py:291
  1025.6 716.9 %while.49 = (s32[]{:T(128)}, bf16[8,128,256]{1,2,0:T(8,128)(2,1)}, bf16[8,128,256]{1,2,0:T(8,128)(2,1)}, f32[8,128,256]{1,2,0:T(8,128)S(1)}, bf16[8,128,256]{1,2...) while((s32[]{:T(128)}, bf16[8,128,256]{1,2,0:T(8,128)(2,1)}, ...), condition=%wide.region_30.31_spmd.clone, body=%wide.region_29.30_spmd.clone.sunk | while | flops 349175840 | bytes 41079092 | solution.py:383
  1029.0 48.1 %collective-permute-done.2 = bf16[8,128,256]{1,2,0:T(8,128)(2,1)S(1)} collective-permute-done((bf16[8,128,256]{1,2,0:T(8,128)(2,1)}, bf16[8,128,256]{1,2,0:T(8,128)(2,1)S(1)}, u32[]{:S(2)}, u32[]{:S(2)}) %collective-permute-start.2) | collective-permute-done | bytes 524320 | tf_op jit(solution)/shard_map/while/body/eval_jaxpr/ppermute | solution.py:23
  1093.5 50.5 %collective-permute-done.2 = bf16[8,128,256]{1,2,0:T(8,128)(2,1)S(1)} collective-permute-done((bf16[8,128,256]{1,2,0:T(8,128)(2,1)}, bf16[8,128,256]{1,2,0:T(8,128)(2,1)S(1)}, u32[]{:S(2)}, u32[]{:S(2)}) %collective-permute-start.2) | collective-permute-done | bytes 524320 | tf_op jit(solution)/shard_map/while/body/eval_jaxpr/ppermute | solution.py:23
  1163.3 49.9 %collective-permute-done.2 = bf16[8,128,256]{1,2,0:T(8,128)(2,1)S(1)} collective-permute-done((bf16[8,128,256]{1,2,0:T(8,128)(2,1)}, bf16[8,128,256]{1,2,0:T(8,128)(2,1)S(1)}, u32[]{:S(2)}, u32[]{:S(2)}) %collective-permute-start.2) | collective-permute-done | bytes 524320 | tf_op jit(solution)/shard_map/while/body/eval_jaxpr/ppermute | solution.py:23
  1234.7 21.4 collective-permute-done.2
  1276.3 22.6 %collective-permute-done.2 = bf16[8,128,256]{1,2,0:T(8,128)(2,1)S(1)} collective-permute-done((bf16[8,128,256]{1,2,0:T(8,128)(2,1)}, bf16[8,128,256]{1,2,0:T(8,128)(2,1)S(1)}, u32[]{:S(2)}, u32[]{:S(2)}) %collective-permute-start.2) | collective-permute-done | bytes 524320 | tf_op jit(solution)/shard_map/while/body/eval_jaxpr/ppermute | solution.py:23
  1318.0 23.8 %collective-permute-done.2 = bf16[8,128,256]{1,2,0:T(8,128)(2,1)S(1)} collective-permute-done((bf16[8,128,256]{1,2,0:T(8,128)(2,1)}, bf16[8,128,256]{1,2,0:T(8,128)(2,1)S(1)}, u32[]{:S(2)}, u32[]{:S(2)}) %collective-permute-start.2) | collective-permute-done | bytes 524320 | tf_op jit(solution)/shard_map/while/body/eval_jaxpr/ppermute | solution.py:23
  1359.6 25.0 %collective-permute-done.2 = bf16[8,128,256]{1,2,0:T(8,128)(2,1)S(1)} collective-permute-done((bf16[8,128,256]{1,2,0:T(8,128)(2,1)}, bf16[8,128,256]{1,2,0:T(8,128)(2,1)S(1)}, u32[]{:S(2)}, u32[]{:S(2)}) %collective-permute-start.2) | collective-permute-done | bytes 524320 | tf_op jit(solution)/shard_map/while/body/eval_jaxpr/ppermute | solution.py:23
  1401.3 26.2 %collective-permute-done.2 = bf16[8,128,256]{1,2,0:T(8,128)(2,1)S(1)} collective-permute-done((bf16[8,128,256]{1,2,0:T(8,128)(2,1)}, bf16[8,128,256]{1,2,0:T(8,128)(2,1)S(1)}, u32[]{:S(2)}, u32[]{:S(2)}) %collective-permute-start.2) | collective-permute-done | bytes 524320 | tf_op jit(solution)/shard_map/while/body/eval_jaxpr/ppermute | solution.py:23
  1442.9 27.5 %collective-permute-done.2 = bf16[8,128,256]{1,2,0:T(8,128)(2,1)S(1)} collective-permute-done((bf16[8,128,256]{1,2,0:T(8,128)(2,1)}, bf16[8,128,256]{1,2,0:T(8,128)(2,1)S(1)}, u32[]{:S(2)}, u32[]{:S(2)}) %collective-permute-start.2) | collective-permute-done | bytes 524320 | tf_op jit(solution)/shard_map/while/body/eval_jaxpr/ppermute | solution.py:23
  1485.6 27.6 %collective-permute-done.2 = bf16[8,128,256]{1,2,0:T(8,128)(2,1)S(1)} collective-permute-done((bf16[8,128,256]{1,2,0:T(8,128)(2,1)}, bf16[8,128,256]{1,2,0:T(8,128)(2,1)S(1)}, u32[]{:S(2)}, u32[]{:S(2)}) %collective-permute-start.2) | collective-permute-done | bytes 524320 | tf_op jit(solution)/shard_map/while/body/eval_jaxpr/ppermute | solution.py:23
  1528.5 27.6 %collective-permute-done.2 = bf16[8,128,256]{1,2,0:T(8,128)(2,1)S(1)} collective-permute-done((bf16[8,128,256]{1,2,0:T(8,128)(2,1)}, bf16[8,128,256]{1,2,0:T(8,128)(2,1)S(1)}, u32[]{:S(2)}, u32[]{:S(2)}) %collective-permute-start.2) | collective-permute-done | bytes 524320 | tf_op jit(solution)/shard_map/while/body/eval_jaxpr/ppermute | solution.py:23
  1571.3 27.6 %collective-permute-done.2 = bf16[8,128,256]{1,2,0:T(8,128)(2,1)S(1)} collective-permute-done((bf16[8,128,256]{1,2,0:T(8,128)(2,1)}, bf16[8,128,256]{1,2,0:T(8,128)(2,1)S(1)}, u32[]{:S(2)}, u32[]{:S(2)}) %collective-permute-start.2) | collective-permute-done | bytes 524320 | tf_op jit(solution)/shard_map/while/body/eval_jaxpr/ppermute | solution.py:23
  1614.2 27.6 %collective-permute-done.2 = bf16[8,128,256]{1,2,0:T(8,128)(2,1)S(1)} collective-permute-done((bf16[8,128,256]{1,2,0:T(8,128)(2,1)}, bf16[8,128,256]{1,2,0:T(8,128)(2,1)S(1)}, u32[]{:S(2)}, u32[]{:S(2)}) %collective-permute-start.2) | collective-permute-done | bytes 524320 | tf_op jit(solution)/shard_map/while/body/eval_jaxpr/ppermute | solution.py:23
  1657.0 27.6 %collective-permute-done.2 = bf16[8,128,256]{1,2,0:T(8,128)(2,1)S(1)} collective-permute-done((bf16[8,128,256]{1,2,0:T(8,128)(2,1)}, bf16[8,128,256]{1,2,0:T(8,128)(2,1)S(1)}, u32[]{:S(2)}, u32[]{:S(2)}) %collective-permute-start.2) | collective-permute-done | bytes 524320 | tf_op jit(solution)/shard_map/while/body/eval_jaxpr/ppermute | solution.py:23
  1699.9 27.6 %collective-permute-done.2 = bf16[8,128,256]{1,2,0:T(8,128)(2,1)S(1)} collective-permute-done((bf16[8,128,256]{1,2,0:T(8,128)(2,1)}, bf16[8,128,256]{1,2,0:T(8,128)(2,1)S(1)}, u32[]{:S(2)}, u32[]{:S(2)}) %collective-permute-start.2) | collective-permute-done | bytes 524320 | tf_op jit(solution)/shard_map/while/body/eval_jaxpr/ppermute | solution.py:23
  1800.1 25.0 %reduce-scatter.31.cloned.1.call-done = bf16[16,3]{1,0:T(8,128)(2,1)} async-done(((bf16[256,3]{1,0:T(8,128)(2,1)}), bf16[16,3]{1,0:T(8,128)(2,1)}) %reduce-scatter.31.cloned.1.call-update) | async-done | bytes 112
  1826.5 61.8 %reduce-scatter.33.cloned.1.call-done = bf16[128,256]{1,0:T(8,128)(2,1)} async-done(((bf16[2048,256]{1,0:T(8,128)(2,1)}), bf16[128,256]{1,0:T(8,128)(2,1)}) %reduce-scatter.33.cloned.1.call-update) | async-done | bytes 65552
  1889.9 66.0 %reduce-scatter.29.cloned.1.call-done = bf16[128,3,256]{2,0,1:T(8,128)(2,1)} async-done(((bf16[2048,3,256]{2,0,1:T(8,128)(2,1)}), bf16[128,3,256]{2,0,1:T(8,128)(2,1)}) %reduce-scatter.29.cloned.1.call-update) | async-done | bytes 196624 | tf_op jit(solution)/shard_map/reduce_scatter | solution.py:411
  1957.6 85.7 %reduce-scatter.27.cloned.1.call-done = bf16[128,2048]{1,0:T(8,128)(2,1)} async-done(((bf16[1024,2048]{1,0:T(8,128)(2,1)}), bf16[128,2048]{1,0:T(8,128)(2,1)}) %reduce-scatter.27.cloned.1.call-update) | async-done | bytes 524304 | tf_op jit(solution)/shard_map/reduce_scatter | solution.py:398
  2045.0 70.4 %all-reduce.14 = (f32[2048]{0:T(1024)S(1)}, f32[2048]{0:T(1024)S(1)}, f32[2048]{0:T(1024)S(1)}, f32[2048]{0:T(1024)S(1)}) all-reduce(f32[2048]{0:T(1024)S(1)} %get-tuple-element.853, f32[2048]{0:T(1024)S(1)} %get-tuple-element.858, f32[2048]{0:T(1024)S(1)} %copy-done.26, ...), channel_id=6, replica_groups=mesh['ulysses'=8,'blk'=16] {'ulysses','blk'}, use_global_device_ids=true, to_apply=%region_35.36.clone | all-reduce | flops 8192 | bytes 65536
  2117.7 13.8 reduce-scatter.23.cloned.1.call-done
  (1197 shorter events, 666.3 us)
Async XLA Ops:
  7.2 64.4 %all-gather.17.cloned.1.call-start = ((), (), s32[]{:S(2)}) async-start(), calls=%async_computation.11 | async-start | bytes 3342336 | tf_op jit(solution)/shard_map/all_gather | solution.py:124
  9.0 119.6 %all-gather.15.cloned.1.call-start = ((), (), s32[]{:S(2)}) async-start(), calls=%async_computation.10 | async-start | bytes 4718592 | tf_op jit(solution)/shard_map/all_gather | solution.py:149
  51.4 423.1 %all-gather.19.cloned.1.call-start = ((), (), s32[]{:S(2)}) async-start(), calls=%async_computation.12 | async-start | bytes 1114112 | tf_op jit(solution)/shard_map/all_gather | solution.py:126
  52.1 507.4 %reduce-scatter.21.cloned.1.call-start = ((), (), s32[]{:S(2)}) async-start(), calls=%async_computation.13 | async-start | bytes 4718592 | tf_op jit(solution)/shard_map/reduce_scatter | solution.py:223
  479.4 120.7 %all-gather.25.cloned.1.call-start = ((), (), s32[]{:S(2)}) async-start(), calls=%async_computation.16 | async-start | bytes 3063808 | tf_op jit(solution)/shard_map/all_gather | solution.py:128
  480.0 194.0 %all-gather.21.cloned.1.call-start = ((), (), s32[]{:S(2)}) async-start(), calls=%async_computation.14 | async-start | bytes 4718592 | tf_op jit(solution)/shard_map/all_gather | solution.py:231
  564.4 149.5 %all-gather.23.cloned.1.call-start = ((), (), s32[]{:S(2)}) async-start(), calls=%async_computation.15 | async-start | bytes 3063808 | tf_op jit(solution)/shard_map/all_gather | solution.py:127
  565.1 190.8 %all-gather.27.cloned.1.call-start = ((), (), s32[]{:S(2)}) async-start(), calls=%async_computation.17 | async-start | bytes 3063808 | tf_op jit(solution)/shard_map/all_gather | solution.py:129
  565.9 264.2 %all-gather.29.cloned.1.call-start = ((), (), s32[]{:S(2)}) async-start(), calls=%async_computation.19 | async-start | bytes 4718592 | tf_op jit(solution)/shard_map/all_gather | solution.py:150
  566.6 365.4 %reduce-scatter.25.cloned.1.call-start = ((), (), s32[]{:S(2)}) async-start(), calls=%async_computation.20 | async-start | bytes 4718592 | tf_op jit(solution)/shard_map/reduce_scatter | solution.py:278
  849.1 158.2 %all-gather.31.cloned.1.call-start = ((), (), s32[]{:S(2)}) async-start(), calls=%async_computation.21 | async-start | bytes 4718592 | tf_op jit(solution)/shard_map/all_gather | solution.py:291
  936.8 857.7 %reduce-scatter.39.cloned.1.call-start = ((), (), s32[]{:S(2)}) async-start(), calls=%async_computation.28 | async-start | bytes 3342336
  949.0 847.4 %reduce-scatter.35.cloned.1.call-start = ((), (), s32[]{:S(2)}) async-start(), calls=%async_computation.26 | async-start | bytes 3342336
  961.2 837.1 %reduce-scatter.37.cloned.1.call-start = ((), (), s32[]{:S(2)}) async-start(), calls=%async_computation.27 | async-start | bytes 3342336
  974.0 851.2 %reduce-scatter.31.cloned.1.call-start = ((), (), s32[]{:S(2)}) async-start(), calls=%async_computation.24 | async-start | bytes 69632
  1025.6 59.9 %collective-permute-start.5 = (bf16[8,128,256]{1,2,0:T(8,128)(2,1)}, bf16[8,128,256]{1,2,0:T(8,128)(2,1)}, u32[]{:S(2)}, u32[]{:S(2)}) collective-permute-start(bf16[8,128,256]{1,2,0:T(8,128)(2,1)} %get-tuple-element.1370), channel_id=1, source_target_pairs={{15,0},{0,1},{1,2},{2,3},{3,4},{4,5},{5,6},{6,7},{7,8},{8,9},{9,10... | collective-permute-start | bytes 1572872 | tf_op jit(solution)/shard_map/while/body/eval_jaxpr/ppermute | solution.py:23
  1025.6 64.4 %collective-permute-start.4 = (bf16[8,128,256]{1,2,0:T(8,128)(2,1)}, bf16[8,128,256]{1,2,0:T(8,128)(2,1)}, u32[]{:S(2)}, u32[]{:S(2)}) collective-permute-start(bf16[8,128,256]{1,2,0:T(8,128)(2,1)} %get-tuple-element.1369), channel_id=1, source_target_pairs={{15,0},{0,1},{1,2},{2,3},{3,4},{4,5},{5,6},{6,7},{7,8},{8,9},{9,10... | collective-permute-start | bytes 1572872 | tf_op jit(solution)/shard_map/while/body/eval_jaxpr/ppermute | solution.py:23
  1026.3 52.6 %collective-permute-start.3 = (bf16[8,128,256]{1,2,0:T(8,128)(2,1)}, bf16[8,128,256]{1,2,0:T(8,128)(2,1)S(1)}, u32[]{:S(2)}, u32[]{:S(2)}) collective-permute-start(bf16[8,128,256]{1,2,0:T(8,128)(2,1)} %get-tuple-element.1367), channel_id=1, source_target_pairs={{15,0},{0,1},{1,2},{2,3},{3,4},{4,5},{5,6},{6,7},{7,8},{8,9},{9,10... | collective-permute-start | bytes 1572872 | tf_op jit(solution)/shard_map/while/body/eval_jaxpr/ppermute | solution.py:23
  1026.3 50.8 %collective-permute-start.2 = (bf16[8,128,256]{1,2,0:T(8,128)(2,1)}, bf16[8,128,256]{1,2,0:T(8,128)(2,1)S(1)}, u32[]{:S(2)}, u32[]{:S(2)}) collective-permute-start(bf16[8,128,256]{1,2,0:T(8,128)(2,1)} %get-tuple-element.1366), channel_id=1, source_target_pairs={{15,0},{0,1},{1,2},{2,3},{3,4},{4,5},{5,6},{6,7},{7,8},{8,9},{9,10... | collective-permute-start | bytes 1572872 | tf_op jit(solution)/shard_map/while/body/eval_jaxpr/ppermute | solution.py:23
  1092.1 60.4 %collective-permute-start.5 = (bf16[8,128,256]{1,2,0:T(8,128)(2,1)}, bf16[8,128,256]{1,2,0:T(8,128)(2,1)}, u32[]{:S(2)}, u32[]{:S(2)}) collective-permute-start(bf16[8,128,256]{1,2,0:T(8,128)(2,1)} %get-tuple-element.1370), channel_id=1, source_target_pairs={{15,0},{0,1},{1,2},{2,3},{3,4},{4,5},{5,6},{6,7},{7,8},{8,9},{9,10... | collective-permute-start | bytes 1572872 | tf_op jit(solution)/shard_map/while/body/eval_jaxpr/ppermute | solution.py:23
  1092.1 64.8 %collective-permute-start.4 = (bf16[8,128,256]{1,2,0:T(8,128)(2,1)}, bf16[8,128,256]{1,2,0:T(8,128)(2,1)}, u32[]{:S(2)}, u32[]{:S(2)}) collective-permute-start(bf16[8,128,256]{1,2,0:T(8,128)(2,1)} %get-tuple-element.1369), channel_id=1, source_target_pairs={{15,0},{0,1},{1,2},{2,3},{3,4},{4,5},{5,6},{6,7},{7,8},{8,9},{9,10... | collective-permute-start | bytes 1572872 | tf_op jit(solution)/shard_map/while/body/eval_jaxpr/ppermute | solution.py:23
  1092.1 53.6 %collective-permute-start.3 = (bf16[8,128,256]{1,2,0:T(8,128)(2,1)}, bf16[8,128,256]{1,2,0:T(8,128)(2,1)S(1)}, u32[]{:S(2)}, u32[]{:S(2)}) collective-permute-start(bf16[8,128,256]{1,2,0:T(8,128)(2,1)} %get-tuple-element.1367), channel_id=1, source_target_pairs={{15,0},{0,1},{1,2},{2,3},{3,4},{4,5},{5,6},{6,7},{7,8},{8,9},{9,10... | collective-permute-start | bytes 1572872 | tf_op jit(solution)/shard_map/while/body/eval_jaxpr/ppermute | solution.py:23
  1092.1 51.9 %collective-permute-start.2 = (bf16[8,128,256]{1,2,0:T(8,128)(2,1)}, bf16[8,128,256]{1,2,0:T(8,128)(2,1)S(1)}, u32[]{:S(2)}, u32[]{:S(2)}) collective-permute-start(bf16[8,128,256]{1,2,0:T(8,128)(2,1)} %get-tuple-element.1366), channel_id=1, source_target_pairs={{15,0},{0,1},{1,2},{2,3},{3,4},{4,5},{5,6},{6,7},{7,8},{8,9},{9,10... | collective-permute-start | bytes 1572872 | tf_op jit(solution)/shard_map/while/body/eval_jaxpr/ppermute | solution.py:23
  1159.1 62.7 %collective-permute-start.5 = (bf16[8,128,256]{1,2,0:T(8,128)(2,1)}, bf16[8,128,256]{1,2,0:T(8,128)(2,1)}, u32[]{:S(2)}, u32[]{:S(2)}) collective-permute-start(bf16[8,128,256]{1,2,0:T(8,128)(2,1)} %get-tuple-element.1370), channel_id=1, source_target_pairs={{15,0},{0,1},{1,2},{2,3},{3,4},{4,5},{5,6},{6,7},{7,8},{8,9},{9,10... | collective-permute-start | bytes 1572872 | tf_op jit(solution)/shard_map/while/body/eval_jaxpr/ppermute | solution.py:23
  1159.1 67.1 %collective-permute-start.4 = (bf16[8,128,256]{1,2,0:T(8,128)(2,1)}, bf16[8,128,256]{1,2,0:T(8,128)(2,1)}, u32[]{:S(2)}, u32[]{:S(2)}) collective-permute-start(bf16[8,128,256]{1,2,0:T(8,128)(2,1)} %get-tuple-element.1369), channel_id=1, source_target_pairs={{15,0},{0,1},{1,2},{2,3},{3,4},{4,5},{5,6},{6,7},{7,8},{8,9},{9,10... | collective-permute-start | bytes 1572872 | tf_op jit(solution)/shard_map/while/body/eval_jaxpr/ppermute | solution.py:23
  1159.1 55.9 %collective-permute-start.3 = (bf16[8,128,256]{1,2,0:T(8,128)(2,1)}, bf16[8,128,256]{1,2,0:T(8,128)(2,1)S(1)}, u32[]{:S(2)}, u32[]{:S(2)}) collective-permute-start(bf16[8,128,256]{1,2,0:T(8,128)(2,1)} %get-tuple-element.1367), channel_id=1, source_target_pairs={{15,0},{0,1},{1,2},{2,3},{3,4},{4,5},{5,6},{6,7},{7,8},{8,9},{9,10... | collective-permute-start | bytes 1572872 | tf_op jit(solution)/shard_map/while/body/eval_jaxpr/ppermute | solution.py:23
  1160.0 53.3 %collective-permute-start.2 = (bf16[8,128,256]{1,2,0:T(8,128)(2,1)}, bf16[8,128,256]{1,2,0:T(8,128)(2,1)S(1)}, u32[]{:S(2)}, u32[]{:S(2)}) collective-permute-start(bf16[8,128,256]{1,2,0:T(8,128)(2,1)} %get-tuple-element.1366), channel_id=1, source_target_pairs={{15,0},{0,1},{1,2},{2,3},{3,4},{4,5},{5,6},{6,7},{7,8},{8,9},{9,10... | collective-permute-start | bytes 1572872 | tf_op jit(solution)/shard_map/while/body/eval_jaxpr/ppermute | solution.py:23
  1228.3 40.7 %collective-permute-start.4 = (bf16[8,128,256]{1,2,0:T(8,128)(2,1)}, bf16[8,128,256]{1,2,0:T(8,128)(2,1)}, u32[]{:S(2)}, u32[]{:S(2)}) collective-permute-start(bf16[8,128,256]{1,2,0:T(8,128)(2,1)} %get-tuple-element.1369), channel_id=1, source_target_pairs={{15,0},{0,1},{1,2},{2,3},{3,4},{4,5},{5,6},{6,7},{7,8},{8,9},{9,10... | collective-permute-start | bytes 1572872 | tf_op jit(solution)/shard_map/while/body/eval_jaxpr/ppermute | solution.py:23
  1271.2 36.3 %collective-permute-start.5 = (bf16[8,128,256]{1,2,0:T(8,128)(2,1)}, bf16[8,128,256]{1,2,0:T(8,128)(2,1)}, u32[]{:S(2)}, u32[]{:S(2)}) collective-permute-start(bf16[8,128,256]{1,2,0:T(8,128)(2,1)} %get-tuple-element.1370), channel_id=1, source_target_pairs={{15,0},{0,1},{1,2},{2,3},{3,4},{4,5},{5,6},{6,7},{7,8},{8,9},{9,10... | collective-permute-start | bytes 1572872 | tf_op jit(solution)/shard_map/while/body/eval_jaxpr/ppermute | solution.py:23
  1271.2 40.7 %collective-permute-start.4 = (bf16[8,128,256]{1,2,0:T(8,128)(2,1)}, bf16[8,128,256]{1,2,0:T(8,128)(2,1)}, u32[]{:S(2)}, u32[]{:S(2)}) collective-permute-start(bf16[8,128,256]{1,2,0:T(8,128)(2,1)} %get-tuple-element.1369), channel_id=1, source_target_pairs={{15,0},{0,1},{1,2},{2,3},{3,4},{4,5},{5,6},{6,7},{7,8},{8,9},{9,10... | collective-permute-start | bytes 1572872 | tf_op jit(solution)/shard_map/while/body/eval_jaxpr/ppermute | solution.py:23
  1314.0 40.7 %collective-permute-start.4 = (bf16[8,128,256]{1,2,0:T(8,128)(2,1)}, bf16[8,128,256]{1,2,0:T(8,128)(2,1)}, u32[]{:S(2)}, u32[]{:S(2)}) collective-permute-start(bf16[8,128,256]{1,2,0:T(8,128)(2,1)} %get-tuple-element.1369), channel_id=1, source_target_pairs={{15,0},{0,1},{1,2},{2,3},{3,4},{4,5},{5,6},{6,7},{7,8},{8,9},{9,10... | collective-permute-start | bytes 1572872 | tf_op jit(solution)/shard_map/while/body/eval_jaxpr/ppermute | solution.py:23
  1356.9 36.3 %collective-permute-start.5 = (bf16[8,128,256]{1,2,0:T(8,128)(2,1)}, bf16[8,128,256]{1,2,0:T(8,128)(2,1)}, u32[]{:S(2)}, u32[]{:S(2)}) collective-permute-start(bf16[8,128,256]{1,2,0:T(8,128)(2,1)} %get-tuple-element.1370), channel_id=1, source_target_pairs={{15,0},{0,1},{1,2},{2,3},{3,4},{4,5},{5,6},{6,7},{7,8},{8,9},{9,10... | collective-permute-start | bytes 1572872 | tf_op jit(solution)/shard_map/while/body/eval_jaxpr/ppermute | solution.py:23
  1356.9 40.7 %collective-permute-start.4 = (bf16[8,128,256]{1,2,0:T(8,128)(2,1)}, bf16[8,128,256]{1,2,0:T(8,128)(2,1)}, u32[]{:S(2)}, u32[]{:S(2)}) collective-permute-start(bf16[8,128,256]{1,2,0:T(8,128)(2,1)} %get-tuple-element.1369), channel_id=1, source_target_pairs={{15,0},{0,1},{1,2},{2,3},{3,4},{4,5},{5,6},{6,7},{7,8},{8,9},{9,10... | collective-permute-start | bytes 1572872 | tf_op jit(solution)/shard_map/while/body/eval_jaxpr/ppermute | solution.py:23
  1399.7 40.7 %collective-permute-start.4 = (bf16[8,128,256]{1,2,0:T(8,128)(2,1)}, bf16[8,128,256]{1,2,0:T(8,128)(2,1)}, u32[]{:S(2)}, u32[]{:S(2)}) collective-permute-start(bf16[8,128,256]{1,2,0:T(8,128)(2,1)} %get-tuple-element.1369), channel_id=1, source_target_pairs={{15,0},{0,1},{1,2},{2,3},{3,4},{4,5},{5,6},{6,7},{7,8},{8,9},{9,10... | collective-permute-start | bytes 1572872 | tf_op jit(solution)/shard_map/while/body/eval_jaxpr/ppermute | solution.py:23
  1442.6 36.3 %collective-permute-start.5 = (bf16[8,128,256]{1,2,0:T(8,128)(2,1)}, bf16[8,128,256]{1,2,0:T(8,128)(2,1)}, u32[]{:S(2)}, u32[]{:S(2)}) collective-permute-start(bf16[8,128,256]{1,2,0:T(8,128)(2,1)} %get-tuple-element.1370), channel_id=1, source_target_pairs={{15,0},{0,1},{1,2},{2,3},{3,4},{4,5},{5,6},{6,7},{7,8},{8,9},{9,10... | collective-permute-start | bytes 1572872 | tf_op jit(solution)/shard_map/while/body/eval_jaxpr/ppermute | solution.py:23
  1442.6 40.7 %collective-permute-start.4 = (bf16[8,128,256]{1,2,0:T(8,128)(2,1)}, bf16[8,128,256]{1,2,0:T(8,128)(2,1)}, u32[]{:S(2)}, u32[]{:S(2)}) collective-permute-start(bf16[8,128,256]{1,2,0:T(8,128)(2,1)} %get-tuple-element.1369), channel_id=1, source_target_pairs={{15,0},{0,1},{1,2},{2,3},{3,4},{4,5},{5,6},{6,7},{7,8},{8,9},{9,10... | collective-permute-start | bytes 1572872 | tf_op jit(solution)/shard_map/while/body/eval_jaxpr/ppermute | solution.py:23
  1485.4 40.7 %collective-permute-start.4 = (bf16[8,128,256]{1,2,0:T(8,128)(2,1)}, bf16[8,128,256]{1,2,0:T(8,128)(2,1)}, u32[]{:S(2)}, u32[]{:S(2)}) collective-permute-start(bf16[8,128,256]{1,2,0:T(8,128)(2,1)} %get-tuple-element.1369), channel_id=1, source_target_pairs={{15,0},{0,1},{1,2},{2,3},{3,4},{4,5},{5,6},{6,7},{7,8},{8,9},{9,10... | collective-permute-start | bytes 1572872 | tf_op jit(solution)/shard_map/while/body/eval_jaxpr/ppermute | solution.py:23
  1528.3 36.3 %collective-permute-start.5 = (bf16[8,128,256]{1,2,0:T(8,128)(2,1)}, bf16[8,128,256]{1,2,0:T(8,128)(2,1)}, u32[]{:S(2)}, u32[]{:S(2)}) collective-permute-start(bf16[8,128,256]{1,2,0:T(8,128)(2,1)} %get-tuple-element.1370), channel_id=1, source_target_pairs={{15,0},{0,1},{1,2},{2,3},{3,4},{4,5},{5,6},{6,7},{7,8},{8,9},{9,10... | collective-permute-start | bytes 1572872 | tf_op jit(solution)/shard_map/while/body/eval_jaxpr/ppermute | solution.py:23
  1528.3 40.7 %collective-permute-start.4 = (bf16[8,128,256]{1,2,0:T(8,128)(2,1)}, bf16[8,128,256]{1,2,0:T(8,128)(2,1)}, u32[]{:S(2)}, u32[]{:S(2)}) collective-permute-start(bf16[8,128,256]{1,2,0:T(8,128)(2,1)} %get-tuple-element.1369), channel_id=1, source_target_pairs={{15,0},{0,1},{1,2},{2,3},{3,4},{4,5},{5,6},{6,7},{7,8},{8,9},{9,10... | collective-permute-start | bytes 1572872 | tf_op jit(solution)/shard_map/while/body/eval_jaxpr/ppermute | solution.py:23
  1571.1 40.7 %collective-permute-start.4 = (bf16[8,128,256]{1,2,0:T(8,128)(2,1)}, bf16[8,128,256]{1,2,0:T(8,128)(2,1)}, u32[]{:S(2)}, u32[]{:S(2)}) collective-permute-start(bf16[8,128,256]{1,2,0:T(8,128)(2,1)} %get-tuple-element.1369), channel_id=1, source_target_pairs={{15,0},{0,1},{1,2},{2,3},{3,4},{4,5},{5,6},{6,7},{7,8},{8,9},{9,10... | collective-permute-start | bytes 1572872 | tf_op jit(solution)/shard_map/while/body/eval_jaxpr/ppermute | solution.py:23
  1614.0 36.3 %collective-permute-start.5 = (bf16[8,128,256]{1,2,0:T(8,128)(2,1)}, bf16[8,128,256]{1,2,0:T(8,128)(2,1)}, u32[]{:S(2)}, u32[]{:S(2)}) collective-permute-start(bf16[8,128,256]{1,2,0:T(8,128)(2,1)} %get-tuple-element.1370), channel_id=1, source_target_pairs={{15,0},{0,1},{1,2},{2,3},{3,4},{4,5},{5,6},{6,7},{7,8},{8,9},{9,10... | collective-permute-start | bytes 1572872 | tf_op jit(solution)/shard_map/while/body/eval_jaxpr/ppermute | solution.py:23
  1614.0 40.7 %collective-permute-start.4 = (bf16[8,128,256]{1,2,0:T(8,128)(2,1)}, bf16[8,128,256]{1,2,0:T(8,128)(2,1)}, u32[]{:S(2)}, u32[]{:S(2)}) collective-permute-start(bf16[8,128,256]{1,2,0:T(8,128)(2,1)} %get-tuple-element.1369), channel_id=1, source_target_pairs={{15,0},{0,1},{1,2},{2,3},{3,4},{4,5},{5,6},{6,7},{7,8},{8,9},{9,10... | collective-permute-start | bytes 1572872 | tf_op jit(solution)/shard_map/while/body/eval_jaxpr/ppermute | solution.py:23
  1656.8 40.7 %collective-permute-start.4 = (bf16[8,128,256]{1,2,0:T(8,128)(2,1)}, bf16[8,128,256]{1,2,0:T(8,128)(2,1)}, u32[]{:S(2)}, u32[]{:S(2)}) collective-permute-start(bf16[8,128,256]{1,2,0:T(8,128)(2,1)} %get-tuple-element.1369), channel_id=1, source_target_pairs={{15,0},{0,1},{1,2},{2,3},{3,4},{4,5},{5,6},{6,7},{7,8},{8,9},{9,10... | collective-permute-start | bytes 1572872 | tf_op jit(solution)/shard_map/while/body/eval_jaxpr/ppermute | solution.py:23
  1699.7 40.7 %collective-permute-start.4 = (bf16[8,128,256]{1,2,0:T(8,128)(2,1)}, bf16[8,128,256]{1,2,0:T(8,128)(2,1)}, u32[]{:S(2)}, u32[]{:S(2)}) collective-permute-start(bf16[8,128,256]{1,2,0:T(8,128)(2,1)} %get-tuple-element.1369), channel_id=1, source_target_pairs={{15,0},{0,1},{1,2},{2,3},{3,4},{4,5},{5,6},{6,7},{7,8},{8,9},{9,10... | collective-permute-start | bytes 1572872 | tf_op jit(solution)/shard_map/while/body/eval_jaxpr/ppermute | solution.py:23
  1766.1 122.2 %reduce-scatter.33.cloned.1.call-start = ((), (), s32[]{:S(2)}) async-start(), calls=%async_computation.25 | async-start | bytes 1114112
  1771.0 185.0 %reduce-scatter.29.cloned.1.call-start = ((), (), s32[]{:S(2)}) async-start(), calls=%async_computation.23 | async-start | bytes 3342336 | tf_op jit(solution)/shard_map/reduce_scatter | solution.py:411
  1778.9 264.4 %reduce-scatter.27.cloned.1.call-start = ((), (), s32[]{:S(2)}) async-start(), calls=%async_computation.22 | async-start | bytes 4718592 | tf_op jit(solution)/shard_map/reduce_scatter | solution.py:398
  1786.0 345.4 %reduce-scatter.23.cloned.1.call-start = ((), (), s32[]{:S(2)}) async-start(), calls=%async_computation.18 | async-start | bytes 4718592 | tf_op jit(solution)/shard_map/reduce_scatter | solution.py:239
  (124 other events, 7121.4 us)
Sparse Core Ops, SparseCore 0:
  10.2 43.7 all-gather.16
  56.9 71.6 all-gather.14
  130.2 33.2 all-gather.18
  479.6 79.9 reduce-scatter.20
  561.0 39.0 all-gather.24
  602.3 71.7 all-gather.20
  675.7 38.1 all-gather.22
  715.5 40.4 all-gather.26
  758.3 71.7 all-gather.28
  849.2 82.7 reduce-scatter.24
  936.9 70.3 all-gather.30
  1009.6 69.2 reduce-scatter.38
  1081.3 70.6 reduce-scatter.34
  1154.3 70.1 reduce-scatter.36
  1766.2 58.8 reduce-scatter.30
  1828.1 60.1 reduce-scatter.32
  1890.5 65.3 reduce-scatter.28
  1959.6 83.6 reduce-scatter.26
  2047.2 84.1 reduce-scatter.22
where the time goes:
time: 2150 us; the launch traced here: 2140 us
  waiting for transfers between devices  1360 us (63%)
  matrix products  374 us (17%)
  blocking collectives  159 us (7%)
  other arithmetic  110 us (5%)
  local copies, waits for them, and re-layouts  80.4 us (4%)
  starting transfers between devices  33.8 us (2%)
    ppermute x92, waiting for transfers between devices, from_behind(): return lax.ppermute(block, axis, route)  641 us
    dot_general x124, matrix products, head_scores(): jnp.einsum('cqd,ckd->cqk', query_all[..., columns], keys_band[..., column...  135 us
    unnamed x24, waiting for transfers between devices  90.3 us
    reduce_scatter x1, waiting for transfers between devices, local(): lax.psum_scatter(lax.dot_general(grad_joint, qkv_full, contract_cols, pre...  85.7 us
    reduce_scatter x1, waiting for transfers between devices, local(): lax.psum_scatter((lax.dot_general(grad_gate, gate_full, contract_cols, pr...  82.9 us
    all_gather x1, waiting for transfers between devices, local(): lax.all_gather(cotangent, 'ulysses', axis=0, tiled=True)  74.1 us
    all_gather x1, waiting for transfers between devices, local(): group_two = lax.all_gather(normed_two, 'ulysses', axis=0, tiled=True)  73.9 us
    unnamed x1, blocking collectives  70.4 us
  transfers between devices with their start and end apart: 111, of which 61 were waited for; matrix products, arithmetic and copies ran while one was open for 25% of the time, Pallas kernels for 0%

commit v1 on v0

v1 whole, which is shorter than its diff:
```python
import functools

import jax
import jax.numpy as jnp
from jax import lax
from jax.experimental import pallas as pl
from jax.experimental.pallas import tpu as pltpu
from jax.sharding import Mesh
from jax.sharding import PartitionSpec as P

D = 2048
HEADS = 32
HEAD_DIM = 64
ROT = 16
BLK_TOK = 128
HID = 704
HID_PAD = 768
SHARED = 3 * HID_PAD + 256

eps = 1e-05
rope_base = 10000.0
masked_score = -1e30
score_scale = HEAD_DIM ** (-0.5)

AXES = ("yh", "x", "z", "yl", "k")
PLANE = ("yh", "z", "yl", "k")
BLK = ("z", "yl", "k")
Y = ("yh", "yl")

VMEM_LIMIT = 60 * 1024 * 1024
TINY = pl.CostEstimate(flops=1, bytes_accessed=1, transcendentals=0)


def mm(a, b, ca=1, cb=0):
    return lax.dot_general(a, b, (((ca,), (cb,)), ((), ())), preferred_element_type=jnp.float32)


def swap_core(value):
    return lax.ppermute(value, ("k",), [(0, 1), (1, 0)])


def exchange(parts, axes):
    return lax.all_to_all(parts, axes, 0, 0, tiled=True)


def send(value, axes, step):
    return lax.ppermute(value, axes, [(i, (i + step) % 4) for i in range(4)])


def gather(value, axes, *others):
    me = lax.axis_index(axes)
    pieces = [send(value, axes, step) for step in (1, 3, 2)]
    if others:
        pieces = after(pieces, *others)
    buffer = jnp.zeros((4,) + value.shape, value.dtype)
    for step, piece in zip((0, 1, 3, 2), [value] + pieces):
        buffer = lax.dynamic_update_index_in_dim(buffer, piece, (me - step) % 4, 0)
    return buffer


def ring_gather(value):
    return exchange(jnp.broadcast_to(value, (4,) + value.shape), ("x",))


def send(value, axes, step):
    return lax.ppermute(value, axes, [(i, (i + step) % 4) for i in range(4)])


def gather(value, axes, *others):
    me = lax.axis_index(axes)
    pieces = [send(value, axes, step) for step in (1, 3, 2)]
    if others:
        pieces = after(pieces, *others)
    buffer = jnp.zeros((4,) + value.shape, value.dtype)
    for step, piece in zip((0, 1, 3, 2), [value] + pieces):
        buffer = lax.dynamic_update_index_in_dim(buffer, piece, (me - step) % 4, 0)
    return buffer


def ring_gather(value):
    return exchange(jnp.broadcast_to(value, (4,) + value.shape), ("x",))


def after(value, *others):
    return lax.optimization_barrier((value,) + others)[0]


def rotary_tables(positions):
    halfway = ROT // 2
    counter = jnp.arange(halfway, dtype=jnp.float32)
    frequency = rope_base ** (-2.0 * counter / ROT)
    lane = jnp.arange(128) % HEAD_DIM
    frequency = jnp.where(lane < ROT, jnp.tile(frequency, 16), 0.0)
    angles = positions.astype(jnp.float32)[:, None] * frequency[None, :]
    sine = jnp.sin(angles)
    return (
        jnp.cos(angles),
        jnp.where(lane < halfway, -sine, 0.0),
        jnp.where((lane >= halfway) & (lane < ROT), sine, 0.0),
    )


def pack_joint_kernel(qkv_ref, out_ref, vectors_ref, bias_ref, h0_ref, h1_ref, small_ref):
    out_t = jnp.transpose(out_ref[...])
    for j, h_ref in enumerate((h0_ref, h1_ref)):
        for part in range(3):
            column = part * 256 + j * 128
            h_ref[:128, part * 128 : (part + 1) * 128] = qkv_ref[:, column : column + 128]
        h_ref[:128, 384:] = out_t[:, j * 128 : (j + 1) * 128]
    small_ref[...] = jnp.zeros_like(small_ref)
    small_ref[0:4, :128] = vectors_ref[...].astype(jnp.float32)
    small_ref[8:11, :16] = bias_ref[...].astype(jnp.float32)
    h0_ref[128:, :] = small_ref[...].astype(jnp.bfloat16)


def pack_joint_call(qkv, out, vectors, bias):
    vmem = pl.BlockSpec(memory_space=pltpu.VMEM)
    return pl.pallas_call(
        pack_joint_kernel,
        in_specs=[vmem] * 4,
        out_specs=[vmem] * 2,
        out_shape=[
            jax.ShapeDtypeStruct((144, 512), jnp.bfloat16),
            jax.ShapeDtypeStruct((128, 512), jnp.bfloat16),
        ],
        scratch_shapes=[pltpu.VMEM((16, 512), jnp.float32)],
    )(qkv, out, vectors, bias)


def pack_hidden_kernel(gate_ref, up_ref, down_ref, rest_ref):
    down = jnp.transpose(down_ref[...])
    for i, weights in enumerate((gate_ref[...], up_ref[...], down)):
        first = i * HID_PAD
        rest_ref[:, first + HID_PAD - 128 : first + HID_PAD] = jnp.zeros((128, 128), jnp.bfloat16)
        rest_ref[:, first : first + HID] = weights


def pack_hidden_call(gate, up, down):
    return whole_call(
        pack_hidden_kernel, jax.ShapeDtypeStruct((128, 3 * HID_PAD), jnp.bfloat16), gate, up, down
    )


def core_columns(ref, core, blocks):
    columns = [ref[:blocks, :, pl.ds(pl.multiple_of((2 * i + core) * 128, 128), 128)] for i in range(8)]
    return jnp.concatenate(columns, 2).reshape(blocks * 128, 1024)


def core_rows(w0_ref, w1_ref):
    w0 = jnp.concatenate([w0_ref[z, 0, yl, :128] for z in range(4) for yl in range(2)], 0)
    w1 = jnp.concatenate([w1_ref[0, yl, z] for z in range(4) for yl in range(2)], 0)
    return jnp.concatenate([w0, w1], 1)


def normalise(values):
    centred = values - jnp.mean(values, -1, keepdims=True)
    inverse = lax.rsqrt(jnp.mean(centred * centred, -1, keepdims=True) + eps)
    return centred * inverse, inverse


def qkv_kernel(
    core_ref,
    x_ref,
    before_ref,
    gain_ref,
    shift_ref,
    own0_ref,
    own1_ref,
    oth0_ref,
    oth1_ref,
    bias_ref,
    cos_ref,
    up_ref,
    down_ref,
    out_ref,
    normed_ref,
    x_cores,
):
    part = pl.program_id(1)
    core = core_ref[0]

    @pl.when((pl.program_id(0) == 0) & (part == 0))
    def _():
        for b in range(5):
            block = x_ref[b] if b < 4 else before_ref[...]
            unit, _ = normalise(block.astype(jnp.float32))
            normed = (unit * gain_ref[...] + shift_ref[...]).astype(jnp.bfloat16)
            if b < 4:
                normed_ref[b] = normed
            for c in range(16):
                column = pl.multiple_of((c // 2 + 8 * ((c + core) % 2)) * 128, 128)
                x_cores[b * 128 : (b + 1) * 128, pl.ds(column, 128)] = normed[:, c * 128 : (c + 1) * 128]

    def joint(rows):
        weights = jnp.concatenate([core_rows(own0_ref, own1_ref), core_rows(oth0_ref, oth1_ref)], 0)
        return mm(x_cores[:rows], weights) + bias_ref[0, 0]

    def turned(value):
        rows = value.shape[0]
        return (
            value * cos_ref[:rows]
            + pltpu.roll(value, 120, 1) * up_ref[:rows]
            + pltpu.roll(value, 8, 1) * down_ref[:rows]
        )

    @pl.when(part == 0)
    def _():
        value = joint(512)
        for j in range(2):
            query = turned(value[:, j * 128 : (j + 1) * 128]) * score_scale
            out_ref[j, 0, :, 4] = query.astype(jnp.bfloat16).reshape(4, 128, 128)

    @pl.when(part > 0)
    def _():
        value = joint(640)
        for j in range(2):
            block = value[:, j * 128 : (j + 1) * 128]
            block = jnp.where(part == 1, turned(block), block)
            block = block.astype(jnp.bfloat16).reshape(5, 128, 128)

            @pl.when(part == 1)
            def _():
                out_ref[j, 0, :, 2] = block[:4]
                out_ref[j, 0, 1:, 0] = block[:3]
                out_ref[j, 0, 0, 0] = block[4]

            @pl.when(part == 2)
            def _():
                out_ref[j, 0, :, 3] = block[:4]
                out_ref[j, 0, 1:, 1] = block[:3]
                out_ref[j, 0, 0, 1] = block[4]


def qkv_call(core, tokens, before, gain, shift, weights, bias, tables):
    table = pl.BlockSpec((640, 128), lambda h, p: (0, 0))
    vector = pl.BlockSpec((1, D), lambda h, p: (0, 0))
    first = pl.BlockSpec((4, 1, 2, 144, 128), lambda h, p: (0, h, 0, 0, p))
    second = pl.BlockSpec((1, 2, 4, 128, 128), lambda h, p: (h, 0, 0, 0, p))
    return pl.pallas_call(
        qkv_kernel,
        grid=(2, 3),
        in_specs=[
            pl.BlockSpec(memory_space=pltpu.SMEM),
            pl.BlockSpec((4, 128, D), lambda h, p: (0, 0, 0)),
            pl.BlockSpec((128, D), lambda h, p: (0, 0)),
            vector,
            vector,
            first,
            second,
            first,
            second,
            pl.BlockSpec((1, 1, 1, 256), lambda h, p: (h, p, 0, 0)),
            table,
            table,
            table,
        ],
        out_specs=[
            pl.BlockSpec((2, 1, 4, 5, 128, 128), lambda h, p: (0, h, 0, 0, 0, 0)),
            pl.BlockSpec((4, 128, D), lambda h, p: (0, 0, 0)),
        ],
        out_shape=[
            jax.ShapeDtypeStruct((2, 2, 4, 5, 128, 128), jnp.bfloat16),
            jax.ShapeDtypeStruct((4, 128, D), jnp.bfloat16),
        ],
        scratch_shapes=[pltpu.VMEM((640, D), jnp.bfloat16)],
        compiler_params=pltpu.CompilerParams(vmem_limit_bytes=VMEM_LIMIT),
        cost_estimate=TINY,
    )(core, tokens, before, gain, shift, *weights, bias, *tables)


def whole_call(kernel, out_shape, *operands, scratch=()):
    vmem = pl.BlockSpec(memory_space=pltpu.VMEM)
    return pl.pallas_call(
        kernel,
        in_specs=[vmem] * len(operands),
        out_specs=jax.tree.map(lambda _: vmem, out_shape),
        out_shape=out_shape,
        scratch_shapes=list(scratch),
        compiler_params=pltpu.CompilerParams(vmem_limit_bytes=VMEM_LIMIT),
        cost_estimate=TINY,
    )(*operands)


def middle_kernel(came_ref, tokens_ref, gain_ref, shift_ref, middle_ref, normed_ref):
    middle = tokens_ref[...].astype(jnp.float32)
    for i in range(4):
        middle = middle + came_ref[i].astype(jnp.float32)
    middle_ref[...] = middle
    normed = (normalise(middle)[0] * gain_ref[...] + shift_ref[...]).astype(jnp.bfloat16)
    for i in range(4):
        normed_ref[i] = normed


def back_through(came_ref, values, gain):
    grad = came_ref[0].astype(jnp.float32)
    for i in range(1, 4):
        grad = grad + came_ref[i].astype(jnp.float32)
    unit, inverse = normalise(values)
    grad_unit = grad * gain
    centred_grad = (
        grad_unit
        - jnp.mean(grad_unit, -1, keepdims=True)
        - unit * jnp.mean(grad_unit * unit, -1, keepdims=True)
    )
    gain_grad = jnp.sum(grad * unit, 0, keepdims=True)
    return inverse * centred_grad, gain_grad, jnp.sum(grad, 0, keepdims=True)


def middle_back_kernel(came_ref, middle_ref, cot_ref, gain_ref, grad_ref, ring_ref, gain_grad_ref, shift_grad_ref):
    grad, gain_grad_ref[...], shift_grad_ref[...] = back_through(came_ref, middle_ref[...], gain_ref[...])
    grad = grad + cot_ref[...].astype(jnp.float32)
    grad_ref[...] = grad
    for i in range(4):
        ring_ref[i] = grad.astype(jnp.bfloat16)


def input_back_kernel(came_ref, tokens_ref, grad_ref, gain_ref, out_ref, gain_grad_ref, shift_grad_ref):
    values = tokens_ref[...].astype(jnp.float32)
    grad, gain_grad_ref[...], shift_grad_ref[...] = back_through(came_ref, values, gain_ref[...])
    out_ref[...] = grad_ref[...] + grad


def mixed_kernel(came_ref, middle_ref, out_ref):
    total = middle_ref[...]
    for i in range(4):
        total = total + came_ref[i].astype(jnp.float32)
    out_ref[...] = total.astype(jnp.bfloat16)


def shared_end_kernel(total_ref, gate_ref, up_ref, down_ref, out_ref):
    total = total_ref[...].astype(jnp.float32)
    for c in range(3):
        width = min(HID, c * 256 + 256) - c * 256
        gate_ref[:, c * 256 : c * 256 + width] = total[:, c * 512 : c * 512 + width]
        up_ref[:, c * 256 : c * 256 + width] = total[:, c * 512 + 256 : c * 512 + 256 + width]
    down_ref[...] = jnp.transpose(total[:, 2 * HID_PAD : 3 * HID_PAD])[:HID]
    out_ref[...] = jnp.transpose(total[:, 3 * HID_PAD :])


def joint_end_kernel(*refs):
    for j in range(2):
        total = sum(ref[...].astype(jnp.float32) for ref in refs[4 * j : 4 * j + 4])
        for part in range(3):
            refs[8][:, part * 256 + j * 128 : part * 256 + j * 128 + 128] = total[:, part * 128 : part * 128 + 128]


def ordered(core_ref, own, other):
    first = core_ref[0] == 0
    return jnp.concatenate([jnp.where(first, own, other), jnp.where(first, other, own)], 0)


def project_kernel(core_ref, att_ref, own0_ref, own1_ref, oth0_ref, oth1_ref, out_ref):
    att = jnp.concatenate([att_ref[j, h].reshape(512, 128) for h in range(2) for j in range(2)], 1)

    def rows(w0_ref, w1_ref):
        return jnp.concatenate(
            [w for h in range(2) for w in (w0_ref[0, h, 0, :128], w1_ref[h, 0, 0])], 1
        )

    weights = ordered(core_ref, rows(own0_ref, own1_ref), rows(oth0_ref, oth1_ref))
    out_ref[...] = mm(att, weights, 1, 1).astype(jnp.bfloat16).reshape(4, 128, 256)


def project_call(core, att, weights):
    first = pl.BlockSpec((1, 2, 1, 144, 128), lambda n: (n // 2, 0, n % 2, 0, 3))
    second = pl.BlockSpec((2, 1, 1, 128, 128), lambda n: (0, n % 2, n // 2, 0, 3))
    return pl.pallas_call(
        project_kernel,
        grid=(8,),
        in_specs=[
            pl.BlockSpec(memory_space=pltpu.SMEM),
            pl.BlockSpec((2, 2, 4, 128, 128), lambda n: (0, 0, 0, 0, 0)),
            first,
            second,
            first,
            second,
        ],
        out_specs=pl.BlockSpec((4, 128, 256), lambda n: (0, 0, n)),
        out_shape=jax.ShapeDtypeStruct((4, 128, D), jnp.bfloat16),
        compiler_params=pltpu.CompilerParams(vmem_limit_bytes=VMEM_LIMIT),
        cost_estimate=TINY,
    )(core, att, *weights)


def project_back_kernel(core_ref, grad_ref, own0_ref, own1_ref, oth0_ref, oth1_ref, out_ref):
    core = core_ref[0]
    grad = mm(core_columns(grad_ref, core, 4), core_rows(own0_ref, own1_ref))
    grad = grad + mm(core_columns(grad_ref, 1 - core, 4), core_rows(oth0_ref, oth1_ref))
    grad = grad.astype(jnp.bfloat16)
    for j in range(2):
        out_ref[j, 0] = grad[:, j * 128 : (j + 1) * 128].reshape(4, 128, 128)


def project_back_call(core, grad, weights):
    first = pl.BlockSpec((4, 1, 2, 144, 128), lambda h: (0, h, 0, 0, 3))
    second = pl.BlockSpec((1, 2, 4, 128, 128), lambda h: (h, 0, 0, 0, 3))
    return pl.pallas_call(
        project_back_kernel,
        grid=(2,),
        in_specs=[
            pl.BlockSpec(memory_space=pltpu.SMEM),
            pl.BlockSpec((4, 128, D), lambda h: (0, 0, 0)),
            first,
            second,
            first,
            second,
        ],
        out_specs=pl.BlockSpec((2, 1, 4, 128, 128), lambda h: (0, h, 0, 0, 0)),
        out_shape=jax.ShapeDtypeStruct((2, 2, 4, 128, 128), jnp.bfloat16),
        compiler_params=pltpu.CompilerParams(vmem_limit_bytes=VMEM_LIMIT),
        cost_estimate=TINY,
    )(core, grad, *weights)


def feed_forward_kernel(
    x_ref, cot_ref, gate_ref, up_ref, down_ref, active_ref, grads_ref, back_ref, out_ref, back_sum, out_sum
):
    step = pl.program_id(0) * 3 + pl.program_id(1)
    x = x_ref[...].reshape(512, D)
    gate = mm(x, gate_ref[0])
    up = mm(x, up_ref[0])
    grad_active = mm(cot_ref[...].reshape(512, D), down_ref[0])
    sigmoid = jax.nn.sigmoid(gate)
    silu = gate * sigmoid
    active = (silu * up).astype(jnp.bfloat16)
    grad_gate = (grad_active * up * (sigmoid + silu * (1.0 - sigmoid))).astype(jnp.bfloat16)
    grad_up = (grad_active * silu).astype(jnp.bfloat16)
    grads = jnp.concatenate([grad_gate, grad_up], 1)
    active_ref[0] = active
    grads_ref[0] = grads
    back = mm(grads, jnp.concatenate([gate_ref[0], up_ref[0]], 1), 1, 1)
    out = mm(active, down_ref[0], 1, 1)

    @pl.when(step == 0)
    def _():
        back_sum[...] = back
        out_sum[...] = out

    @pl.when((step > 0) & (step < 5))
    def _():
        back_sum[...] += back
        out_sum[...] += out

    @pl.when(step == 5)
    def _():
        back_ref[...] = (back_sum[...] + back).astype(jnp.bfloat16).reshape(4, 128, D)
        out_ref[...] = (out_sum[...] + out).astype(jnp.bfloat16).reshape(4, 128, D)


def feed_forward_call(x, ring, rest):
    tokens = pl.BlockSpec((4, 128, D), lambda h, c: (0, 0, 0))
    weight = [pl.BlockSpec((1, D, 256), lambda h, c, first=first: (h, 0, first + c)) for first in (0, 3, 6)]
    ring_shape = jax.ShapeDtypeStruct((4, 128, D), jnp.bfloat16)
    return pl.pallas_call(
        feed_forward_kernel,
        grid=(2, 3),
        in_specs=[tokens, pl.BlockSpec((4, 128, D), lambda h, c: (0, 1, 0))] + weight,
        out_specs=[
            pl.BlockSpec((1, 512, 256), lambda h, c: (h, 0, c)),
            pl.BlockSpec((1, 512, 512), lambda h, c: (h, 0, c)),
            tokens,
            tokens,
        ],
        out_shape=[
            jax.ShapeDtypeStruct((2, 512, HID_PAD), jnp.bfloat16),
            jax.ShapeDtypeStruct((2, 512, 2 * HID_PAD), jnp.bfloat16),
            ring_shape,
            ring_shape,
        ],
        scratch_shapes=[pltpu.VMEM((512, D), jnp.float32), pltpu.VMEM((512, D), jnp.float32)],
        compiler_params=pltpu.CompilerParams(vmem_limit_bytes=VMEM_LIMIT),
        cost_estimate=TINY,
    )(x, ring, rest, rest, rest)


def plane_grad_kernel(core_ref, left_ref, left_other_ref, right_ref, right_other_ref, *refs):
    out_ref, left_t = refs[-2:]

    @pl.when((pl.program_id(0) == 0) & (pl.program_id(1) == 0))
    def _():
        left_t[:, :512] = jnp.transpose(core_columns(left_ref, core_ref[0], 4))
        left_t[:, 512:] = jnp.transpose(core_columns(left_other_ref, core_ref[0], 4))

    total = mm(left_t[...], jnp.concatenate([right_ref[0], right_other_ref[0]], 0)).astype(jnp.bfloat16)
    for z in range(4):
        for yl in range(2):
            row = (z * 2 + yl) * 128
            out_ref[0, yl, z] = total[row : row + 128]


def plane_grad_call(core, left, right, columns, before, first, shared=None):
    left_block = pl.BlockSpec((4, 128, D), lambda n, h: (0, before, 0))
    right_block = pl.BlockSpec((1, 512, 256), lambda n, h: (h, 0, n))
    extra = [] if shared is None else [shared]
    return pl.pallas_call(
        plane_grad_kernel,
        grid=(columns // 256, 2),
        in_specs=[
            pl.BlockSpec(memory_space=pltpu.SMEM),
            left_block,
            left_block,
            right_block,
            right_block,
        ]
        + [pl.BlockSpec(memory_space=pl.ANY)] * len(extra),
        out_specs=pl.BlockSpec((1, 2, 4, 128, 256), lambda n, h: (h, 0, 0, 0, first // 256 + n)),
        out_shape=jax.ShapeDtypeStruct((2, 2, 4, 128, SHARED), jnp.bfloat16),
        input_output_aliases={5: 0} if extra else {},
        scratch_shapes=[pltpu.VMEM((1024, 1024), jnp.bfloat16)],
        compiler_params=pltpu.CompilerParams(vmem_limit_bytes=VMEM_LIMIT),
        cost_estimate=TINY,
    )(core, *left, *right, *extra)


def weight_grad_kernel(core_ref, place_ref, left_ref, left_other_ref, right_ref, right_other_ref, *refs):
    outs, left_t = refs[:4], refs[4]
    h = pl.program_id(1)

    @pl.when((h == 0) & (pl.program_id(0) == 0))
    def _():
        left_t[:, :512] = jnp.transpose(core_columns(left_ref, core_ref[0], 4))
        left_t[:, 512:] = jnp.transpose(core_columns(left_other_ref, core_ref[0], 4))

    total = mm(left_t[...], jnp.concatenate([right_ref[0], right_other_ref[0]], 0)).astype(jnp.bfloat16)
    for z in range(4):
        for yl in range(2):
            row = (z * 2 + yl) * 128
            chip = (h * 2 + yl) * 4 + z
            step, slot = place_ref[0, chip], place_ref[1, chip]
            for t in range(4):

                @pl.when(step == t)
                def _():
                    outs[t][slot] = total[row : row + 128]


def weight_grad_call(core, place, left, right, first, columns):
    width = 256 if columns % 256 == 0 else 384
    smem = pl.BlockSpec(memory_space=pltpu.SMEM)
    left_block = pl.BlockSpec((4, 128, D), lambda n, h: (0, 0, 0))
    right_block = pl.BlockSpec((1, 512, width), lambda n, h: (h, 0, first // width + n))
    return pl.pallas_call(
        weight_grad_kernel,
        grid=(columns // width, 2),
        in_specs=[smem, smem, left_block, left_block, right_block, right_block],
        out_specs=[pl.BlockSpec((4, 128, width), lambda n, h: (0, 0, n))] * 4,
        out_shape=[jax.ShapeDtypeStruct((4, 128, columns), jnp.bfloat16)] * 4,
        scratch_shapes=[pltpu.VMEM((1024, 1024), jnp.bfloat16)],
        compiler_params=pltpu.CompilerParams(vmem_limit_bytes=VMEM_LIMIT),
        cost_estimate=TINY,
    )(core, place, *left, *right)


def split_sum_kernel(place_ref, a_ref, b_ref, c_ref, d_ref, *out_refs):
    for t in range(4):
        i = (place_ref[0] + t) % 4
        total = sum(ref[i].astype(jnp.float32) for ref in (a_ref, b_ref, c_ref, d_ref))
        out_refs[t][...] = total.astype(jnp.bfloat16)


def split_sum_call(place, parts):
    columns = parts[0].shape[2]
    width = 256 if columns % 256 == 0 else 384
    return pl.pallas_call(
        split_sum_kernel,
        grid=(columns // width,),
        in_specs=[pl.BlockSpec(memory_space=pltpu.SMEM)]
        + [pl.BlockSpec((4, 128, width), lambda n: (0, 0, n))] * 4,
        out_specs=[pl.BlockSpec((128, width), lambda n: (0, n))] * 4,
        out_shape=[jax.ShapeDtypeStruct((128, columns), jnp.bfloat16)] * 4,
        compiler_params=pltpu.CompilerParams(vmem_limit_bytes=VMEM_LIMIT),
        cost_estimate=TINY,
    )(place, *parts)


def chip_places(y_first):
    y, z = jnp.arange(16, dtype=jnp.int32) // 4, jnp.arange(16, dtype=jnp.int32) % 4
    if y_first:
        return jnp.stack([(y - lax.axis_index(Y)) % 4, z])
    return jnp.stack([(z - lax.axis_index("z")) % 4, y])


def with_other(value):
    return value, swap_core(value)


def first_send(parts, y_first):
    axes = Y if y_first else ("z",)
    return [parts[0]] + [send(parts[t], axes, t) for t in (1, 3, 2)]


def first_sum(parts, y_first):
    return split_sum_call(lax.axis_index(("z",) if y_first else Y).reshape(1), parts)


def second_send(parts, y_first):
    axes = ("z",) if y_first else Y
    return [parts[0]] + [send(parts[t], axes, t) for t in (1, 3, 2)]


def head_masks():
    lane = lax.broadcasted_iota(jnp.int32, (128, 128), 1)
    low = lane < HEAD_DIM
    return low, low.astype(jnp.float32).astype(jnp.bfloat16), (~low).astype(jnp.float32).astype(jnp.bfloat16)


def attend_kernel(lo_ref, r_ref, o32_ref, o16_ref, lse_ref, s_ref):
    low, first_head, second_head = head_masks()
    row = lax.broadcasted_iota(jnp.int32, (256, 128), 0) % 128
    causal = row >= lax.broadcasted_iota(jnp.int32, (256, 128), 1)

    def one_query(q, _):
        query = r_ref[q, 4]
        stacked = jnp.concatenate([query * first_head, query * second_head], 0)
        lo = lo_ref[q]
        chunks = (q + 18 - lo) // 2

        def scores(kb):
            return mm(stacked, r_ref[kb & 15, (kb >> 4) * 2], 1, 1)

        def values(kb):
            return r_ref[kb & 15, (kb >> 4) * 2 + 1]

        s1 = jnp.where(causal, scores(q + 16), masked_score)
        s0 = jnp.where(q + 15 >= lo, scores(q + 15), masked_score)
        s_ref[0, :, :128] = s0
        s_ref[0, :, 128:] = s1

        def first(i, top):
            kb = q + 15 - 2 * i
            s1 = scores(kb + 1)
            s0 = jnp.where(kb >= lo, scores(kb), masked_score)
            s_ref[i, :, :128] = s0
            s_ref[i, :, 128:] = s1
            return jnp.maximum(top, jnp.maximum(s0, s1))

        top = lax.fori_loop(1, chunks, first, jnp.maximum(s0, s1))
        top = jnp.max(top, -1, keepdims=True)

        def second(i, carry):
            total, sums = carry
            kb = q + 15 - 2 * i
            p0 = jnp.exp(s_ref[i, :, :128] - top)
            p1 = jnp.exp(s_ref[i, :, 128:] - top)
            weights = jnp.concatenate([p0, p1], 1).astype(jnp.bfloat16)
            value = jnp.concatenate([values(kb), values(kb + 1)], 0)
            return total + p0 + p1, sums + mm(weights, value)

        empty = jnp.zeros((256, 128), jnp.float32)
        total, sums = lax.fori_loop(0, chunks, second, (empty, empty))
        total = jnp.sum(total, -1, keepdims=True)
        out = sums / total
        out = jnp.where(low, out[:128], out[128:])
        o32_ref[q] = out
        o16_ref[q] = out.astype(jnp.bfloat16)
        lse = jnp.broadcast_to(top + jnp.log(total), (256, 128))
        lse_ref[q] = jnp.transpose(lse)[:1]
        return 0

    lax.fori_loop(0, 16, one_query, 0)


def attend_call(lo, blocks):
    vmem = pl.BlockSpec(memory_space=pltpu.VMEM)
    return pl.pallas_call(
        attend_kernel,
        in_specs=[pl.BlockSpec(memory_space=pltpu.SMEM), vmem],
        out_specs=[vmem, vmem, vmem],
        out_shape=[
            jax.ShapeDtypeStruct((16, 128, 128), jnp.float32),
            jax.ShapeDtypeStruct((16, 128, 128), jnp.bfloat16),
            jax.ShapeDtypeStruct((16, 1, 256), jnp.float32),
        ],
        scratch_shapes=[pltpu.VMEM((8, 256, 256), jnp.float32)],
        compiler_params=pltpu.CompilerParams(vmem_limit_bytes=VMEM_LIMIT),
        cost_estimate=TINY,
    )(lo, blocks)


def attend_back_kernel(lo_ref, r_ref, do_ref, o32_ref, lse_ref, out_ref, dk_ref, dv_ref):
    low, first_head, second_head = head_masks()
    key_row = lax.broadcasted_iota(jnp.int32, (128, 256), 0)
    causal = key_row <= lax.broadcasted_iota(jnp.int32, (128, 256), 1) % 128
    dk_ref[...] = jnp.zeros_like(dk_ref)
    dv_ref[...] = jnp.zeros_like(dv_ref)

    def one_query(q, _):
        def stack(block):
            return jnp.concatenate([block * first_head, block * second_head], 0)

        queries = stack(r_ref[q, 4])
        grads = stack(do_ref[q])
        out = o32_ref[q]
        delta = grads.astype(jnp.float32) * jnp.concatenate([out, out], 0)
        delta = jnp.sum(jnp.transpose(delta), 0, keepdims=True)
        lse = lse_ref[q]
        lo = lo_ref[q]
        chunks = (q + 18 - lo) // 2

        def chunk(i, grad_query, mask1):
            kb = q + 15 - 2 * i

            def half(kb, mask):
                key = r_ref[kb & 15, (kb >> 4) * 2]
                value = r_ref[kb & 15, (kb >> 4) * 2 + 1]
                weights = jnp.exp(mm(key, queries, 1, 1) - lse)
                if mask is not None:
                    weights = jnp.where(mask, weights, 0.0)
                grad_scores = weights * (mm(value, grads, 1, 1) - delta)
                grad_scores = grad_scores.astype(jnp.bfloat16)
                dv_ref[kb] += mm(weights.astype(jnp.bfloat16), grads)
                dk_ref[kb] += mm(grad_scores, queries)
                return key, grad_scores

            key1, grad1 = half(kb + 1, mask1)
            key0, grad0 = half(kb, kb >= lo)
            keys = jnp.concatenate([key0, key1], 0)
            grad_scores = jnp.concatenate([grad0, grad1], 0)
            return grad_query + mm(grad_scores, keys, 0, 0)

        grad_query = chunk(0, jnp.zeros((256, 128), jnp.float32), causal)
        grad_query = lax.fori_loop(1, chunks, lambda i, g: chunk(i, g, None), grad_query)
        grad_query = jnp.where(low, grad_query[:128], grad_query[128:]) * score_scale
        out_ref[q, 4] = grad_query.astype(jnp.bfloat16)
        return 0

    lax.fori_loop(0, 16, one_query, 0)

    def finish(c, _):
        out_ref[c, 0] = dk_ref[c].astype(jnp.bfloat16)
        out_ref[c, 1] = dv_ref[c].astype(jnp.bfloat16)
        out_ref[c, 2] = dk_ref[c + 16].astype(jnp.bfloat16)
        out_ref[c, 3] = dv_ref[c + 16].astype(jnp.bfloat16)
        return 0

    lax.fori_loop(0, 16, finish, 0)


def attend_back_call(lo, blocks, grads, out, lse):
    vmem = pl.BlockSpec(memory_space=pltpu.VMEM)
    return pl.pallas_call(
        attend_back_kernel,
        in_specs=[pl.BlockSpec(memory_space=pltpu.SMEM), vmem, vmem, vmem, vmem],
        out_specs=vmem,
        out_shape=jax.ShapeDtypeStruct((16, 5, 128, 128), jnp.bfloat16),
        scratch_shapes=[
            pltpu.VMEM((32, 128, 128), jnp.float32),
            pltpu.VMEM((32, 128, 128), jnp.float32),
        ],
        compiler_params=pltpu.CompilerParams(vmem_limit_bytes=VMEM_LIMIT),
        cost_estimate=TINY,
    )(lo, blocks, grads, out, lse)


def turn_back_kernel(r_ref, halo_ref, cos_ref, up_ref, down_ref, out_ref, bias_ref):
    for j in range(2):
        sums = [jnp.zeros((1, 128), jnp.float32) for _ in range(3)]
        for x in range(4):
            rows = slice(x * 128, (x + 1) * 128)

            def turned(grad):
                return (
                    grad * cos_ref[rows]
                    - pltpu.roll(grad, 120, 1) * up_ref[rows]
                    - pltpu.roll(grad, 8, 1) * down_ref[rows]
                )

            def read(slot):
                later = r_ref[j, 0, x + 1, slot] if x < 3 else halo_ref[j, 0, slot]
                return r_ref[j, 0, x, slot + 2].astype(jnp.float32) + later.astype(jnp.float32)

            parts = (
                turned(r_ref[j, 0, x, 4].astype(jnp.float32)),
                turned(read(0)),
                read(1),
            )
            for part in range(3):
                grad = parts[part].astype(jnp.bfloat16)
                column = (j * 3 + part) * 128
                out_ref[0, rows, column : column + 128] = grad
                sums[part] = sums[part] + jnp.sum(grad.astype(jnp.float32), 0, keepdims=True)
        for part in range(3):
            column = (j * 3 + part) * 128
            bias_ref[0, :, column : column + 128] = sums[part]


def turn_back_call(blocks, halo, tables):
    table = pl.BlockSpec((512, 128), lambda h: (0, 0))
    return pl.pallas_call(
        turn_back_kernel,
        grid=(2,),
        in_specs=[
            pl.BlockSpec((2, 1, 4, 5, 128, 128), lambda h: (0, h, 0, 0, 0, 0)),
            pl.BlockSpec((2, 1, 2, 128, 128), lambda h: (0, h, 0, 0, 0)),
            table,
            table,
            table,
        ],
        out_specs=[
            pl.BlockSpec((1, 512, 768), lambda h: (h, 0, 0)),
            pl.BlockSpec((1, 1, 768), lambda h: (h, 0, 0)),
        ],
        out_shape=[
            jax.ShapeDtypeStruct((2, 512, 768), jnp.bfloat16),
            jax.ShapeDtypeStruct((2, 1, 768), jnp.float32),
        ],
        compiler_params=pltpu.CompilerParams(vmem_limit_bytes=VMEM_LIMIT),
        cost_estimate=TINY,
    )(blocks, halo, *tables)


def normed_back_kernel(core_ref, g_ref, own0_ref, own1_ref, oth0_ref, oth1_ref, out_ref):
    grads = jnp.concatenate([g_ref[0], g_ref[1]], 1)

    def rows(w0_ref, w1_ref):
        return jnp.concatenate(
            [w[:, :384] for h in range(2) for w in (w0_ref[0, h, 0, :128], w1_ref[h, 0, 0])], 1
        )

    weights = ordered(core_ref, rows(own0_ref, own1_ref), rows(oth0_ref, oth1_ref))
    out_ref[...] = mm(grads, weights, 1, 1).astype(jnp.bfloat16).reshape(4, 128, 256)


def normed_back_call(core, grad_joint, weights):
    first = pl.BlockSpec((1, 2, 1, 144, 512), lambda n: (n // 2, 0, n % 2, 0, 0))
    second = pl.BlockSpec((2, 1, 1, 128, 512), lambda n: (0, n % 2, n // 2, 0, 0))
    return pl.pallas_call(
        normed_back_kernel,
        grid=(8,),
        in_specs=[
            pl.BlockSpec(memory_space=pltpu.SMEM),
            pl.BlockSpec((2, 512, 768), lambda n: (0, 0, 0)),
            first,
            second,
            first,
            second,
        ],
        out_specs=pl.BlockSpec((4, 128, 256), lambda n: (0, 0, n)),
        out_shape=jax.ShapeDtypeStruct((4, 128, D), jnp.bfloat16),
        compiler_params=pltpu.CompilerParams(vmem_limit_bytes=VMEM_LIMIT),
        cost_estimate=TINY,
    )(core, grad_joint, *weights)


def local(
    tokens,
    cotangent,
    doc_ids,
    ln1_gain,
    ln1_shift,
    w_qkv,
    b_qkv,
    w_out,
    ln2_gain,
    ln2_shift,
    w_gate,
    w_up,
    w_down,
):
    half = lax.axis_index("yh")
    blk = lax.axis_index(BLK)

    core = lax.axis_index("k").reshape(1)
    vectors = jnp.stack([ln1_gain, ln1_shift, ln2_gain, ln2_shift])
    first_pair, second_pair = pack_joint_call(w_qkv.reshape(128, 768), w_out, vectors, b_qkv)
    ring = ring_gather(jnp.concatenate([tokens, cotangent], 0))
    own0 = gather(gather(first_pair, Y), ("z",)).reshape(4, 2, 2, 144, 512)
    own1 = gather(gather(second_pair, ("z",)), Y).reshape(2, 2, 4, 128, 512)
    own0 = after(own0, ring)
    weights = (own0, own1, swap_core(own0), swap_core(own1))
    rest = pack_hidden_call(w_gate, w_up, w_down)
    rest = after(rest, own0, own1)
    rest = lax.all_gather(rest, PLANE, axis=0, tiled=True).reshape(2, D, 3 * HID_PAD)

    small = jnp.stack([own0[:, :, :, 128:, :128], weights[2][:, :, :, 128:, :128]])
    small = jnp.where(core[0] == 0, small, small[::-1]).astype(jnp.float32)
    bias = small[..., 8:11, :16].transpose(2, 4, 1, 3, 0, 5).reshape(2, 3, 2, 128).reshape(2, 3, 1, 256)
    vectors = small[:, :, 0, :, :4].transpose(3, 1, 2, 0, 4).reshape(4, D)
    gain_one, shift_one, gain_two, shift_two = [vectors[i : i + 1] for i in range(4)]

    first_block = jnp.sum((doc_ids[None, :] < doc_ids[:, None]).astype(jnp.int32), axis=1)
    cycles = jnp.arange(4, dtype=jnp.int32) * 16 + half * 64 + blk
    cycles = jnp.concatenate([cycles, 48 + blk.reshape(1)])
    block_position = (cycles - first_block[cycles]) * BLK_TOK
    positions = (block_position[:, None] + jnp.arange(BLK_TOK, dtype=jnp.int32)).reshape(640)
    tables = rotary_tables(positions)
    first_query = half * 64 + (blk % 4) * 16
    lo = lax.dynamic_slice(first_block, (first_query,), (16,)) - (first_query - 16)

    before = lax.ppermute(ring[3, :128], ("yh",), [(0, 1)])
    payload, normed_one = qkv_call(core, ring, before, gain_one, shift_one, weights, bias, tables)
    blocks = exchange(payload.reshape(16, 5, 128, 128), BLK)
    att32, att16, lse = attend_call(lo, blocks)
    attended = exchange(att16, BLK).reshape(2, 2, 4, 128, 128)
    came = exchange(project_call(core, attended, weights), ("x",))
    token_shape = jax.ShapeDtypeStruct((128, D), jnp.float32)
    ring_shape = jax.ShapeDtypeStruct((4, 128, D), jnp.bfloat16)
    vector_shape = jax.ShapeDtypeStruct((1, D), jnp.float32)
    middle, normed_two = whole_call(
        middle_kernel, [token_shape, ring_shape], came, tokens, gain_two, shift_two
    )

    ring_two = exchange(normed_two, ("x",))
    active, grad_gu, ring_grad, ring_out = feed_forward_call(ring_two, ring, rest)
    shared = plane_grad_call(core, with_other(ring), with_other(active), HID_PAD, 1, 2 * HID_PAD)
    came = after(exchange(ring_grad, ("x",)), shared)
    grad_middle, ring_branch, grad_gain_two, grad_shift_two = whole_call(
        middle_back_kernel,
        [token_shape, ring_shape, vector_shape, vector_shape],
        came,
        middle,
        cotangent,
        gain_two,
    )
    shared = plane_grad_call(
        core, with_other(ring_two), with_other(grad_gu), 2 * HID_PAD, 0, 0, shared
    )
    ring_branch = after(exchange(ring_branch, ("x",)), shared)
    grad_att = project_back_call(core, ring_branch, weights).reshape(16, 128, 128)
    attended = attended.transpose(1, 2, 3, 0, 4).reshape(2, 512, 256)
    shared = plane_grad_call(
        core, with_other(ring_branch), with_other(attended), 256, 0, 3 * HID_PAD, shared
    )
    shared = lax.psum_scatter(
        shared.reshape(2048, SHARED), ("yh", "yl", "z"), scatter_dimension=0, tiled=True
    )
    grad_att = exchange(grad_att, BLK)

    out_came = exchange(after(ring_out, grad_att), ("x",))
    back = attend_back_call(lo, blocks, grad_att, att32, lse)
    mixed = whole_call(
        mixed_kernel, jax.ShapeDtypeStruct((128, D), jnp.bfloat16), after(out_came, back), middle
    )
    back = exchange(back, BLK).reshape(2, 2, 4, 5, 128, 128)
    back = after(back, mixed)
    halo_back = lax.ppermute(back[:, :, 0, :2], ("yh",), [(1, 0)])
    grad_joint, grad_bias = turn_back_call(back, halo_back, tables)
    ring_one = normed_back_call(core, grad_joint, weights)
    places = (chip_places(True), chip_places(False))
    joint_left, joint_right = with_other(normed_one), with_other(grad_joint)
    pair_parts = [
        weight_grad_call(core, places[j], joint_left, joint_right, j * 384, 384) for j in range(2)
    ]
    pair_came = [first_send(part, j == 0) for j, part in enumerate(pair_parts)]
    came = after(exchange(ring_one, ("x",)), pair_parts[0][0], pair_parts[1][0])
    input_grad, grad_gain_one, grad_shift_one = whole_call(
        input_back_kernel,
        [token_shape, vector_shape, vector_shape],
        came,
        tokens,
        grad_middle,
        gain_one,
    )
    pair_came = [second_send(first_sum(part, j == 0), j == 0) for j, part in enumerate(pair_came)]

    def shape(*dims):
        return jax.ShapeDtypeStruct(dims, jnp.float32)

    grad_gate, grad_up, grad_down, grad_out = whole_call(
        shared_end_kernel,
        [shape(128, HID), shape(128, HID), shape(HID, 128), shape(256, 128)],
        after(shared, input_grad),
    )
    grad_qkv = whole_call(joint_end_kernel, shape(128, 768), *pair_came[0], *pair_came[1])

    norms = jnp.concatenate([grad_gain_one, grad_shift_one, grad_gain_two, grad_shift_two], 0)
    norms = norms.reshape(4, 2, 4, 16, 16).transpose(1, 2, 3, 0, 4).reshape(2, 4, 16, 64)
    biases = grad_bias.reshape(2, 2, 3, 8, 16).transpose(0, 1, 3, 2, 4).reshape(2, 1, 16, 48)
    plane = jnp.arange(4).reshape(1, 4, 1, 1) == lax.axis_index("x")
    biases = jnp.where(plane, biases, 0.0)
    sums = jnp.concatenate([norms, biases, jnp.zeros((2, 4, 16, 16), jnp.float32)], 3)
    sums = jnp.sum(exchange(sums.reshape(128, 128), AXES), 0)
    norms = sums[:64].reshape(4, 16)

    return (
        mixed,
        input_grad,
        norms[0],
        norms[1],
        grad_qkv.reshape(128, 3, 256),
        sums[64:112].reshape(3, 16),
        grad_out,
        norms[2],
        norms[3],
        grad_gate,
        grad_up,
        grad_down,
    )


def solution(mesh):
    whole = Mesh(mesh.devices.reshape(2, 4, 4, 2, 2), AXES)
    ulysses, blk = ("yh", "x"), BLK
    both = ulysses + blk
    placed = (
        P(both, None),
        P(both, None),
        P(),
        P(blk),
        P(blk),
        P(blk, None, ulysses),
        P(None, both),
        P(ulysses, blk),
        P(blk),
        P(blk),
        P(blk, ulysses),
        P(blk, ulysses),
        P(ulysses, blk),
    )
    return jax.shard_map(
        local,
        mesh=whole,
        in_specs=placed,
        out_specs=(
            P(both, None),
            P(both, None),
            P(both),
            P(both),
            P(blk, None, ulysses),
            P(None, both),
            P(ulysses, blk),
            P(both),
            P(both),
            P(blk, ulysses),
            P(blk, ulysses),
            P(ulysses, blk),
        ),
        check_vma=False,
    )
```

time: 2150 us -> 675 us (0.31)
  waiting for transfers between devices: 1360 us -> 228 us
  matrix products: 374 us -> 0 us
  Pallas kernels: 0 us -> 192 us
  other arithmetic: 110 us -> 7.99 us
  blocking collectives: 159 us -> 95.6 us
  starting transfers between devices: 33.8 us -> 94.3 us
  local copies, waits for them, and re-layouts: 80.4 us -> 31.7 us
    ppermute x92 -> x36, waiting for transfers between devices: 641 us -> 58.1 us  [the longest x24 26.2 us: send(): return lax.ppermute(value, axes, [(i, (i + step) % 4) for i in range(4)])]
    dot_general x459 -> x0, matrix products: 374 us -> none  [the longest x124 135 us: head_scores(): jnp.einsum('cqd,ckd->cqk', query_all[..., columns], keys_band[..., column...]
    all_gather x9 -> x1, waiting for transfers between devices: 337 us -> 0.01 us  [local(): lax.all_gather(rest, PLANE, axis=0, tiled=True).reshape(2, D, 3 * HID_PAD)]
    reduce_scatter x5 -> x1, waiting for transfers between devices: 294 us -> 0.01 us  [local(): lax.psum_scatter(shared.reshape(2048, SHARED), ('yh', 'yl', 'z'), scatter...]
    pallas_call x0 -> x23, Pallas kernels: none -> 192 us  [the longest x1 37.7 us: feed_forward_call(): pl.pallas_call(feed_forward_kernel, grid=(2, 3), in_specs=[tokens, pl.Blo...]
    all_to_all x0 -> x8, waiting for transfers between devices: none -> 170 us  [exchange(): return lax.all_to_all(parts, axes, 0, 0, tiled=True)]
    all_to_all x0 -> x4, blocking collectives: none -> 95.6 us  [exchange(): return lax.all_to_all(parts, axes, 0, 0, tiled=True)]
    unnamed x24 -> x2, waiting for transfers between devices: 90.3 us -> 0.03 us
  transfers between devices with their start and end apart: 111 -> 46, of which waited for: 61 -> 19; matrix products, arithmetic and copies ran while one was open for 25% -> 4% of each run, Pallas kernels for 0% -> 27%
where the time goes in v1:
time: 675 us; the launch traced here: 665 us
  waiting for transfers between devices  228 us (34%)
  Pallas kernels  192 us (28%)
  blocking collectives  95.6 us (14%)
  starting transfers between devices  94.3 us (14%)
  local copies, waits for them, and re-layouts  31.7 us (5%)
  between operations  15.2 us (2%)
  other arithmetic  7.99 us (1%)
    all_to_all x8, waiting for transfers between devices, exchange(): return lax.all_to_all(parts, axes, 0, 0, tiled=True)  170 us
    all_to_all x4, blocking collectives, exchange(): return lax.all_to_all(parts, axes, 0, 0, tiled=True)  95.6 us
    all_to_all x8, starting transfers between devices, exchange(): return lax.all_to_all(parts, axes, 0, 0, tiled=True)  52.1 us
    pallas_call x1, Pallas kernels, feed_forward_call(): pl.pallas_call(feed_forward_kernel, grid=(2, 3), in_specs=[tokens, pl.Blo...  37.7 us
    ppermute x24, starting transfers between devices, send(): return lax.ppermute(value, axes, [(i, (i + step) % 4) for i in range(4)])  34.1 us
    pallas_call x3, Pallas kernels, plane_grad_call(): pl.pallas_call(plane_grad_kernel, grid=(columns // 256, 2), in_specs=[pl....  30.2 us
    ppermute x24, waiting for transfers between devices, send(): return lax.ppermute(value, axes, [(i, (i + step) % 4) for i in range(4)])  26.2 us
    pallas_call x1, Pallas kernels, attend_back_call(): pl.pallas_call(attend_back_kernel, in_specs=[pl.BlockSpec(memory_space=pl...  22.8 us
  transfers between devices with their start and end apart: 46, of which 19 were waited for; matrix products, arithmetic and copies ran while one was open for 4% of the time, Pallas kernels for 27%

profile of v1, /device:TPU:0, one launch (start us, length us, event | category | flops | bytes accessed | tf_op | source)
XLA Modules:
  0.0 665.1 jit_solution(14880084685811460587)
XLA Ops:
  25.2 5.0 all-to-all-start
  37.2 2.6 collective-permute-start.12
  46.2 7.6 %collective-permute-done.11 = bf16[4,128,512]{2,1,0:T(8,128)(2,1)S(1)} collective-permute-done((bf16[4,128,512]{2,1,0:T(8,128)(2,1)S(1)}, bf16[4,128,512]{2,1,0:T(8,128)(2,1)S(1)}, u32[]{:S(2)}, u32[]{:S(2)}) %collective-permute-start.11) | collective-permute-done | bytes 524320 | tf_op jit(solution)/shard_map/ppermute | solution.py:66
  55.6 6.1 collective-permute-done.12
  62.6 4.9 collective-permute-done.4
  67.7 10.3 %all-to-all-done.x_ref.cot_ref.left_ref = bf16[4,256,2048]{2,1,0:T(8,128)(2,1)} async-done(((bf16[4,256,2048]{2,1,0:T(8,128)(2,1)}), bf16[4,256,2048]{2,1,0:T(8,128)(2,1)}, u32[]{:S(2)}, u32[]{:S(2)}) %all-to-all-start) | async-done | bytes 4194336 | tf_op jit(solution)/shard_map/all_to_all | solution.py:43
  83.1 4.1 collective-permute-start
  91.6 18.4 %collective-permute-done.before_ref = bf16[128,2048]{1,0:T(8,128)(2,1)S(1)} collective-permute-done((bf16[128,2048]{1,0:T(8,128)(2,1)S(1)}, bf16[128,2048]{1,0:T(8,128)(2,1)S(1)}, u32[]{:S(2)}, u32[]{:S(2)}) %collective-permute-start) | collective-permute-done | bytes 524320 | tf_op jit(solution)/shard_map/ppermute | solution.py:890
  110.9 14.2 %shard_map.221 = (bf16[2,2,4,5,128,128]{5,4,3,2,1,0:T(8,128)(2,1)}, bf16[4,128,2048]{2,1,0:T(8,128)(2,1)}) custom-call(s32[1]{0:T(128)} %bitcast.core_ref, bf16[4,256,2048]{2,1,0:T(8,128)(2,1)} %all-to-all-done.x_ref.cot_ref.left_ref, bf16[128,2048]{1,0:T(8,128)(2,1)} %copy-done.10, f32[1,2048]{1,0:T(1,128)} %bitcast.112, f32[1,2048]{1,0:T(1,128)} %bitcast.116, ...), custom_call_target="tpu_custom_call" | custom-call | flops 1 | bytes 1 | tf_op jit(solution)/shard_map/pallas_call | solution.py:239
  125.1 4.5 all-to-all-start.1
  130.2 61.1 %all-to-all-done.1.r_ref = bf16[16,5,128,128]{3,2,1,0:T(8,128)(2,1)} async-done(((bf16[16,5,128,128]{3,2,1,0:T(8,128)(2,1)}), bf16[16,5,128,128]{3,2,1,0:T(8,128)(2,1)}, u32[]{:S(2)}, u32[]{:S(2)}) %all-to-all-start.1) | async-done | bytes 2621472 | tf_op jit(solution)/shard_map/all_to_all | solution.py:43
  191.3 19.2 %shard_map.222 = (f32[16,128,128]{2,1,0:T(8,128)}, bf16[16,128,128]{2,1,0:T(8,128)(2,1)}, f32[16,1,256]{2,1,0:T(1,128)}) custom-call(s32[16]{0:T(128)} %dynamic-slice_subtract_fusion.lo_ref, bf16[16,5,128,128]{3,2,1,0:T(8,128)(2,1)} %all-to-all-done.1.r_ref), custom_call_target="tpu_custom_call" | custom-call | flops 1 | bytes 1 | tf_op jit(solution)/shard_map/pallas_call | solution.py:665
  210.5 28.6 %all_to_all.64 = bf16[16,128,128]{2,1,0:T(8,128)(2,1)} all-to-all(bf16[16,128,128]{2,1,0:T(8,128)(2,1)} %get-tuple-element.67), channel_id=1, replica_groups=mesh['yh'=2,'x'=4,'z'=4,'yl'=2,'k'=2] {'z','yl','k'}, dimensions={0} | all-to-all | bytes 1048576 | tf_op jit(solution)/shard_map/all_to_all | solution.py:43
  239.1 7.2 %shard_map.223 = bf16[4,128,2048]{2,1,0:T(8,128)(2,1)} custom-call(s32[1]{0:T(128)} %bitcast.core_ref, bf16[2,2,4,128,128]{4,3,2,1,0:T(8,128)(2,1)} %bitcast.103, bf16[4,2,2,144,512]{4,3,2,1,0:T(8,128)(2,1)} %bitcast.93, bf16[2,2,4,128,512]{4,3,2,1,0:T(8,128)(2,1)} %bitcast.98, bf16[4,2,2,144,512]{4,3,2,1,0:T(8,128)(2,1)} %collective-permute-done.7.oth0_ref, ...), custom_call_target="tpu_custom_call" | custom-call | flops 1 | bytes 1 | tf_op jit(solution)/shard_map/pallas_call | solution.py:367
  246.3 3.6 all-to-all-start.3
  251.2 24.8 %all-to-all-done.3.came_ref = bf16[4,128,2048]{2,1,0:T(8,128)(2,1)S(1)} async-done(((bf16[4,128,2048]{2,1,0:T(8,128)(2,1)}), bf16[4,128,2048]{2,1,0:T(8,128)(2,1)S(1)}, u32[]{:S(2)}, u32[]{:S(2)}) %all-to-all-start.3) | async-done | bytes 2097184 | tf_op jit(solution)/shard_map/all_to_all | solution.py:43
  277.4 3.9 shard_map.224
  281.3 30.0 %all_to_all.65.x_ref.left_ref = bf16[4,128,2048]{2,1,0:T(8,128)(2,1)} all-to-all(bf16[4,128,2048]{2,1,0:T(8,128)(2,1)} %get-tuple-element.68), channel_id=1, replica_groups=mesh['yh'=2,'x'=4,'z'=4,'yl'=2,'k'=2] {'x'}, dimensions={0} | all-to-all | bytes 4194304 | tf_op jit(solution)/shard_map/all_to_all | solution.py:43
  311.4 37.7 %shard_map.226 = (bf16[2,512,768]{2,1,0:T(8,128)(2,1)}, bf16[2,512,1536]{2,1,0:T(8,128)(2,1)}, bf16[4,128,2048]{2,1,0:T(8,128)(2,1)}, bf16[4,128,2048]{2,1,0:T(8,128)(2,1)}) custom-call(bf16[4,128,2048]{2,1,0:T(8,128)(2,1)} %all_to_all.65.x_ref.left_ref, bf16[4,256,2048]{2,1,0:T(8,128)(2,1)} %all-to-all-done.x_ref.cot_ref.left_ref, ...), custom_call_target="tpu_custom_call" | custom-call | flops 1 | bytes 1 | tf_op jit(solution)/shard_map/pallas_call | solution.py:454
  349.2 4.6 all-to-all-start.5
  354.5 9.4 %shard_map.227.refs_0_ = bf16[2,2,4,128,2560]{4,3,2,1,0:T(8,128)(2,1)} custom-call(s32[1]{0:T(128)} %bitcast.core_ref, bf16[4,256,2048]{2,1,0:T(8,128)(2,1)} %all-to-all-done.x_ref.cot_ref.left_ref, bf16[4,256,2048]{2,1,0:T(8,128)(2,1)} %collective-permute-done.15.left_other_ref, bf16[2,512,768]{2,1,0:T(8,128)(2,1)} %get-tuple-element.72.right_ref, ...), custom_call_target="tpu_custom_call" | custom-call | flops 1 | bytes 1 | tf_op jit(solution)/shard_map/pallas_call | solution.py:495
  363.9 17.2 %all-to-all-done.5.came_ref = bf16[4,128,2048]{2,1,0:T(8,128)(2,1)} async-done(((bf16[4,128,2048]{2,1,0:T(8,128)(2,1)}), bf16[4,128,2048]{2,1,0:T(8,128)(2,1)}, u32[]{:S(2)}, u32[]{:S(2)}) %all-to-all-start.5) | async-done | bytes 2097184 | tf_op jit(solution)/shard_map/all_to_all | solution.py:43
  381.1 4.9 shard_map.228
  386.0 4.4 all-to-all-start.6
  390.5 15.4 %shard_map.229.refs_0_ = bf16[2,2,4,128,2560]{4,3,2,1,0:T(8,128)(2,1)} custom-call(s32[1]{0:T(128)} %bitcast.core_ref, bf16[4,128,2048]{2,1,0:T(8,128)(2,1)} %all_to_all.65.x_ref.left_ref, bf16[4,128,2048]{2,1,0:T(8,128)(2,1)} %collective-permute-done.17.left_other_ref, ...), custom_call_target="tpu_custom_call", output_to_operand_aliasing={{}: (5, {})} | custom-call | flops 1 | bytes 1 | tf_op jit(solution)/shard_map/pallas_call | solution.py:495
  405.9 11.1 %all-to-all-done.6.grad_ref.left_ref = bf16[4,128,2048]{2,1,0:T(8,128)(2,1)} async-done(((bf16[4,128,2048]{2,1,0:T(8,128)(2,1)}), bf16[4,128,2048]{2,1,0:T(8,128)(2,1)}, u32[]{:S(2)}, u32[]{:S(2)}) %all-to-all-start.6) | async-done | bytes 2097184 | tf_op jit(solution)/shard_map/all_to_all | solution.py:43
  418.6 3.2 collective-permute-done.35.right_other_ref
  424.1 5.3 shard_map.241
  429.5 4.2 shard_map.230
  433.7 21.0 %all_to_all.66.do_ref = bf16[16,128,128]{2,1,0:T(8,128)(2,1)} all-to-all(bf16[16,128,128]{2,1,0:T(8,128)(2,1)} %bitcast.106), channel_id=1, replica_groups=mesh['yh'=2,'x'=4,'z'=4,'yl'=2,'k'=2] {'z','yl','k'}, dimensions={0} | all-to-all | bytes 1048576 | tf_op jit(solution)/shard_map/all_to_all | solution.py:43
  454.7 3.6 all-to-all-start.8
  458.3 22.8 %shard_map.231 = bf16[16,5,128,128]{3,2,1,0:T(8,128)(2,1)} custom-call(s32[16]{0:T(128)} %dynamic-slice_subtract_fusion.lo_ref, bf16[16,5,128,128]{3,2,1,0:T(8,128)(2,1)} %all-to-all-done.1.r_ref, bf16[16,128,128]{2,1,0:T(8,128)(2,1)} %all_to_all.66.do_ref, f32[16,128,128]{2,1,0:T(8,128)} %get-tuple-element.79.o32_ref, f32[16,1,256]{2,1,0:T(1,128)} %get-tuple-element.80.lse_ref), custom_call_target="tpu_custom_call" | custom-call | flops 1 | bytes 1 | tf_op jit(solution)/shard_map/pallas_call | solution.py:741
  481.2 3.7 all-to-all-done.8.came_ref
  486.2 22.3 %all-to-all-start.9 = ((bf16[16,5,128,128]{3,2,1,0:T(8,128)(2,1)}), bf16[16,5,128,128]{3,2,1,0:T(8,128)(2,1)S(1)}, u32[]{:S(2)}, u32[]{:S(2)}) async-start(bf16[16,5,128,128]{3,2,1,0:T(8,128)(2,1)} %shard_map.231), calls=%async_computation.9 | async-start | bytes 5242880 | tf_op jit(solution)/shard_map/all_to_all | solution.py:43
  508.9 3.0 shard_map.232
  511.9 34.8 %all-to-all-done.9 = bf16[16,5,128,128]{3,2,1,0:T(8,128)(2,1)S(1)} async-done(((bf16[16,5,128,128]{3,2,1,0:T(8,128)(2,1)}), bf16[16,5,128,128]{3,2,1,0:T(8,128)(2,1)S(1)}, u32[]{:S(2)}, u32[]{:S(2)}) %all-to-all-start.9) | async-done | bytes 2621472 | tf_op jit(solution)/shard_map/all_to_all | solution.py:43
  548.0 10.2 %collective-permute-done.19.halo_ref = bf16[2,2,2,128,128]{4,3,2,1,0:T(8,128)(2,1)S(1)} collective-permute-done((bf16[2,2,2,128,128]{4,3,2,1,0:T(8,128)(2,1)S(1)}, bf16[2,2,2,128,128]{4,3,2,1,0:T(8,128)(2,1)S(1)}, u32[]{:S(2)}, u32[]{:S(2)}) %collective-permute-start.19) | collective-permute-done | bytes 262176 | tf_op jit(solution)/shard_map/ppermute | solution.py:936
  558.9 3.7 shard_map.233
  562.6 9.9 %shard_map.234 = bf16[4,128,2048]{2,1,0:T(8,128)(2,1)} custom-call(s32[1]{0:T(128)} %bitcast.core_ref, bf16[2,512,768]{2,1,0:T(8,128)(2,1)} %get-tuple-element.83.g_ref.right_ref, bf16[4,2,2,144,512]{4,3,2,1,0:T(8,128)(2,1)} %bitcast.95, bf16[2,2,4,128,512]{4,3,2,1,0:T(8,128)(2,1)} %bitcast.100, ...), custom_call_target="tpu_custom_call" | custom-call | flops 1 | bytes 1 | tf_op jit(solution)/shard_map/pallas_call | solution.py:827
  572.5 4.1 all-to-all-start.10
  577.2 7.3 %shard_map.236 = (bf16[4,128,384]{2,1,0:T(8,128)(2,1)}, bf16[4,128,384]{2,1,0:T(8,128)(2,1)}, bf16[4,128,384]{2,1,0:T(8,128)(2,1)}, bf16[4,128,384]{2,1,0:T(8,128)(2,1)}) custom-call(s32[1]{0:T(128)} %bitcast.core_ref, s32[2,16]{1,0:T(2,128)} %pad_add_fusion.1.place_ref, bf16[4,128,2048]{2,1,0:T(8,128)(2,1)} %get-tuple-element.84.left_ref, ...), custom_call_target="tpu_custom_call" | custom-call | flops 1 | bytes 1 | tf_op jit(solution)/shard_map/pallas_call | solution.py:542
  585.9 3.1 collective-permute-start.29
  589.1 7.3 %shard_map.235 = (bf16[4,128,384]{2,1,0:T(8,128)(2,1)}, bf16[4,128,384]{2,1,0:T(8,128)(2,1)}, bf16[4,128,384]{2,1,0:T(8,128)(2,1)}, bf16[4,128,384]{2,1,0:T(8,128)(2,1)}) custom-call(s32[1]{0:T(128)} %bitcast.core_ref, s32[2,16]{1,0:T(2,128)} %pad_add_fusion.place_ref, bf16[4,128,2048]{2,1,0:T(8,128)(2,1)} %get-tuple-element.84.left_ref, ...), custom_call_target="tpu_custom_call" | custom-call | flops 1 | bytes 1 | tf_op jit(solution)/shard_map/pallas_call | solution.py:542
  596.4 7.1 %all-to-all-done.10.came_ref = bf16[4,128,2048]{2,1,0:T(8,128)(2,1)S(1)} async-done(((bf16[4,128,2048]{2,1,0:T(8,128)(2,1)}), bf16[4,128,2048]{2,1,0:T(8,128)(2,1)S(1)}, u32[]{:S(2)}, u32[]{:S(2)}) %all-to-all-start.10) | async-done | bytes 2097184 | tf_op jit(solution)/shard_map/all_to_all | solution.py:43
  603.9 3.1 collective-permute-start.23
  607.0 4.1 shard_map.237
  615.7 15.9 %all_to_all.67 = f32[128,1,128]{2,1,0:T(1,128)S(1)} all-to-all(f32[128,1,128]{2,1,0:T(1,128)S(1)} %copy.108), channel_id=1, replica_groups=mesh['yh'=2,'x'=4,'z'=4,'yl'=2,'k'=2] {'yh','x','z','yl','k'}, dimensions={0} | all-to-all | bytes 131072 | tf_op jit(solution)/shard_map/all_to_all | solution.py:43
  644.5 2.7 collective-permute-done.27.refs_3_
  (226 shorter events, 86.5 us)
Async XLA Ops:
  12.1 22.1 %collective-permute-start.8 = (bf16[128,512]{1,0:T(8,128)(2,1)}, bf16[128,512]{1,0:T(8,128)(2,1)S(1)}, u32[]{:S(2)}, u32[]{:S(2)}) collective-permute-start(bf16[128,512]{1,0:T(8,128)(2,1)} %get-tuple-element.65), channel_id=1, source_target_pairs={{0,4},{4,8},{8,12},{12,0},{1,5},{5,9},{9,13},{13,1},{2,6},{6,10},{... | collective-permute-start | bytes 393224 | tf_op jit(solution)/shard_map/ppermute | solution.py:66
  14.1 22.2 %collective-permute-start.9 = (bf16[128,512]{1,0:T(8,128)(2,1)}, bf16[128,512]{1,0:T(8,128)(2,1)S(1)}, u32[]{:S(2)}, u32[]{:S(2)}) collective-permute-start(bf16[128,512]{1,0:T(8,128)(2,1)} %get-tuple-element.65), channel_id=1, source_target_pairs={{0,12},{4,0},{8,4},{12,8},{1,13},{5,1},{9,5},{13,9},{2,14},{6,2},{... | collective-permute-start | bytes 393224 | tf_op jit(solution)/shard_map/ppermute | solution.py:66
  16.2 20.1 %collective-permute-start.10 = (bf16[128,512]{1,0:T(8,128)(2,1)}, bf16[128,512]{1,0:T(8,128)(2,1)S(1)}, u32[]{:S(2)}, u32[]{:S(2)}) collective-permute-start(bf16[128,512]{1,0:T(8,128)(2,1)} %get-tuple-element.65), channel_id=1, source_target_pairs={{0,8},{4,12},{8,0},{12,4},{1,9},{5,13},{9,1},{13,5},{2,10},{6,14},... | collective-permute-start | bytes 393224 | tf_op jit(solution)/shard_map/ppermute | solution.py:66
  18.1 21.9 %collective-permute-start.1 = (bf16[144,512]{1,0:T(8,128)(2,1)}, bf16[144,512]{1,0:T(8,128)(2,1)S(1)}, u32[]{:S(2)}, u32[]{:S(2)}) collective-permute-start(bf16[144,512]{1,0:T(8,128)(2,1)} %get-tuple-element.63), channel_id=1, source_target_pairs={{0,2},{2,64},{64,66},{66,0},{1,3},{3,65},{65,67},{67,1},{4,6},{6,6... | collective-permute-start | bytes 442376 | tf_op jit(solution)/shard_map/ppermute | solution.py:66
  19.7 20.7 %collective-permute-start.2 = (bf16[144,512]{1,0:T(8,128)(2,1)}, bf16[144,512]{1,0:T(8,128)(2,1)S(1)}, u32[]{:S(2)}, u32[]{:S(2)}) collective-permute-start(bf16[144,512]{1,0:T(8,128)(2,1)} %get-tuple-element.63), channel_id=1, source_target_pairs={{0,66},{2,0},{64,2},{66,64},{1,67},{3,1},{65,3},{67,65},{4,70},{6,... | collective-permute-start | bytes 442376 | tf_op jit(solution)/shard_map/ppermute | solution.py:66
  25.2 52.8 %all-to-all-start = ((bf16[4,256,2048]{2,1,0:T(8,128)(2,1)}), bf16[4,256,2048]{2,1,0:T(8,128)(2,1)}, u32[]{:S(2)}, u32[]{:S(2)}) async-start(bf16[4,256,2048]{2,1,0:T(8,128)(2,1)} %broadcast_in_dim.121), calls=%async_computation | async-start | bytes 8388608 | tf_op jit(solution)/shard_map/all_to_all | solution.py:43
  30.2 281.2 %all-gather.2.cloned.1.call-start = ((), (), s32[]{:S(2)}) async-start(), calls=%async_computation.13 | async-start | bytes 19464192 | tf_op jit(solution)/shard_map/all_gather | solution.py:873
  34.3 8.4 %collective-permute-start.3 = (bf16[144,512]{1,0:T(8,128)(2,1)S(1)}, bf16[144,512]{1,0:T(8,128)(2,1)S(1)}, u32[]{:S(2)}, u32[]{:S(2)}) collective-permute-start(bf16[144,512]{1,0:T(8,128)(2,1)S(1)} %copy-done.20), channel_id=1, source_target_pairs={{0,64},{2,66},{64,0},{66,2},{1,65},{3,67},{65,1},{67,3},{4,68},{6,... | collective-permute-start | bytes 442376 | tf_op jit(solution)/shard_map/ppermute | solution.py:66
  36.4 17.5 %collective-permute-start.11 = (bf16[4,128,512]{2,1,0:T(8,128)(2,1)S(1)}, bf16[4,128,512]{2,1,0:T(8,128)(2,1)S(1)}, u32[]{:S(2)}, u32[]{:S(2)}) collective-permute-start(bf16[4,128,512]{2,1,0:T(8,128)(2,1)S(1)} %bitcast_dynamic-update-slice_fusion.12), channel_id=1, source_target_pairs={{0,2},{2,64},{64,66},{66,0},{1,3},{3,65},{65,67},{67,1},{4,6},{6,6... | collective-permute-start | bytes 1572872 | tf_op jit(solution)/shard_map/ppermute | solution.py:66
  37.2 24.5 %collective-permute-start.12 = (bf16[4,128,512]{2,1,0:T(8,128)(2,1)S(1)}, bf16[4,128,512]{2,1,0:T(8,128)(2,1)S(1)}, u32[]{:S(2)}, u32[]{:S(2)}) collective-permute-start(bf16[4,128,512]{2,1,0:T(8,128)(2,1)S(1)} %bitcast_dynamic-update-slice_fusion.12), channel_id=1, source_target_pairs={{0,66},{2,0},{64,2},{66,64},{1,67},{3,1},{65,3},{67,65},{4,70},{6,... | collective-permute-start | bytes 1572872 | tf_op jit(solution)/shard_map/ppermute | solution.py:66
  40.0 22.6 %collective-permute-start.13 = (bf16[4,128,512]{2,1,0:T(8,128)(2,1)S(1)}, bf16[4,128,512]{2,1,0:T(8,128)(2,1)S(1)}, u32[]{:S(2)}, u32[]{:S(2)}) collective-permute-start(bf16[4,128,512]{2,1,0:T(8,128)(2,1)S(1)} %bitcast_dynamic-update-slice_fusion.12), channel_id=1, source_target_pairs={{0,64},{2,66},{64,0},{66,2},{1,65},{3,67},{65,1},{67,3},{4,68},{6,... | collective-permute-start | bytes 1572872 | tf_op jit(solution)/shard_map/ppermute | solution.py:66
  42.6 24.9 %collective-permute-start.4 = (bf16[4,144,512]{2,1,0:T(8,128)(2,1)S(1)}, bf16[4,144,512]{2,1,0:T(8,128)(2,1)S(1)}, u32[]{:S(2)}, u32[]{:S(2)}) collective-permute-start(bf16[4,144,512]{2,1,0:T(8,128)(2,1)S(1)} %bitcast_dynamic-update-slice_fusion.8), channel_id=1, source_target_pairs={{0,4},{4,8},{8,12},{12,0},{1,5},{5,9},{9,13},{13,1},{2,6},{6,10},{... | collective-permute-start | bytes 1769480 | tf_op jit(solution)/shard_map/ppermute | solution.py:66
  43.7 23.8 %collective-permute-start.5 = (bf16[4,144,512]{2,1,0:T(8,128)(2,1)S(1)}, bf16[4,144,512]{2,1,0:T(8,128)(2,1)S(1)}, u32[]{:S(2)}, u32[]{:S(2)}) collective-permute-start(bf16[4,144,512]{2,1,0:T(8,128)(2,1)S(1)} %bitcast_dynamic-update-slice_fusion.8), channel_id=1, source_target_pairs={{0,12},{4,0},{8,4},{12,8},{1,13},{5,1},{9,5},{13,9},{2,14},{6,2},{... | collective-permute-start | bytes 1769480 | tf_op jit(solution)/shard_map/ppermute | solution.py:66
  53.9 13.8 %collective-permute-start.6 = (bf16[4,144,512]{2,1,0:T(8,128)(2,1)S(1)}, bf16[4,144,512]{2,1,0:T(8,128)(2,1)S(1)}, u32[]{:S(2)}, u32[]{:S(2)}) collective-permute-start(bf16[4,144,512]{2,1,0:T(8,128)(2,1)S(1)} %bitcast_dynamic-update-slice_fusion.8), channel_id=1, source_target_pairs={{0,8},{4,12},{8,0},{12,4},{1,9},{5,13},{9,1},{13,5},{2,10},{6,14},... | collective-permute-start | bytes 1769480 | tf_op jit(solution)/shard_map/ppermute | solution.py:66
  67.7 21.1 %copy-start = (bf16[4,4,144,512]{3,2,1,0:T(8,128)(2,1)}, bf16[4,4,144,512]{3,2,1,0:T(8,128)(2,1)S(1)}, u32[]{:S(2)}) copy-start(bf16[4,4,144,512]{3,2,1,0:T(8,128)(2,1)S(1)} %bitcast_dynamic-update-slice_fusion) | copy-start | bytes 7077892
  78.0 9.1 %collective-permute-start.7 = (bf16[4,2,2,144,512]{4,3,2,1,0:T(8,128)(2,1)S(1)}, bf16[4,2,2,144,512]{4,3,2,1,0:T(8,128)(2,1)}, u32[]{:S(2)}, u32[]{:S(2)}) collective-permute-start(bf16[4,2,2,144,512]{4,3,2,1,0:T(8,128)(2,1)S(1)} %bitcast.90), channel_id=1, source_target_pairs={{0,1},{1,0},{2,3},{3,2},{4,5},{5,4},{6,7},{7,6},{8,9},{9,8},{10,11... | collective-permute-start | bytes 7077896 | tf_op jit(solution)/shard_map/ppermute | solution.py:39
  79.4 12.3 %collective-permute-start.14 = (bf16[2,2,4,128,512]{4,3,2,1,0:T(8,128)(2,1)}, bf16[2,2,4,128,512]{4,3,2,1,0:T(8,128)(2,1)}, u32[]{:S(2)}, u32[]{:S(2)}) collective-permute-start(bf16[2,2,4,128,512]{4,3,2,1,0:T(8,128)(2,1)} %bitcast.96), channel_id=1, source_target_pairs={{0,1},{1,0},{2,3},{3,2},{4,5},{5,4},{6,7},{7,6},{8,9},{9,8},{10,11... | collective-permute-start | bytes 6291464 | tf_op jit(solution)/shard_map/ppermute | solution.py:39
  83.1 27.0 %collective-permute-start = (bf16[128,2048]{1,0:T(8,128)(2,1)S(1)}, bf16[128,2048]{1,0:T(8,128)(2,1)S(1)}, u32[]{:S(2)}, u32[]{:S(2)}) collective-permute-start(bf16[128,2048]{1,0:T(8,128)(2,1)S(1)} %slice_bitcast_fusion), channel_id=1, source_target_pairs={{0,64},{1,65},{2,66},{3,67},{4,68},{5,69},{6,70},{7,71},{8,72},{9,... | collective-permute-start | bytes 1572872 | tf_op jit(solution)/shard_map/ppermute | solution.py:890
  125.1 66.2 %all-to-all-start.1 = ((bf16[16,5,128,128]{3,2,1,0:T(8,128)(2,1)}), bf16[16,5,128,128]{3,2,1,0:T(8,128)(2,1)}, u32[]{:S(2)}, u32[]{:S(2)}) async-start(bf16[16,5,128,128]{3,2,1,0:T(8,128)(2,1)} %bitcast.105), calls=%async_computation.1 | async-start | bytes 5242880 | tf_op jit(solution)/shard_map/all_to_all | solution.py:43
  246.3 29.7 %all-to-all-start.3 = ((bf16[4,128,2048]{2,1,0:T(8,128)(2,1)}), bf16[4,128,2048]{2,1,0:T(8,128)(2,1)S(1)}, u32[]{:S(2)}, u32[]{:S(2)}) async-start(bf16[4,128,2048]{2,1,0:T(8,128)(2,1)} %shard_map.223), calls=%async_computation.3 | async-start | bytes 4194304 | tf_op jit(solution)/shard_map/all_to_all | solution.py:43
  249.9 104.5 %collective-permute-start.15 = (bf16[4,256,2048]{2,1,0:T(8,128)(2,1)}, bf16[4,256,2048]{2,1,0:T(8,128)(2,1)}, u32[]{:S(2)}, u32[]{:S(2)}) collective-permute-start(bf16[4,256,2048]{2,1,0:T(8,128)(2,1)} %all-to-all-done.x_ref.cot_ref.left_ref), channel_id=1, source_target_pairs={{0,1},{1,0},{2,3},{3,2},{4,5},{5,4},{6,7},{7,6},{8,9},{9,8},{10,11... | collective-permute-start | bytes 12582920 | tf_op jit(solution)/shard_map/ppermute | solution.py:39
  349.1 5.4 collective-permute-start.16
  349.2 31.9 %all-to-all-start.5 = ((bf16[4,128,2048]{2,1,0:T(8,128)(2,1)}), bf16[4,128,2048]{2,1,0:T(8,128)(2,1)}, u32[]{:S(2)}, u32[]{:S(2)}) async-start(bf16[4,128,2048]{2,1,0:T(8,128)(2,1)} %get-tuple-element.71), calls=%async_computation.5 | async-start | bytes 4194304 | tf_op jit(solution)/shard_map/all_to_all | solution.py:43
  353.8 36.7 %collective-permute-start.18 = (bf16[2,512,1536]{2,1,0:T(8,128)(2,1)}, bf16[2,512,1536]{2,1,0:T(8,128)(2,1)}, u32[]{:S(2)}, u32[]{:S(2)}) collective-permute-start(bf16[2,512,1536]{2,1,0:T(8,128)(2,1)} %get-tuple-element.76.right_ref), channel_id=1, source_target_pairs={{0,1},{1,0},{2,3},{3,2},{4,5},{5,4},{6,7},{7,6},{8,9},{9,8},{10,11... | collective-permute-start | bytes 9437192 | tf_op jit(solution)/shard_map/ppermute | solution.py:39
  354.3 36.2 %collective-permute-start.17 = (bf16[4,128,2048]{2,1,0:T(8,128)(2,1)S(1)}, bf16[4,128,2048]{2,1,0:T(8,128)(2,1)}, u32[]{:S(2)}, u32[]{:S(2)}) collective-permute-start(bf16[4,128,2048]{2,1,0:T(8,128)(2,1)S(1)} %copy-done.2), channel_id=1, source_target_pairs={{0,1},{1,0},{2,3},{3,2},{4,5},{5,4},{6,7},{7,6},{8,9},{9,8},{10,11... | collective-permute-start | bytes 6291464 | tf_op jit(solution)/shard_map/ppermute | solution.py:39
  386.0 31.0 %all-to-all-start.6 = ((bf16[4,128,2048]{2,1,0:T(8,128)(2,1)}), bf16[4,128,2048]{2,1,0:T(8,128)(2,1)}, u32[]{:S(2)}, u32[]{:S(2)}) async-start(bf16[4,128,2048]{2,1,0:T(8,128)(2,1)} %get-tuple-element.75), calls=%async_computation.6 | async-start | bytes 4194304 | tf_op jit(solution)/shard_map/all_to_all | solution.py:43
  390.4 26.5 %copy-start.7 = (bf16[16,128,128]{2,1,0:T(8,128)(2,1)S(1)}, bf16[16,128,128]{2,1,0:T(8,128)(2,1)}, u32[]{:S(2)}) copy-start(bf16[16,128,128]{2,1,0:T(8,128)(2,1)} %all_to_all.64) | copy-start | bytes 1572868
  390.5 261.5 %reduce-scatter.2.cloned.1.call-start = ((), (), s32[]{:S(2)}) async-start(), calls=%async_computation.14 | async-start | bytes 11141120 | tf_op jit(solution)/shard_map/reduce_scatter | solution.py:924
  417.0 4.9 collective-permute-start.34
  417.9 4.0 collective-permute-start.35
  454.7 30.1 %all-to-all-start.8 = ((bf16[4,128,2048]{2,1,0:T(8,128)(2,1)}), bf16[4,128,2048]{2,1,0:T(8,128)(2,1)S(1)}, u32[]{:S(2)}, u32[]{:S(2)}) async-start(bf16[4,128,2048]{2,1,0:T(8,128)(2,1)} %get-tuple-element.78), calls=%async_computation.8 | async-start | bytes 4194304 | tf_op jit(solution)/shard_map/all_to_all | solution.py:43
  486.2 60.5 %all-to-all-start.9 = ((bf16[16,5,128,128]{3,2,1,0:T(8,128)(2,1)}), bf16[16,5,128,128]{3,2,1,0:T(8,128)(2,1)S(1)}, u32[]{:S(2)}, u32[]{:S(2)}) async-start(bf16[16,5,128,128]{3,2,1,0:T(8,128)(2,1)} %shard_map.231), calls=%async_computation.9 | async-start | bytes 5242880 | tf_op jit(solution)/shard_map/all_to_all | solution.py:43
  508.5 68.7 %collective-permute-start.20 = (bf16[4,128,2048]{2,1,0:T(8,128)(2,1)}, bf16[4,128,2048]{2,1,0:T(8,128)(2,1)}, u32[]{:S(2)}, u32[]{:S(2)}) collective-permute-start(bf16[4,128,2048]{2,1,0:T(8,128)(2,1)} %get-tuple-element.84.left_ref), channel_id=1, source_target_pairs={{0,1},{1,0},{2,3},{3,2},{4,5},{5,4},{6,7},{7,6},{8,9},{9,8},{10,11... | collective-permute-start | bytes 6291464 | tf_op jit(solution)/shard_map/ppermute | solution.py:39
  546.7 11.5 %collective-permute-start.19 = (bf16[2,2,2,128,128]{4,3,2,1,0:T(8,128)(2,1)S(1)}, bf16[2,2,2,128,128]{4,3,2,1,0:T(8,128)(2,1)S(1)}, u32[]{:S(2)}, u32[]{:S(2)}) collective-permute-start(bf16[2,2,2,128,128]{4,3,2,1,0:T(8,128)(2,1)S(1)} %slice_bitcast_fusion.1), channel_id=1, source_target_pairs={{64,0},{65,1},{66,2},{67,3},{68,4},{69,5},{70,6},{71,7},{72,8},{73... | collective-permute-start | bytes 786440 | tf_op jit(solution)/shard_map/ppermute | solution.py:936
  562.6 14.6 %collective-permute-start.21 = (bf16[2,512,768]{2,1,0:T(8,128)(2,1)}, bf16[2,512,768]{2,1,0:T(8,128)(2,1)}, u32[]{:S(2)}, u32[]{:S(2)}) collective-permute-start(bf16[2,512,768]{2,1,0:T(8,128)(2,1)} %get-tuple-element.83.g_ref.right_ref), channel_id=1, source_target_pairs={{0,1},{1,0},{2,3},{3,2},{4,5},{5,4},{6,7},{7,6},{8,9},{9,8},{10,11... | collective-permute-start | bytes 4718600 | tf_op jit(solution)/shard_map/ppermute | solution.py:39
  572.5 31.1 %all-to-all-start.10 = ((bf16[4,128,2048]{2,1,0:T(8,128)(2,1)}), bf16[4,128,2048]{2,1,0:T(8,128)(2,1)S(1)}, u32[]{:S(2)}, u32[]{:S(2)}) async-start(bf16[4,128,2048]{2,1,0:T(8,128)(2,1)} %shard_map.234), calls=%async_computation.10 | async-start | bytes 4194304 | tf_op jit(solution)/shard_map/all_to_all | solution.py:43
  584.5 26.5 %collective-permute-start.28 = (bf16[4,128,384]{2,1,0:T(8,128)(2,1)}, bf16[4,128,384]{2,1,0:T(8,128)(2,1)S(1)}, u32[]{:S(2)}, u32[]{:S(2)}) collective-permute-start(bf16[4,128,384]{2,1,0:T(8,128)(2,1)} %get-tuple-element.102), channel_id=1, source_target_pairs={{0,4},{4,8},{8,12},{12,0},{1,5},{5,9},{9,13},{13,1},{2,6},{6,10},{... | collective-permute-start | bytes 1179656 | tf_op jit(solution)/shard_map/ppermute | solution.py:66
  585.9 26.6 %collective-permute-start.29 = (bf16[4,128,384]{2,1,0:T(8,128)(2,1)}, bf16[4,128,384]{2,1,0:T(8,128)(2,1)}, u32[]{:S(2)}, u32[]{:S(2)}) collective-permute-start(bf16[4,128,384]{2,1,0:T(8,128)(2,1)} %get-tuple-element.103), channel_id=1, source_target_pairs={{0,12},{4,0},{8,4},{12,8},{1,13},{5,1},{9,5},{13,9},{2,14},{6,2},{... | collective-permute-start | bytes 1179656 | tf_op jit(solution)/shard_map/ppermute | solution.py:66
  589.0 23.5 %collective-permute-start.30 = (bf16[4,128,384]{2,1,0:T(8,128)(2,1)}, bf16[4,128,384]{2,1,0:T(8,128)(2,1)}, u32[]{:S(2)}, u32[]{:S(2)}) collective-permute-start(bf16[4,128,384]{2,1,0:T(8,128)(2,1)} %get-tuple-element.104), channel_id=1, source_target_pairs={{0,8},{4,12},{8,0},{12,4},{1,9},{5,13},{9,1},{13,5},{2,10},{6,14},... | collective-permute-start | bytes 1179656 | tf_op jit(solution)/shard_map/ppermute | solution.py:66
  603.6 29.4 %collective-permute-start.22 = (bf16[4,128,384]{2,1,0:T(8,128)(2,1)}, bf16[4,128,384]{2,1,0:T(8,128)(2,1)S(1)}, u32[]{:S(2)}, u32[]{:S(2)}) collective-permute-start(bf16[4,128,384]{2,1,0:T(8,128)(2,1)} %get-tuple-element.95), channel_id=1, source_target_pairs={{0,2},{2,64},{64,66},{66,0},{1,3},{3,65},{65,67},{67,1},{4,6},{6,6... | collective-permute-start | bytes 1179656 | tf_op jit(solution)/shard_map/ppermute | solution.py:66
  603.9 30.6 %collective-permute-start.23 = (bf16[4,128,384]{2,1,0:T(8,128)(2,1)}, bf16[4,128,384]{2,1,0:T(8,128)(2,1)S(1)}, u32[]{:S(2)}, u32[]{:S(2)}) collective-permute-start(bf16[4,128,384]{2,1,0:T(8,128)(2,1)} %get-tuple-element.96), channel_id=1, source_target_pairs={{0,66},{2,0},{64,2},{66,64},{1,67},{3,1},{65,3},{67,65},{4,70},{6,... | collective-permute-start | bytes 1179656 | tf_op jit(solution)/shard_map/ppermute | solution.py:66
  611.1 23.5 %collective-permute-start.24 = (bf16[4,128,384]{2,1,0:T(8,128)(2,1)}, bf16[4,128,384]{2,1,0:T(8,128)(2,1)S(1)}, u32[]{:S(2)}, u32[]{:S(2)}) collective-permute-start(bf16[4,128,384]{2,1,0:T(8,128)(2,1)} %get-tuple-element.97), channel_id=1, source_target_pairs={{0,64},{2,66},{64,0},{66,2},{1,65},{3,67},{65,1},{67,3},{4,68},{6,... | collective-permute-start | bytes 1179656 | tf_op jit(solution)/shard_map/ppermute | solution.py:66
  614.7 26.2 %collective-permute-start.31 = (bf16[128,384]{1,0:T(8,128)(2,1)}, bf16[128,384]{1,0:T(8,128)(2,1)S(1)}, u32[]{:S(2)}, u32[]{:S(2)}) collective-permute-start(bf16[128,384]{1,0:T(8,128)(2,1)} %get-tuple-element.106), channel_id=1, source_target_pairs={{0,2},{2,64},{64,66},{66,0},{1,3},{3,65},{65,67},{67,1},{4,6},{6,6... | collective-permute-start | bytes 294920 | tf_op jit(solution)/shard_map/ppermute | solution.py:66
  631.8 10.9 %collective-permute-start.32 = (bf16[128,384]{1,0:T(8,128)(2,1)}, bf16[128,384]{1,0:T(8,128)(2,1)S(1)}, u32[]{:S(2)}, u32[]{:S(2)}) collective-permute-start(bf16[128,384]{1,0:T(8,128)(2,1)} %get-tuple-element.107), channel_id=1, source_target_pairs={{0,66},{2,0},{64,2},{66,64},{1,67},{3,1},{65,3},{67,65},{4,70},{6,... | collective-permute-start | bytes 294920 | tf_op jit(solution)/shard_map/ppermute | solution.py:66
  632.9 9.7 %collective-permute-start.33 = (bf16[128,384]{1,0:T(8,128)(2,1)}, bf16[128,384]{1,0:T(8,128)(2,1)S(1)}, u32[]{:S(2)}, u32[]{:S(2)}) collective-permute-start(bf16[128,384]{1,0:T(8,128)(2,1)} %get-tuple-element.108), channel_id=1, source_target_pairs={{0,64},{2,66},{64,0},{66,2},{1,65},{3,67},{65,1},{67,3},{4,68},{6,... | collective-permute-start | bytes 294920 | tf_op jit(solution)/shard_map/ppermute | solution.py:66
  637.6 6.0 collective-permute-start.25
  638.4 6.1 collective-permute-start.26
  640.9 6.3 collective-permute-start.27
  (30 other events, 139.2 us)
Sparse Core Ops, SparseCore 0:
  78.1 144.0 all-gather.1
  429.6 114.0 reduce-scatter.1

commit v2 on v1

--- a/solution.py
+++ b/solution.py
@@ -15,7 +15,7 @@
 BLK_TOK = 128
 HID = 704
 HID_PAD = 768
-SHARED = 3 * HID_PAD + 256
+SHARED = 3 * HID_PAD
 
 eps = 1e-05
 rope_base = 10000.0
@@ -104,8 +104,7 @@
     out_t = jnp.transpose(out_ref[...])
     for j, h_ref in enumerate((h0_ref, h1_ref)):
         for part in range(3):
-            column = part * 256 + j * 128
-            h_ref[:128, part * 128 : (part + 1) * 128] = qkv_ref[:, column : column + 128]
+            h_ref[:128, part * 128 : (part + 1) * 128] = qkv_ref[part, :, j * 128 : (j + 1) * 128]
         h_ref[:128, 384:] = out_t[:, j * 128 : (j + 1) * 128]
     small_ref[...] = jnp.zeros_like(small_ref)
     small_ref[0:4, :128] = vectors_ref[...].astype(jnp.float32)
@@ -128,11 +127,10 @@
 
 
 def pack_hidden_kernel(gate_ref, up_ref, down_ref, rest_ref):
-    down = jnp.transpose(down_ref[...])
-    for i, weights in enumerate((gate_ref[...], up_ref[...], down)):
+    for i, ref in enumerate((gate_ref, up_ref, down_ref)):
         first = i * HID_PAD
         rest_ref[:, first + HID_PAD - 128 : first + HID_PAD] = jnp.zeros((128, 128), jnp.bfloat16)
-        rest_ref[:, first : first + HID] = weights
+        rest_ref[:, first : first + HID] = jnp.transpose(ref[...])
 
 
 def pack_hidden_call(gate, up, down):
@@ -174,6 +172,7 @@
     down_ref,
     out_ref,
     normed_ref,
+    unit_ref,
     x_cores,
 ):
     part = pl.program_id(1)
@@ -187,6 +186,7 @@
             normed = (unit * gain_ref[...] + shift_ref[...]).astype(jnp.bfloat16)
             if b < 4:
                 normed_ref[b] = normed
+                unit_ref[b] = unit.astype(jnp.bfloat16)
             for c in range(16):
                 column = pl.multiple_of((c // 2 + 8 * ((c + core) % 2)) * 128, 128)
                 x_cores[b * 128 : (b + 1) * 128, pl.ds(column, 128)] = normed[:, c * 128 : (c + 1) * 128]
@@ -257,9 +257,11 @@
         out_specs=[
             pl.BlockSpec((2, 1, 4, 5, 128, 128), lambda h, p: (0, h, 0, 0, 0, 0)),
             pl.BlockSpec((4, 128, D), lambda h, p: (0, 0, 0)),
+            pl.BlockSpec((4, 128, D), lambda h, p: (0, 0, 0)),
         ],
         out_shape=[
             jax.ShapeDtypeStruct((2, 2, 4, 5, 128, 128), jnp.bfloat16),
+            jax.ShapeDtypeStruct((4, 128, D), jnp.bfloat16),
             jax.ShapeDtypeStruct((4, 128, D), jnp.bfloat16),
         ],
         scratch_shapes=[pltpu.VMEM((640, D), jnp.bfloat16)],
@@ -314,10 +316,9 @@
         ring_ref[i] = grad.astype(jnp.bfloat16)
 
 
-def input_back_kernel(came_ref, tokens_ref, grad_ref, gain_ref, out_ref, gain_grad_ref, shift_grad_ref):
+def input_back_kernel(came_ref, tokens_ref, grad_ref, gain_ref, out_ref):
     values = tokens_ref[...].astype(jnp.float32)
-    grad, gain_grad_ref[...], shift_grad_ref[...] = back_through(came_ref, values, gain_ref[...])
-    out_ref[...] = grad_ref[...] + grad
+    out_ref[...] = grad_ref[...] + back_through(came_ref, values, gain_ref[...])[0]
 
 
 def mixed_kernel(came_ref, middle_ref, out_ref):
@@ -327,21 +328,24 @@
     out_ref[...] = total.astype(jnp.bfloat16)
 
 
-def shared_end_kernel(total_ref, gate_ref, up_ref, down_ref, out_ref):
-    total = total_ref[...].astype(jnp.float32)
+def shared_end_kernel(total_ref, gate_ref, up_ref, down_ref):
+    total = jnp.transpose(total_ref[...].astype(jnp.float32))
     for c in range(3):
         width = min(HID, c * 256 + 256) - c * 256
-        gate_ref[:, c * 256 : c * 256 + width] = total[:, c * 512 : c * 512 + width]
-        up_ref[:, c * 256 : c * 256 + width] = total[:, c * 512 + 256 : c * 512 + 256 + width]
-    down_ref[...] = jnp.transpose(total[:, 2 * HID_PAD : 3 * HID_PAD])[:HID]
-    out_ref[...] = jnp.transpose(total[:, 3 * HID_PAD :])
+        gate_ref[c * 256 : c * 256 + width] = total[c * 512 : c * 512 + width]
+        up_ref[c * 256 : c * 256 + width] = total[c * 512 + 256 : c * 512 + 256 + width]
+    down_ref[...] = total[2 * HID_PAD : 2 * HID_PAD + HID]
+
+
+def out_end_kernel(*refs):
+    refs[4][...] = jnp.transpose(sum(ref[...].astype(jnp.float32) for ref in refs[:4]))
 
 
 def joint_end_kernel(*refs):
     for j in range(2):
         total = sum(ref[...].astype(jnp.float32) for ref in refs[4 * j : 4 * j + 4])
         for part in range(3):
-            refs[8][:, part * 256 + j * 128 : part * 256 + j * 128 + 128] = total[:, part * 128 : part * 128 + 128]
+            refs[8][part, :, j * 128 : (j + 1) * 128] = total[:, part * 128 : part * 128 + 128]
 
 
 def ordered(core_ref, own, other):
@@ -352,21 +356,23 @@
 def project_kernel(core_ref, att_ref, own0_ref, own1_ref, oth0_ref, oth1_ref, out_ref):
     att = jnp.concatenate([att_ref[j, h].reshape(512, 128) for h in range(2) for j in range(2)], 1)
 
-    def rows(w0_ref, w1_ref):
+    def rows(w0_ref, w1_ref, yl):
         return jnp.concatenate(
-            [w for h in range(2) for w in (w0_ref[0, h, 0, :128], w1_ref[h, 0, 0])], 1
+            [w for h in range(2) for w in (w0_ref[0, h, yl, :128], w1_ref[h, yl, 0])], 1
         )
 
-    weights = ordered(core_ref, rows(own0_ref, own1_ref), rows(oth0_ref, oth1_ref))
-    out_ref[...] = mm(att, weights, 1, 1).astype(jnp.bfloat16).reshape(4, 128, 256)
+    weights = jnp.concatenate(
+        [ordered(core_ref, rows(own0_ref, own1_ref, yl), rows(oth0_ref, oth1_ref, yl)) for yl in range(2)], 0
+    )
+    out_ref[...] = mm(att, weights, 1, 1).astype(jnp.bfloat16).reshape(4, 128, 512)
 
 
 def project_call(core, att, weights):
-    first = pl.BlockSpec((1, 2, 1, 144, 128), lambda n: (n // 2, 0, n % 2, 0, 3))
-    second = pl.BlockSpec((2, 1, 1, 128, 128), lambda n: (0, n % 2, n // 2, 0, 3))
+    first = pl.BlockSpec((1, 2, 2, 144, 128), lambda n: (n, 0, 0, 0, 3))
+    second = pl.BlockSpec((2, 2, 1, 128, 128), lambda n: (0, 0, n, 0, 3))
     return pl.pallas_call(
         project_kernel,
-        grid=(8,),
+        grid=(4,),
         in_specs=[
             pl.BlockSpec(memory_space=pltpu.SMEM),
             pl.BlockSpec((2, 2, 4, 128, 128), lambda n: (0, 0, 0, 0, 0)),
@@ -375,7 +381,7 @@
             first,
             second,
         ],
-        out_specs=pl.BlockSpec((4, 128, 256), lambda n: (0, 0, n)),
+        out_specs=pl.BlockSpec((4, 128, 512), lambda n: (0, 0, n)),
         out_shape=jax.ShapeDtypeStruct((4, 128, D), jnp.bfloat16),
         compiler_params=pltpu.CompilerParams(vmem_limit_bytes=VMEM_LIMIT),
         cost_estimate=TINY,
@@ -454,7 +460,7 @@
     return pl.pallas_call(
         feed_forward_kernel,
         grid=(2, 3),
-        in_specs=[tokens, pl.BlockSpec((4, 128, D), lambda h, c: (0, 1, 0))] + weight,
+        in_specs=[tokens, tokens] + weight,
         out_specs=[
             pl.BlockSpec((1, 512, 256), lambda h, c: (h, 0, c)),
             pl.BlockSpec((1, 512, 512), lambda h, c: (h, 0, c)),
@@ -488,8 +494,8 @@
             out_ref[0, yl, z] = total[row : row + 128]
 
 
-def plane_grad_call(core, left, right, columns, before, first, shared=None):
-    left_block = pl.BlockSpec((4, 128, D), lambda n, h: (0, before, 0))
+def plane_grad_call(core, left, right, columns, first, shared=None):
+    left_block = pl.BlockSpec((4, 128, D), lambda n, h: (0, 0, 0))
     right_block = pl.BlockSpec((1, 512, 256), lambda n, h: (h, 0, n))
     extra = [] if shared is None else [shared]
     return pl.pallas_call(
@@ -534,21 +540,60 @@
                     outs[t][slot] = total[row : row + 128]
 
 
-def weight_grad_call(core, place, left, right, first, columns):
-    width = 256 if columns % 256 == 0 else 384
+def weight_grad_call(core, place, left, right, columns):
     smem = pl.BlockSpec(memory_space=pltpu.SMEM)
     left_block = pl.BlockSpec((4, 128, D), lambda n, h: (0, 0, 0))
-    right_block = pl.BlockSpec((1, 512, width), lambda n, h: (h, 0, first // width + n))
+    right_block = pl.BlockSpec((1, 512, 256), lambda n, h: (h, 0, n))
     return pl.pallas_call(
         weight_grad_kernel,
-        grid=(columns // width, 2),
+        grid=(columns // 256, 2),
         in_specs=[smem, smem, left_block, left_block, right_block, right_block],
-        out_specs=[pl.BlockSpec((4, 128, width), lambda n, h: (0, 0, n))] * 4,
+        out_specs=[pl.BlockSpec((4, 128, 256), lambda n, h: (0, 0, n))] * 4,
         out_shape=[jax.ShapeDtypeStruct((4, 128, columns), jnp.bfloat16)] * 4,
         scratch_shapes=[pltpu.VMEM((1024, 1024), jnp.bfloat16)],
         compiler_params=pltpu.CompilerParams(vmem_limit_bytes=VMEM_LIMIT),
         cost_estimate=TINY,
     )(core, place, *left, *right)
+
+
+def joint_grad_kernel(core_ref, place_ref, left_ref, left_other_ref, right_ref, right_other_ref, *refs):
+    outs, left_t = refs[:8], refs[8]
+    h = pl.program_id(0)
+
+    @pl.when(h == 0)
+    def _():
+        left_t[:, :512] = jnp.transpose(core_columns(left_ref, core_ref[0], 4))
+        left_t[:, 512:] = jnp.transpose(core_columns(left_other_ref, core_ref[0], 4))
+
+    right = jnp.concatenate([right_ref[0], right_other_ref[0]], 0)
+    total = mm(left_t[...], right).astype(jnp.bfloat16)
+    for z in range(4):
+        for yl in range(2):
+            row = (z * 2 + yl) * 128
+            chip = (h * 2 + yl) * 4 + z
+            for j in range(2):
+                step, slot = place_ref[2 * j, chip], place_ref[2 * j + 1, chip]
+                for t in range(4):
+
+                    @pl.when(step == t)
+                    def _():
+                        outs[4 * j + t][slot] = total[row : row + 128, j * 384 : j * 384 + 384]
+
+
+def joint_grad_call(core, places, left, right):
+    smem = pl.BlockSpec(memory_space=pltpu.SMEM)
+    left_block = pl.BlockSpec((4, 128, D), lambda h: (0, 0, 0))
+    right_block = pl.BlockSpec((1, 512, 768), lambda h: (h, 0, 0))
+    return pl.pallas_call(
+        joint_grad_kernel,
+        grid=(2,),
+        in_specs=[smem, smem, left_block, left_block, right_block, right_block],
+        out_specs=[pl.BlockSpec((4, 128, 384), lambda h: (0, 0, 0))] * 8,
+        out_shape=[jax.ShapeDtypeStruct((4, 128, 384), jnp.bfloat16)] * 8,
+        scratch_shapes=[pltpu.VMEM((1024, 1024), jnp.bfloat16)],
+        compiler_params=pltpu.CompilerParams(vmem_limit_bytes=VMEM_LIMIT),
+        cost_estimate=TINY,
+    )(core, jnp.concatenate(places, 0), *left, *right)
 
 
 def split_sum_kernel(place_ref, a_ref, b_ref, c_ref, d_ref, *out_refs):
@@ -580,6 +625,11 @@
     return jnp.stack([(z - lax.axis_index("z")) % 4, y])
 
 
+def plane_sum(parts):
+    parts = parts.reshape(2048, parts.shape[-1])
+    return lax.psum_scatter(parts, ("yh", "yl", "z"), scatter_dimension=0, tiled=True)
+
+
 def with_other(value):
     return value, swap_core(value)
 
@@ -598,66 +648,83 @@
     return [parts[0]] + [send(parts[t], axes, t) for t in (1, 3, 2)]
 
 
-def head_masks():
-    lane = lax.broadcasted_iota(jnp.int32, (128, 128), 1)
-    low = lane < HEAD_DIM
-    return low, low.astype(jnp.float32).astype(jnp.bfloat16), (~low).astype(jnp.float32).astype(jnp.bfloat16)
-
-
-def attend_kernel(lo_ref, r_ref, o32_ref, o16_ref, lse_ref, s_ref):
-    low, first_head, second_head = head_masks()
-    row = lax.broadcasted_iota(jnp.int32, (256, 128), 0) % 128
-    causal = row >= lax.broadcasted_iota(jnp.int32, (256, 128), 1)
-
-    def one_query(q, _):
-        query = r_ref[q, 4]
-        stacked = jnp.concatenate([query * first_head, query * second_head], 0)
-        lo = lo_ref[q]
-        chunks = (q + 18 - lo) // 2
-
-        def scores(kb):
-            return mm(stacked, r_ref[kb & 15, (kb >> 4) * 2], 1, 1)
-
-        def values(kb):
-            return r_ref[kb & 15, (kb >> 4) * 2 + 1]
-
-        s1 = jnp.where(causal, scores(q + 16), masked_score)
-        s0 = jnp.where(q + 15 >= lo, scores(q + 15), masked_score)
-        s_ref[0, :, :128] = s0
-        s_ref[0, :, 128:] = s1
-
-        def first(i, top):
-            kb = q + 15 - 2 * i
-            s1 = scores(kb + 1)
-            s0 = jnp.where(kb >= lo, scores(kb), masked_score)
-            s_ref[i, :, :128] = s0
-            s_ref[i, :, 128:] = s1
-            return jnp.maximum(top, jnp.maximum(s0, s1))
-
-        top = lax.fori_loop(1, chunks, first, jnp.maximum(s0, s1))
-        top = jnp.max(top, -1, keepdims=True)
-
-        def second(i, carry):
-            total, sums = carry
-            kb = q + 15 - 2 * i
-            p0 = jnp.exp(s_ref[i, :, :128] - top)
-            p1 = jnp.exp(s_ref[i, :, 128:] - top)
-            weights = jnp.concatenate([p0, p1], 1).astype(jnp.bfloat16)
-            value = jnp.concatenate([values(kb), values(kb + 1)], 0)
-            return total + p0 + p1, sums + mm(weights, value)
-
-        empty = jnp.zeros((256, 128), jnp.float32)
-        total, sums = lax.fori_loop(0, chunks, second, (empty, empty))
-        total = jnp.sum(total, -1, keepdims=True)
-        out = sums / total
-        out = jnp.where(low, out[:128], out[128:])
-        o32_ref[q] = out
-        o16_ref[q] = out.astype(jnp.bfloat16)
-        lse = jnp.broadcast_to(top + jnp.log(total), (256, 128))
-        lse_ref[q] = jnp.transpose(lse)[:1]
+def stack_heads(ref, *index):
+    first = (lax.broadcasted_iota(jnp.int32, (128, 128), 1) < HEAD_DIM).astype(jnp.float32).astype(jnp.bfloat16)
+    masks = (first, 1 - first)
+    return jnp.concatenate([ref[i] * mask for i in index for mask in masks], 0)
+
+
+def unstack_heads(values, block):
+    low = lax.broadcasted_iota(jnp.int32, (128, 128), 1) < HEAD_DIM
+    rows = values[block * 256 : block * 256 + 256]
+    return jnp.where(low, rows[:128], rows[128:])
+
+
+def key_blocks(r_ref, block, slot):
+    rows = []
+    for i in range(4):
+        index = jnp.maximum(block + i, 0)
+        rows.append(r_ref[index & 15, (index >> 4) * 2 + slot])
+    return jnp.concatenate(rows, 0)
+
+
+def masked(values, a, block, lo_a, lo_b, diagonal, fill):
+    key_row = lax.broadcasted_iota(jnp.int32, (128, 256), 0)
+    causal = key_row <= lax.broadcasted_iota(jnp.int32, (128, 256), 1) % 128
+    rows = []
+    for k in range(4):
+        parts = []
+        for i, lo in enumerate((lo_a, lo_b)):
+            mask = block + k >= lo
+            if diagonal and k == 2 + i:
+                mask = causal
+            part = values[k * 128 : k * 128 + 128, i * 256 : i * 256 + 256]
+            if diagonal and k == 3 and i == 0:
+                parts.append(jnp.full((128, 256), fill, jnp.float32))
+            else:
+                parts.append(jnp.where(mask, part, fill))
+        rows.append(jnp.concatenate(parts, 1))
+    return jnp.concatenate(rows, 0)
+
+
+def attend_kernel(lo_ref, r_ref, o32_ref, o16_ref, lse_ref):
+    def one_pair(a, _):
+        lo_a, lo_b = lo_ref[2 * a], lo_ref[2 * a + 1]
+        queries = stack_heads(r_ref, (2 * a, 4), (2 * a + 1, 4))
+
+        def scores(block, diagonal):
+            values = mm(key_blocks(r_ref, block, 0), queries, 1, 1)
+            return masked(values, a, block, lo_a, lo_b, diagonal, masked_score)
+
+        def add(scores, block, top):
+            weights = jnp.exp(scores - top)
+            sums = mm(key_blocks(r_ref, block, 1), weights.astype(jnp.bfloat16), 0, 0)
+            return jnp.sum(weights, 0, keepdims=True), sums
+
+        diagonal = scores(2 * a + 14, True)
+        top = jnp.max(diagonal, 0, keepdims=True)
+        total, sums = add(diagonal, 2 * a + 14, top)
+
+        def earlier(i, carry):
+            top, total, sums = carry
+            block = 2 * a + 14 - 4 * i
+            values = scores(block, False)
+            new = jnp.maximum(top, jnp.max(values, 0, keepdims=True))
+            scale = jnp.exp(top - new)
+            more, more_sums = add(values, block, new)
+            return new, total * scale + more, sums * scale + more_sums
+
+        steps = (2 * a + 21 - lo_a) // 4
+        top, total, sums = lax.fori_loop(1, steps, earlier, (top, total, sums))
+        out = jnp.transpose(sums / total)
+        for block in range(2):
+            rows = unstack_heads(out, block)
+            o32_ref[2 * a + block] = rows
+            o16_ref[2 * a + block] = rows.astype(jnp.bfloat16)
+        lse_ref[a] = top + jnp.log(total)
         return 0
 
-    lax.fori_loop(0, 16, one_query, 0)
+    lax.fori_loop(0, 8, one_pair, 0)
 
 
 def attend_call(lo, blocks):
@@ -669,62 +736,50 @@
         out_shape=[
             jax.ShapeDtypeStruct((16, 128, 128), jnp.float32),
             jax.ShapeDtypeStruct((16, 128, 128), jnp.bfloat16),
-            jax.ShapeDtypeStruct((16, 1, 256), jnp.float32),
-        ],
-        scratch_shapes=[pltpu.VMEM((8, 256, 256), jnp.float32)],
+            jax.ShapeDtypeStruct((8, 1, 512), jnp.float32),
+        ],
         compiler_params=pltpu.CompilerParams(vmem_limit_bytes=VMEM_LIMIT),
         cost_estimate=TINY,
     )(lo, blocks)
 
 
 def attend_back_kernel(lo_ref, r_ref, do_ref, o32_ref, lse_ref, out_ref, dk_ref, dv_ref):
-    low, first_head, second_head = head_masks()
-    key_row = lax.broadcasted_iota(jnp.int32, (128, 256), 0)
-    causal = key_row <= lax.broadcasted_iota(jnp.int32, (128, 256), 1) % 128
     dk_ref[...] = jnp.zeros_like(dk_ref)
     dv_ref[...] = jnp.zeros_like(dv_ref)
 
-    def one_query(q, _):
-        def stack(block):
-            return jnp.concatenate([block * first_head, block * second_head], 0)
-
-        queries = stack(r_ref[q, 4])
-        grads = stack(do_ref[q])
-        out = o32_ref[q]
-        delta = grads.astype(jnp.float32) * jnp.concatenate([out, out], 0)
-        delta = jnp.sum(jnp.transpose(delta), 0, keepdims=True)
-        lse = lse_ref[q]
-        lo = lo_ref[q]
-        chunks = (q + 18 - lo) // 2
-
-        def chunk(i, grad_query, mask1):
-            kb = q + 15 - 2 * i
-
-            def half(kb, mask):
-                key = r_ref[kb & 15, (kb >> 4) * 2]
-                value = r_ref[kb & 15, (kb >> 4) * 2 + 1]
-                weights = jnp.exp(mm(key, queries, 1, 1) - lse)
-                if mask is not None:
-                    weights = jnp.where(mask, weights, 0.0)
-                grad_scores = weights * (mm(value, grads, 1, 1) - delta)
-                grad_scores = grad_scores.astype(jnp.bfloat16)
-                dv_ref[kb] += mm(weights.astype(jnp.bfloat16), grads)
-                dk_ref[kb] += mm(grad_scores, queries)
-                return key, grad_scores
-
-            key1, grad1 = half(kb + 1, mask1)
-            key0, grad0 = half(kb, kb >= lo)
-            keys = jnp.concatenate([key0, key1], 0)
-            grad_scores = jnp.concatenate([grad0, grad1], 0)
-            return grad_query + mm(grad_scores, keys, 0, 0)
-
-        grad_query = chunk(0, jnp.zeros((256, 128), jnp.float32), causal)
-        grad_query = lax.fori_loop(1, chunks, lambda i, g: chunk(i, g, None), grad_query)
-        grad_query = jnp.where(low, grad_query[:128], grad_query[128:]) * score_scale
-        out_ref[q, 4] = grad_query.astype(jnp.bfloat16)
+    def one_pair(a, _):
+        lo_a, lo_b = lo_ref[2 * a], lo_ref[2 * a + 1]
+        queries = stack_heads(r_ref, (2 * a, 4), (2 * a + 1, 4))
+        grads = stack_heads(do_ref, 2 * a, 2 * a + 1)
+        out = jnp.concatenate([o32_ref[2 * a]] * 2 + [o32_ref[2 * a + 1]] * 2, 0)
+        delta = jnp.sum(jnp.transpose(grads.astype(jnp.float32) * out), 0, keepdims=True)
+        lse = lse_ref[a]
+
+        def blocks_back(block, diagonal):
+            keys, values = key_blocks(r_ref, block, 0), key_blocks(r_ref, block, 1)
+            weights = jnp.exp(mm(keys, queries, 1, 1) - lse)
+            weights = masked(weights, a, block, lo_a, lo_b, diagonal, 0.0)
+            grad_scores = (weights * (mm(values, grads, 1, 1) - delta)).astype(jnp.bfloat16)
+            grad_values = mm(weights.astype(jnp.bfloat16), grads)
+            grad_keys = mm(grad_scores, queries)
+            for k in range(4):
+                index, rows = jnp.maximum(block + k, 0), slice(k * 128, k * 128 + 128)
+                dv_ref[index] += grad_values[rows]
+                dk_ref[index] += grad_keys[rows]
+            return mm(grad_scores, keys, 0, 0)
+
+        def earlier(i, grad_query):
+            return grad_query + blocks_back(2 * a + 14 - 4 * i, False)
+
+        steps = (2 * a + 21 - lo_a) // 4
+        grad_query = blocks_back(2 * a + 14, True)
+        grad_query = lax.fori_loop(1, steps, earlier, grad_query)
+        for block in range(2):
+            rows = unstack_heads(grad_query, block) * score_scale
+            out_ref[2 * a + block, 4] = rows.astype(jnp.bfloat16)
         return 0
 
-    lax.fori_loop(0, 16, one_query, 0)
+    lax.fori_loop(0, 8, one_pair, 0)
 
     def finish(c, _):
         out_ref[c, 0] = dk_ref[c].astype(jnp.bfloat16)
@@ -809,37 +864,52 @@
     )(blocks, halo, *tables)
 
 
-def normed_back_kernel(core_ref, g_ref, own0_ref, own1_ref, oth0_ref, oth1_ref, out_ref):
+def normed_back_kernel(
+    core_ref, g_ref, unit_ref, own0_ref, own1_ref, oth0_ref, oth1_ref, out_ref, gain_grad_ref, shift_grad_ref
+):
     grads = jnp.concatenate([g_ref[0], g_ref[1]], 1)
 
-    def rows(w0_ref, w1_ref):
+    def rows(w0_ref, w1_ref, yl):
         return jnp.concatenate(
-            [w[:, :384] for h in range(2) for w in (w0_ref[0, h, 0, :128], w1_ref[h, 0, 0])], 1
+            [w[:, :384] for h in range(2) for w in (w0_ref[0, h, yl, :128], w1_ref[h, yl, 0])], 1
         )
 
-    weights = ordered(core_ref, rows(own0_ref, own1_ref), rows(oth0_ref, oth1_ref))
-    out_ref[...] = mm(grads, weights, 1, 1).astype(jnp.bfloat16).reshape(4, 128, 256)
-
-
-def normed_back_call(core, grad_joint, weights):
-    first = pl.BlockSpec((1, 2, 1, 144, 512), lambda n: (n // 2, 0, n % 2, 0, 0))
-    second = pl.BlockSpec((2, 1, 1, 128, 512), lambda n: (0, n % 2, n // 2, 0, 0))
+    weights = jnp.concatenate(
+        [ordered(core_ref, rows(own0_ref, own1_ref, yl), rows(oth0_ref, oth1_ref, yl)) for yl in range(2)], 0
+    )
+    total = mm(grads, weights, 1, 1)
+    out_ref[...] = total.astype(jnp.bfloat16).reshape(4, 128, 512)
+    unit = unit_ref[...].reshape(512, 512).astype(jnp.float32)
+    gain_grad_ref[...] = jnp.sum(total * unit, 0, keepdims=True)
+    shift_grad_ref[...] = jnp.sum(total, 0, keepdims=True)
+
+
+def normed_back_call(core, grad_joint, unit, weights):
+    first = pl.BlockSpec((1, 2, 2, 144, 512), lambda n: (n, 0, 0, 0, 0))
+    second = pl.BlockSpec((2, 2, 1, 128, 512), lambda n: (0, 0, n, 0, 0))
+    ring = pl.BlockSpec((4, 128, 512), lambda n: (0, 0, n))
+    vector = pl.BlockSpec((1, 512), lambda n: (0, n))
     return pl.pallas_call(
         normed_back_kernel,
-        grid=(8,),
+        grid=(4,),
         in_specs=[
             pl.BlockSpec(memory_space=pltpu.SMEM),
             pl.BlockSpec((2, 512, 768), lambda n: (0, 0, 0)),
+            ring,
             first,
             second,
             first,
             second,
         ],
-        out_specs=pl.BlockSpec((4, 128, 256), lambda n: (0, 0, n)),
-        out_shape=jax.ShapeDtypeStruct((4, 128, D), jnp.bfloat16),
-        compiler_params=pltpu.CompilerParams(vmem_limit_bytes=VMEM_LIMIT),
-        cost_estimate=TINY,
-    )(core, grad_joint, *weights)
+        out_specs=[ring, vector, vector],
+        out_shape=[
+            jax.ShapeDtypeStruct((4, 128, D), jnp.bfloat16),
+            jax.ShapeDtypeStruct((1, D), jnp.float32),
+            jax.ShapeDtypeStruct((1, D), jnp.float32),
+        ],
+        compiler_params=pltpu.CompilerParams(vmem_limit_bytes=VMEM_LIMIT),
+        cost_estimate=TINY,
+    )(core, grad_joint, unit, *weights)
 
 
 def local(
@@ -862,14 +932,15 @@
 
     core = lax.axis_index("k").reshape(1)
     vectors = jnp.stack([ln1_gain, ln1_shift, ln2_gain, ln2_shift])
-    first_pair, second_pair = pack_joint_call(w_qkv.reshape(128, 768), w_out, vectors, b_qkv)
-    ring = ring_gather(jnp.concatenate([tokens, cotangent], 0))
+    first_pair, second_pair = pack_joint_call(w_qkv.transpose(1, 0, 2), w_out, vectors, b_qkv)
+    ring = ring_gather(tokens)
     own0 = gather(gather(first_pair, Y), ("z",)).reshape(4, 2, 2, 144, 512)
     own1 = gather(gather(second_pair, ("z",)), Y).reshape(2, 2, 4, 128, 512)
     own0 = after(own0, ring)
     weights = (own0, own1, swap_core(own0), swap_core(own1))
-    rest = pack_hidden_call(w_gate, w_up, w_down)
-    rest = after(rest, own0, own1)
+    before = lax.ppermute(ring[3], ("yh",), [(0, 1)])
+    rest = pack_hidden_call(w_gate.T, w_up.T, w_down)
+    rest = after(rest, own0, own1, before)
     rest = lax.all_gather(rest, PLANE, axis=0, tiled=True).reshape(2, D, 3 * HID_PAD)
 
     small = jnp.stack([own0[:, :, :, 128:, :128], weights[2][:, :, :, 128:, :128]])
@@ -887,9 +958,12 @@
     first_query = half * 64 + (blk % 4) * 16
     lo = lax.dynamic_slice(first_block, (first_query,), (16,)) - (first_query - 16)
 
-    before = lax.ppermute(ring[3, :128], ("yh",), [(0, 1)])
-    payload, normed_one = qkv_call(core, ring, before, gain_one, shift_one, weights, bias, tables)
-    blocks = exchange(payload.reshape(16, 5, 128, 128), BLK)
+    payload, normed_one, unit_one = qkv_call(
+        core, ring, before, gain_one, shift_one, weights, bias, tables
+    )
+    cot, payload = lax.optimization_barrier((cotangent, payload))
+    ring_cot = gather(cot, ("x",))
+    blocks = after(exchange(payload.reshape(16, 5, 128, 128), BLK), ring_cot)
     att32, att16, lse = attend_call(lo, blocks)
     attended = exchange(att16, BLK).reshape(2, 2, 4, 128, 128)
     came = exchange(project_call(core, attended, weights), ("x",))
@@ -901,8 +975,8 @@
     )
 
     ring_two = exchange(normed_two, ("x",))
-    active, grad_gu, ring_grad, ring_out = feed_forward_call(ring_two, ring, rest)
-    shared = plane_grad_call(core, with_other(ring), with_other(active), HID_PAD, 1, 2 * HID_PAD)
+    active, grad_gu, ring_grad, ring_out = feed_forward_call(ring_two, ring_cot, rest)
+    shared = plane_grad_call(core, with_other(ring_cot), with_other(active), HID_PAD, 2 * HID_PAD)
     came = after(exchange(ring_grad, ("x",)), shared)
     grad_middle, ring_branch, grad_gain_two, grad_shift_two = whole_call(
         middle_back_kernel,
@@ -912,56 +986,43 @@
         cotangent,
         gain_two,
     )
-    shared = plane_grad_call(
-        core, with_other(ring_two), with_other(grad_gu), 2 * HID_PAD, 0, 0, shared
-    )
+    shared = plane_grad_call(core, with_other(ring_two), with_other(grad_gu), 2 * HID_PAD, 0, shared)
     ring_branch = after(exchange(ring_branch, ("x",)), shared)
     grad_att = project_back_call(core, ring_branch, weights).reshape(16, 128, 128)
-    attended = attended.transpose(1, 2, 3, 0, 4).reshape(2, 512, 256)
-    shared = plane_grad_call(
-        core, with_other(ring_branch), with_other(attended), 256, 0, 3 * HID_PAD, shared
-    )
-    shared = lax.psum_scatter(
-        shared.reshape(2048, SHARED), ("yh", "yl", "z"), scatter_dimension=0, tiled=True
-    )
+    attended_pair = with_other(attended.transpose(1, 2, 3, 0, 4).reshape(2, 512, 256))
+    shared = plane_sum(after(shared, ring_branch))
+    branch_pair = with_other(after(ring_branch, grad_att))
     grad_att = exchange(grad_att, BLK)
 
-    out_came = exchange(after(ring_out, grad_att), ("x",))
+    mixed_came = exchange(after(ring_out, grad_att), ("x",))
     back = attend_back_call(lo, blocks, grad_att, att32, lse)
     mixed = whole_call(
-        mixed_kernel, jax.ShapeDtypeStruct((128, D), jnp.bfloat16), after(out_came, back), middle
-    )
+        mixed_kernel, jax.ShapeDtypeStruct((128, D), jnp.bfloat16), after(mixed_came, back), middle
+    )
+    places = (chip_places(True), chip_places(False))
+    out_parts = weight_grad_call(core, places[1], after(branch_pair, back), attended_pair, 256)
+    out_came = first_send(out_parts, False)
     back = exchange(back, BLK).reshape(2, 2, 4, 5, 128, 128)
     back = after(back, mixed)
+    out_came = second_send(first_sum(after(out_came, back), False), False)
     halo_back = lax.ppermute(back[:, :, 0, :2], ("yh",), [(1, 0)])
     grad_joint, grad_bias = turn_back_call(back, halo_back, tables)
-    ring_one = normed_back_call(core, grad_joint, weights)
-    places = (chip_places(True), chip_places(False))
-    joint_left, joint_right = with_other(normed_one), with_other(grad_joint)
-    pair_parts = [
-        weight_grad_call(core, places[j], joint_left, joint_right, j * 384, 384) for j in range(2)
-    ]
-    pair_came = [first_send(part, j == 0) for j, part in enumerate(pair_parts)]
-    came = after(exchange(ring_one, ("x",)), pair_parts[0][0], pair_parts[1][0])
-    input_grad, grad_gain_one, grad_shift_one = whole_call(
-        input_back_kernel,
-        [token_shape, vector_shape, vector_shape],
-        came,
-        tokens,
-        grad_middle,
-        gain_one,
-    )
+    ring_one, grad_gain_one, grad_shift_one = normed_back_call(core, grad_joint, unit_one, weights)
+    joint_left, joint_right = after((with_other(normed_one), with_other(grad_joint)), out_came[0])
+    parts = joint_grad_call(core, places, joint_left, joint_right)
+    pair_came = [first_send(parts[4 * j : 4 * j + 4], j == 0) for j in range(2)]
     pair_came = [second_send(first_sum(part, j == 0), j == 0) for j, part in enumerate(pair_came)]
+    came = after(exchange(ring_one, ("x",)), pair_came[0][0], pair_came[1][0])
+    input_grad = whole_call(input_back_kernel, token_shape, came, tokens, grad_middle, gain_one)
 
     def shape(*dims):
         return jax.ShapeDtypeStruct(dims, jnp.float32)
 
-    grad_gate, grad_up, grad_down, grad_out = whole_call(
-        shared_end_kernel,
-        [shape(128, HID), shape(128, HID), shape(HID, 128), shape(256, 128)],
-        after(shared, input_grad),
-    )
-    grad_qkv = whole_call(joint_end_kernel, shape(128, 768), *pair_came[0], *pair_came[1])
+    grad_gate, grad_up, grad_down = whole_call(
+        shared_end_kernel, [shape(HID, 128)] * 3, after(shared, input_grad)
+    )
+    grad_out = whole_call(out_end_kernel, shape(256, 128), *after(out_came, input_grad))
+    grad_qkv = whole_call(joint_end_kernel, shape(3, 128, 256), *pair_came[0], *pair_came[1])
 
     norms = jnp.concatenate([grad_gain_one, grad_shift_one, grad_gain_two, grad_shift_two], 0)
     norms = norms.reshape(4, 2, 4, 16, 16).transpose(1, 2, 3, 0, 4).reshape(2, 4, 16, 64)
@@ -969,7 +1030,7 @@
     plane = jnp.arange(4).reshape(1, 4, 1, 1) == lax.axis_index("x")
     biases = jnp.where(plane, biases, 0.0)
     sums = jnp.concatenate([norms, biases, jnp.zeros((2, 4, 16, 16), jnp.float32)], 3)
-    sums = jnp.sum(exchange(sums.reshape(128, 128), AXES), 0)
+    sums = jnp.sum(exchange(after(sums.reshape(128, 128), came), AXES), 0)
     norms = sums[:64].reshape(4, 16)
 
     return (
@@ -977,13 +1038,13 @@
         input_grad,
         norms[0],
         norms[1],
-        grad_qkv.reshape(128, 3, 256),
+        grad_qkv.transpose(1, 0, 2),
         sums[64:112].reshape(3, 16),
         grad_out,
         norms[2],
         norms[3],
-        grad_gate,
-        grad_up,
+        grad_gate.T,
+        grad_up.T,
         grad_down,
     )
 

time: 675 us -> 618 us (0.916)
  blocking collectives: 95.6 us -> 41.4 us
  starting transfers between devices: 94.3 us -> 107 us
  Pallas kernels: 192 us -> 182 us
    all_to_all x4 -> x2, blocking collectives: 95.6 us -> 41.4 us  [exchange(): return lax.all_to_all(parts, axes, 0, 0, tiled=True)]
    ppermute x24 -> x33, waiting for transfers between devices: 26.2 us -> 54.3 us  [send(): return lax.ppermute(value, axes, [(i, (i + step) % 4) for i in range(4)])]
    all_to_all x8 -> x10, waiting for transfers between devices: 170 us -> 152 us  [exchange(): return lax.all_to_all(parts, axes, 0, 0, tiled=True)]
    ppermute x24 -> x33, starting transfers between devices: 34.1 us -> 50.7 us  [send(): return lax.ppermute(value, axes, [(i, (i + step) % 4) for i in range(4)])]
    ppermute x1, waiting for transfers between devices: 18.4 us -> 5.86 us  [local(): before = lax.ppermute(ring[3], ('yh',), [(0, 1)])]
    dynamic_update_slice x16 -> x20, local copies, waits for them, and re-layouts: 0.47 us -> 10.2 us  [gather(): buffer = lax.dynamic_update_index_in_dim(buffer, piece, (me - step) % 4, 0)]
    unnamed x70 -> x90, local copies, waits for them, and re-layouts: 16.2 us -> 9.23 us
    pallas_call x3 -> x2, Pallas kernels: 30.2 us -> 24.7 us  [plane_grad_call(): pl.pallas_call(plane_grad_kernel, grid=(columns // 256, 2), in_specs=[pl....]
  transfers between devices with their start and end apart: 46 -> 57, of which waited for: 19 -> 23; matrix products, arithmetic and copies ran while one was open for 4% -> 5% of each run, Pallas kernels for 27% -> 29%
where the time goes in v2:
time: 618 us; the launch traced here: 610 us
  waiting for transfers between devices  222 us (36%)
  Pallas kernels  182 us (29%)
  starting transfers between devices  107 us (17%)
  blocking collectives  41.4 us (7%)
  local copies, waits for them, and re-layouts  36.3 us (6%)
  between operations  15.6 us (3%)
    all_to_all x10, waiting for transfers between devices, exchange(): return lax.all_to_all(parts, axes, 0, 0, tiled=True)  152 us
    ppermute x33, waiting for transfers between devices, send(): return lax.ppermute(value, axes, [(i, (i + step) % 4) for i in range(4)])  54.3 us
    ppermute x33, starting transfers between devices, send(): return lax.ppermute(value, axes, [(i, (i + step) % 4) for i in range(4)])  50.7 us
    all_to_all x10, starting transfers between devices, exchange(): return lax.all_to_all(parts, axes, 0, 0, tiled=True)  46.8 us
    all_to_all x2, blocking collectives, exchange(): return lax.all_to_all(parts, axes, 0, 0, tiled=True)  41.4 us
    pallas_call x1, Pallas kernels, feed_forward_call(): pl.pallas_call(feed_forward_kernel, grid=(2, 3), in_specs=[tokens, tokens...  37.8 us
    pallas_call x2, Pallas kernels, plane_grad_call(): pl.pallas_call(plane_grad_kernel, grid=(columns // 256, 2), in_specs=[pl....  24.7 us
    pallas_call x8, Pallas kernels, whole_call(): pl.pallas_call(kernel, in_specs=[vmem] * len(operands), out_specs=jax.tre...  23.7 us
  transfers between devices with their start and end apart: 57, of which 23 were waited for; matrix products, arithmetic and copies ran while one was open for 5% of the time, Pallas kernels for 29%

profile of v2, /device:TPU:0, one launch (start us, length us, event | category | flops | bytes accessed | tf_op | source)
XLA Modules:
  0.0 610.0 jit_solution(2386579055510064034)
XLA Ops:
  19.4 2.6 broadcast_in_dim.137
  22.0 4.6 all-to-all-start
  41.1 7.6 %collective-permute-done.11 = bf16[4,128,512]{2,1,0:T(8,128)(2,1)S(1)} collective-permute-done((bf16[4,128,512]{2,1,0:T(8,128)(2,1)S(1)}, bf16[4,128,512]{2,1,0:T(8,128)(2,1)S(1)}, u32[]{:S(2)}, u32[]{:S(2)}) %collective-permute-start.11) | collective-permute-done | bytes 524320 | tf_op jit(solution)/shard_map/ppermute | solution.py:66
  51.3 5.3 collective-permute-done.12
  59.4 4.7 collective-permute-start
  66.4 5.9 collective-permute-done.before_ref
  80.2 15.1 %shard_map.221 = (bf16[2,2,4,5,128,128]{5,4,3,2,1,0:T(8,128)(2,1)}, bf16[4,128,2048]{2,1,0:T(8,128)(2,1)}, bf16[4,128,2048]{2,1,0:T(8,128)(2,1)}) custom-call(s32[1]{0:T(128)} %bitcast.core_ref, bf16[4,128,2048]{2,1,0:T(8,128)(2,1)} %all-to-all-done.x_ref, bf16[128,2048]{1,0:T(8,128)(2,1)} %collective-permute-done.before_ref, f32[1,2048]{1,0:T(1,128)} %bitcast.119, ...), custom_call_target="tpu_custom_call" | custom-call | flops 1 | bytes 1 | tf_op jit(solution)/shard_map/pallas_call | solution.py:239
  95.3 3.9 all-to-all-start.1
  107.1 7.8 %collective-permute-done.15 = bf16[128,2048]{1,0:T(8,128)(2,1)} collective-permute-done((bf16[128,2048]{1,0:T(8,128)(2,1)S(1)}, bf16[128,2048]{1,0:T(8,128)(2,1)}, u32[]{:S(2)}, u32[]{:S(2)}) %collective-permute-start.15) | collective-permute-done | bytes 524320 | tf_op jit(solution)/shard_map/ppermute | solution.py:66
  116.8 9.1 %collective-permute-done.16 = bf16[128,2048]{1,0:T(8,128)(2,1)S(1)} collective-permute-done((bf16[128,2048]{1,0:T(8,128)(2,1)S(1)}, bf16[128,2048]{1,0:T(8,128)(2,1)S(1)}, u32[]{:S(2)}, u32[]{:S(2)}) %collective-permute-start.16) | collective-permute-done | bytes 524320 | tf_op jit(solution)/shard_map/ppermute | solution.py:66
  127.7 33.3 %all-to-all-done.1.r_ref = bf16[16,5,128,128]{3,2,1,0:T(8,128)(2,1)S(1)} async-done(((bf16[16,5,128,128]{3,2,1,0:T(8,128)(2,1)}), bf16[16,5,128,128]{3,2,1,0:T(8,128)(2,1)S(1)}, u32[]{:S(2)}, u32[]{:S(2)}) %all-to-all-start.1) | async-done | bytes 2621472 | tf_op jit(solution)/shard_map/all_to_all | solution.py:43
  162.6 15.5 %shard_map.222 = (f32[16,128,128]{2,1,0:T(8,128)}, bf16[16,128,128]{2,1,0:T(8,128)(2,1)}, f32[8,1,512]{2,1,0:T(1,128)}) custom-call(s32[16]{0:T(128)} %dynamic-slice_subtract_fusion.lo_ref, bf16[16,5,128,128]{3,2,1,0:T(8,128)(2,1)} %copy-done.1), custom_call_target="tpu_custom_call" | custom-call | flops 1 | bytes 1 | tf_op jit(solution)/shard_map/pallas_call | solution.py:732
  178.1 21.0 %all_to_all.64 = bf16[16,128,128]{2,1,0:T(8,128)(2,1)} all-to-all(bf16[16,128,128]{2,1,0:T(8,128)(2,1)} %get-tuple-element.98), channel_id=1, replica_groups=mesh['yh'=2,'x'=4,'z'=4,'yl'=2,'k'=2] {'z','yl','k'}, dimensions={0} | all-to-all | bytes 1048576 | tf_op jit(solution)/shard_map/all_to_all | solution.py:43
  199.1 5.1 shard_map.223
  204.2 4.0 all-to-all-start.3
  209.4 24.9 %all-to-all-done.3.came_ref = bf16[4,128,2048]{2,1,0:T(8,128)(2,1)S(1)} async-done(((bf16[4,128,2048]{2,1,0:T(8,128)(2,1)}), bf16[4,128,2048]{2,1,0:T(8,128)(2,1)S(1)}, u32[]{:S(2)}, u32[]{:S(2)}) %all-to-all-start.3) | async-done | bytes 2097184 | tf_op jit(solution)/shard_map/all_to_all | solution.py:43
  235.6 3.9 shard_map.224
  239.4 4.5 all-to-all-start.4
  244.2 24.9 %all-to-all-done.4.x_ref.left_ref = bf16[4,128,2048]{2,1,0:T(8,128)(2,1)} async-done(((bf16[4,128,2048]{2,1,0:T(8,128)(2,1)}), bf16[4,128,2048]{2,1,0:T(8,128)(2,1)}, u32[]{:S(2)}, u32[]{:S(2)}) %all-to-all-start.4) | async-done | bytes 2097184 | tf_op jit(solution)/shard_map/all_to_all | solution.py:43
  269.1 37.8 %shard_map.226 = (bf16[2,512,768]{2,1,0:T(8,128)(2,1)}, bf16[2,512,1536]{2,1,0:T(8,128)(2,1)}, bf16[4,128,2048]{2,1,0:T(8,128)(2,1)}, bf16[4,128,2048]{2,1,0:T(8,128)(2,1)}) custom-call(bf16[4,128,2048]{2,1,0:T(8,128)(2,1)} %all-to-all-done.4.x_ref.left_ref, bf16[4,128,2048]{2,1,0:T(8,128)(2,1)} %bitcast_dynamic-update-slice_fusion.4.cot_ref.left_ref, ...), custom_call_target="tpu_custom_call" | custom-call | flops 1 | bytes 1 | tf_op jit(solution)/shard_map/pallas_call | solution.py:460
  307.0 3.6 all-to-all-start.5
  311.3 9.4 %shard_map.227.refs_0_ = bf16[2,2,4,128,2304]{4,3,2,1,0:T(8,128)(2,1)} custom-call(s32[1]{0:T(128)} %bitcast.core_ref, bf16[4,128,2048]{2,1,0:T(8,128)(2,1)} %bitcast_dynamic-update-slice_fusion.4.cot_ref.left_ref, bf16[4,128,2048]{2,1,0:T(8,128)(2,1)} %collective-permute-done.18.left_other_ref, bf16[2,512,768]{2,1,0:T(8,128)(2,1)} %get-tuple-element.103.right_ref, ...), custom_call_target="tpu_custom_call" | custom-call | flops 1 | bytes 1 | tf_op jit(solution)/shard_map/pallas_call | solution.py:501
  320.7 17.2 %all-to-all-done.5.came_ref = bf16[4,128,2048]{2,1,0:T(8,128)(2,1)S(1)} async-done(((bf16[4,128,2048]{2,1,0:T(8,128)(2,1)}), bf16[4,128,2048]{2,1,0:T(8,128)(2,1)S(1)}, u32[]{:S(2)}, u32[]{:S(2)}) %all-to-all-start.5) | async-done | bytes 2097184 | tf_op jit(solution)/shard_map/all_to_all | solution.py:43
  339.1 4.8 shard_map.228
  344.0 3.6 all-to-all-start.6
  347.7 15.3 %shard_map.229 = bf16[2,2,4,128,2304]{4,3,2,1,0:T(8,128)(2,1)} custom-call(s32[1]{0:T(128)} %bitcast.core_ref, bf16[4,128,2048]{2,1,0:T(8,128)(2,1)} %all-to-all-done.4.x_ref.left_ref, bf16[4,128,2048]{2,1,0:T(8,128)(2,1)} %collective-permute-done.20.left_other_ref, ...), custom_call_target="tpu_custom_call", output_to_operand_aliasing={{}: (5, {})} | custom-call | flops 1 | bytes 1 | tf_op jit(solution)/shard_map/pallas_call | solution.py:501
  363.0 11.0 %all-to-all-done.6.grad_ref.left_ref = bf16[4,128,2048]{2,1,0:T(8,128)(2,1)S(1)} async-done(((bf16[4,128,2048]{2,1,0:T(8,128)(2,1)}), bf16[4,128,2048]{2,1,0:T(8,128)(2,1)S(1)}, u32[]{:S(2)}, u32[]{:S(2)}) %all-to-all-start.6) | async-done | bytes 2097184 | tf_op jit(solution)/shard_map/all_to_all | solution.py:43
  375.3 4.2 shard_map.230
  379.5 20.4 %all_to_all.65.do_ref = bf16[16,128,128]{2,1,0:T(8,128)(2,1)} all-to-all(bf16[16,128,128]{2,1,0:T(8,128)(2,1)} %bitcast.110), channel_id=1, replica_groups=mesh['yh'=2,'x'=4,'z'=4,'yl'=2,'k'=2] {'z','yl','k'}, dimensions={0} | all-to-all | bytes 1048576 | tf_op jit(solution)/shard_map/all_to_all | solution.py:43
  399.9 4.7 all-to-all-start.8
  404.7 19.9 %shard_map.231 = bf16[16,5,128,128]{3,2,1,0:T(8,128)(2,1)} custom-call(s32[16]{0:T(128)} %dynamic-slice_subtract_fusion.lo_ref, bf16[16,5,128,128]{3,2,1,0:T(8,128)(2,1)} %copy-done.1, bf16[16,128,128]{2,1,0:T(8,128)(2,1)} %all_to_all.65.do_ref, f32[16,128,128]{2,1,0:T(8,128)} %get-tuple-element.110.o32_ref, f32[8,1,512]{2,1,0:T(1,128)} %get-tuple-element.111.lse_ref), custom_call_target="tpu_custom_call" | custom-call | flops 1 | bytes 1 | tf_op jit(solution)/shard_map/pallas_call | solution.py:796
  424.6 5.7 all-to-all-done.8.came_ref
  430.3 4.5 all-to-all-start.9
  435.3 3.0 shard_map.232
  438.3 34.8 %all-to-all-done.9 = bf16[16,5,128,128]{3,2,1,0:T(8,128)(2,1)} async-done(((bf16[16,5,128,128]{3,2,1,0:T(8,128)(2,1)}), bf16[16,5,128,128]{3,2,1,0:T(8,128)(2,1)}, u32[]{:S(2)}, u32[]{:S(2)}) %all-to-all-start.9) | async-done | bytes 2621472 | tf_op jit(solution)/shard_map/all_to_all | solution.py:43
  475.5 9.5 %collective-permute-done.22.halo_ref = bf16[2,2,2,128,128]{4,3,2,1,0:T(8,128)(2,1)S(1)} collective-permute-done((bf16[2,2,2,128,128]{4,3,2,1,0:T(8,128)(2,1)S(1)}, bf16[2,2,2,128,128]{4,3,2,1,0:T(8,128)(2,1)S(1)}, u32[]{:S(2)}, u32[]{:S(2)}) %collective-permute-start.22) | collective-permute-done | bytes 262176 | tf_op jit(solution)/shard_map/ppermute | solution.py:1008
  485.7 3.7 shard_map.233
  490.9 8.4 %shard_map.234 = (bf16[4,128,2048]{2,1,0:T(8,128)(2,1)}, f32[1,2048]{1,0:T(1,128)}, f32[1,2048]{1,0:T(1,128)}) custom-call(s32[1]{0:T(128)} %bitcast.core_ref, bf16[2,512,768]{2,1,0:T(8,128)(2,1)} %get-tuple-element.132.g_ref.right_ref, bf16[4,128,2048]{2,1,0:T(8,128)(2,1)} %get-tuple-element.115.unit_ref, bf16[4,2,2,144,512]{4,3,2,1,0:T(8,128)(2,1)} %bitcast.106, ...), custom_call_target="tpu_custom_call" | custom-call | flops 1 | bytes 1 | tf_op jit(solution)/shard_map/pallas_call | solution.py:892
  499.2 4.5 all-to-all-start.10
  505.1 5.9 shard_map.235
  516.1 5.4 collective-permute-done.27.b_ref
  521.5 4.3 collective-permute-done.28.c_ref
  529.2 9.8 %shard_map.237 = (bf16[4,128,384]{2,1,0:T(8,128)(2,1)}, bf16[4,128,384]{2,1,0:T(8,128)(2,1)}, bf16[4,128,384]{2,1,0:T(8,128)(2,1)}, bf16[4,128,384]{2,1,0:T(8,12...) custom-call(s32[1]{0:T(128)} %bitcast.core_ref, ...), custom_call_target="tpu_custom_call" | custom-call | flops 1 | bytes 1 | tf_op jit(solution)/shard_map/pallas_call | solution.py:587
  548.0 5.4 collective-permute-done.33.b_ref
  553.4 5.6 collective-permute-done.34.c_ref
  570.1 9.0 %all-to-all-start.11 = ((f32[128,1,128]{2,1,0:T(1,128)}), f32[128,1,128]{2,1,0:T(1,128)S(1)}, u32[]{:S(2)}, u32[]{:S(2)}) async-start(f32[128,1,128]{2,1,0:T(1,128)} %copy.74), calls=%async_computation.11 | async-start | bytes 131072 | tf_op jit(solution)/shard_map/all_to_all | solution.py:43
  579.2 4.0 shard_map.240
  595.1 2.7 collective-permute-done.38.refs_3_
  (269 shorter events, 112.8 us)
Async XLA Ops:
  10.2 18.9 %collective-permute-start.8 = (bf16[128,512]{1,0:T(8,128)(2,1)}, bf16[128,512]{1,0:T(8,128)(2,1)S(1)}, u32[]{:S(2)}, u32[]{:S(2)}) collective-permute-start(bf16[128,512]{1,0:T(8,128)(2,1)} %get-tuple-element.93), channel_id=1, source_target_pairs={{0,4},{4,8},{8,12},{12,0},{1,5},{5,9},{9,13},{13,1},{2,6},{6,10},{... | collective-permute-start | bytes 393224 | tf_op jit(solution)/shard_map/ppermute | solution.py:66
  12.2 19.0 %collective-permute-start.9 = (bf16[128,512]{1,0:T(8,128)(2,1)}, bf16[128,512]{1,0:T(8,128)(2,1)S(1)}, u32[]{:S(2)}, u32[]{:S(2)}) collective-permute-start(bf16[128,512]{1,0:T(8,128)(2,1)} %get-tuple-element.93), channel_id=1, source_target_pairs={{0,12},{4,0},{8,4},{12,8},{1,13},{5,1},{9,5},{13,9},{2,14},{6,2},{... | collective-permute-start | bytes 393224 | tf_op jit(solution)/shard_map/ppermute | solution.py:66
  14.3 16.9 %collective-permute-start.10 = (bf16[128,512]{1,0:T(8,128)(2,1)}, bf16[128,512]{1,0:T(8,128)(2,1)S(1)}, u32[]{:S(2)}, u32[]{:S(2)}) collective-permute-start(bf16[128,512]{1,0:T(8,128)(2,1)} %get-tuple-element.93), channel_id=1, source_target_pairs={{0,8},{4,12},{8,0},{12,4},{1,9},{5,13},{9,1},{13,5},{2,10},{6,14},... | collective-permute-start | bytes 393224 | tf_op jit(solution)/shard_map/ppermute | solution.py:66
  16.2 20.8 %collective-permute-start.1 = (bf16[144,512]{1,0:T(8,128)(2,1)}, bf16[144,512]{1,0:T(8,128)(2,1)S(1)}, u32[]{:S(2)}, u32[]{:S(2)}) collective-permute-start(bf16[144,512]{1,0:T(8,128)(2,1)} %get-tuple-element.91), channel_id=1, source_target_pairs={{0,2},{2,64},{64,66},{66,0},{1,3},{3,65},{65,67},{67,1},{4,6},{6,6... | collective-permute-start | bytes 442376 | tf_op jit(solution)/shard_map/ppermute | solution.py:66
  17.8 19.6 %collective-permute-start.2 = (bf16[144,512]{1,0:T(8,128)(2,1)}, bf16[144,512]{1,0:T(8,128)(2,1)S(1)}, u32[]{:S(2)}, u32[]{:S(2)}) collective-permute-start(bf16[144,512]{1,0:T(8,128)(2,1)} %get-tuple-element.91), channel_id=1, source_target_pairs={{0,66},{2,0},{64,2},{66,64},{1,67},{3,1},{65,3},{67,65},{4,70},{6,... | collective-permute-start | bytes 442376 | tf_op jit(solution)/shard_map/ppermute | solution.py:66
  22.0 36.3 %all-to-all-start = ((bf16[4,128,2048]{2,1,0:T(8,128)(2,1)}), bf16[4,128,2048]{2,1,0:T(8,128)(2,1)}, u32[]{:S(2)}, u32[]{:S(2)}) async-start(bf16[4,128,2048]{2,1,0:T(8,128)(2,1)} %broadcast_in_dim.137), calls=%async_computation | async-start | bytes 4194304 | tf_op jit(solution)/shard_map/all_to_all | solution.py:43
  26.6 242.5 %all-gather.2.cloned.1.call-start = ((), (), s32[]{:S(2)}) async-start(), calls=%async_computation.13 | async-start | bytes 19464192 | tf_op jit(solution)/shard_map/all_gather | solution.py:944
  31.3 17.5 %collective-permute-start.11 = (bf16[4,128,512]{2,1,0:T(8,128)(2,1)S(1)}, bf16[4,128,512]{2,1,0:T(8,128)(2,1)S(1)}, u32[]{:S(2)}, u32[]{:S(2)}) collective-permute-start(bf16[4,128,512]{2,1,0:T(8,128)(2,1)S(1)} %bitcast_dynamic-update-slice_fusion.16), channel_id=1, source_target_pairs={{0,2},{2,64},{64,66},{66,0},{1,3},{3,65},{65,67},{67,1},{4,6},{6,6... | collective-permute-start | bytes 1572872 | tf_op jit(solution)/shard_map/ppermute | solution.py:66
  32.0 24.5 %collective-permute-start.12 = (bf16[4,128,512]{2,1,0:T(8,128)(2,1)S(1)}, bf16[4,128,512]{2,1,0:T(8,128)(2,1)S(1)}, u32[]{:S(2)}, u32[]{:S(2)}) collective-permute-start(bf16[4,128,512]{2,1,0:T(8,128)(2,1)S(1)} %bitcast_dynamic-update-slice_fusion.16), channel_id=1, source_target_pairs={{0,66},{2,0},{64,2},{66,64},{1,67},{3,1},{65,3},{67,65},{4,70},{6,... | collective-permute-start | bytes 1572872 | tf_op jit(solution)/shard_map/ppermute | solution.py:66
  37.0 20.5 %collective-permute-start.13 = (bf16[4,128,512]{2,1,0:T(8,128)(2,1)S(1)}, bf16[4,128,512]{2,1,0:T(8,128)(2,1)S(1)}, u32[]{:S(2)}, u32[]{:S(2)}) collective-permute-start(bf16[4,128,512]{2,1,0:T(8,128)(2,1)S(1)} %bitcast_dynamic-update-slice_fusion.16), channel_id=1, source_target_pairs={{0,64},{2,66},{64,0},{66,2},{1,65},{3,67},{65,1},{67,3},{4,68},{6,... | collective-permute-start | bytes 1572872 | tf_op jit(solution)/shard_map/ppermute | solution.py:66
  37.5 26.5 %collective-permute-start.4 = (bf16[4,144,512]{2,1,0:T(8,128)(2,1)S(1)}, bf16[4,144,512]{2,1,0:T(8,128)(2,1)}, u32[]{:S(2)}, u32[]{:S(2)}) collective-permute-start(bf16[4,144,512]{2,1,0:T(8,128)(2,1)S(1)} %bitcast_dynamic-update-slice_fusion.12), channel_id=1, source_target_pairs={{0,4},{4,8},{8,12},{12,0},{1,5},{5,9},{9,13},{13,1},{2,6},{6,10},{... | collective-permute-start | bytes 1769480 | tf_op jit(solution)/shard_map/ppermute | solution.py:66
  38.6 26.6 %collective-permute-start.5 = (bf16[4,144,512]{2,1,0:T(8,128)(2,1)S(1)}, bf16[4,144,512]{2,1,0:T(8,128)(2,1)S(1)}, u32[]{:S(2)}, u32[]{:S(2)}) collective-permute-start(bf16[4,144,512]{2,1,0:T(8,128)(2,1)S(1)} %bitcast_dynamic-update-slice_fusion.12), channel_id=1, source_target_pairs={{0,12},{4,0},{8,4},{12,8},{1,13},{5,1},{9,5},{13,9},{2,14},{6,2},{... | collective-permute-start | bytes 1769480 | tf_op jit(solution)/shard_map/ppermute | solution.py:66
  48.8 16.5 %collective-permute-start.6 = (bf16[4,144,512]{2,1,0:T(8,128)(2,1)S(1)}, bf16[4,144,512]{2,1,0:T(8,128)(2,1)}, u32[]{:S(2)}, u32[]{:S(2)}) collective-permute-start(bf16[4,144,512]{2,1,0:T(8,128)(2,1)S(1)} %bitcast_dynamic-update-slice_fusion.12), channel_id=1, source_target_pairs={{0,8},{4,12},{8,0},{12,4},{1,9},{5,13},{9,1},{13,5},{2,10},{6,14},... | collective-permute-start | bytes 1769480 | tf_op jit(solution)/shard_map/ppermute | solution.py:66
  59.4 12.9 %collective-permute-start = (bf16[128,2048]{1,0:T(8,128)(2,1)S(1)}, bf16[128,2048]{1,0:T(8,128)(2,1)}, u32[]{:S(2)}, u32[]{:S(2)}) collective-permute-start(bf16[128,2048]{1,0:T(8,128)(2,1)S(1)} %slice_bitcast_fusion), channel_id=1, source_target_pairs={{0,64},{1,65},{2,66},{3,67},{4,68},{5,69},{6,70},{7,71},{8,72},{9,... | collective-permute-start | bytes 1572872 | tf_op jit(solution)/shard_map/ppermute | solution.py:941
  95.3 65.7 %all-to-all-start.1 = ((bf16[16,5,128,128]{3,2,1,0:T(8,128)(2,1)}), bf16[16,5,128,128]{3,2,1,0:T(8,128)(2,1)S(1)}, u32[]{:S(2)}, u32[]{:S(2)}) async-start(bf16[16,5,128,128]{3,2,1,0:T(8,128)(2,1)} %bitcast.109), calls=%async_computation.1 | async-start | bytes 5242880 | tf_op jit(solution)/shard_map/all_to_all | solution.py:43
  99.3 15.6 %collective-permute-start.15 = (bf16[128,2048]{1,0:T(8,128)(2,1)S(1)}, bf16[128,2048]{1,0:T(8,128)(2,1)}, u32[]{:S(2)}, u32[]{:S(2)}) collective-permute-start(bf16[128,2048]{1,0:T(8,128)(2,1)S(1)} %copy-done.8), channel_id=1, source_target_pairs={{0,16},{16,32},{32,48},{48,0},{1,17},{17,33},{33,49},{49,1},{2,18}... | collective-permute-start | bytes 1572872 | tf_op jit(solution)/shard_map/ppermute | solution.py:66
  101.1 24.8 %collective-permute-start.16 = (bf16[128,2048]{1,0:T(8,128)(2,1)S(1)}, bf16[128,2048]{1,0:T(8,128)(2,1)S(1)}, u32[]{:S(2)}, u32[]{:S(2)}) collective-permute-start(bf16[128,2048]{1,0:T(8,128)(2,1)S(1)} %copy-done.8), channel_id=1, source_target_pairs={{0,48},{16,0},{32,16},{48,32},{1,49},{17,1},{33,17},{49,33},{2,50}... | collective-permute-start | bytes 1572872 | tf_op jit(solution)/shard_map/ppermute | solution.py:66
  103.2 23.6 %collective-permute-start.17 = (bf16[128,2048]{1,0:T(8,128)(2,1)S(1)}, bf16[128,2048]{1,0:T(8,128)(2,1)S(1)}, u32[]{:S(2)}, u32[]{:S(2)}) collective-permute-start(bf16[128,2048]{1,0:T(8,128)(2,1)S(1)} %copy-done.8), channel_id=1, source_target_pairs={{0,32},{16,48},{32,0},{48,16},{1,33},{17,49},{33,1},{49,17},{2,34}... | collective-permute-start | bytes 1572872 | tf_op jit(solution)/shard_map/ppermute | solution.py:66
  204.2 30.0 %all-to-all-start.3 = ((bf16[4,128,2048]{2,1,0:T(8,128)(2,1)}), bf16[4,128,2048]{2,1,0:T(8,128)(2,1)S(1)}, u32[]{:S(2)}, u32[]{:S(2)}) async-start(bf16[4,128,2048]{2,1,0:T(8,128)(2,1)} %shard_map.223), calls=%async_computation.3 | async-start | bytes 4194304 | tf_op jit(solution)/shard_map/all_to_all | solution.py:43
  239.4 29.7 %all-to-all-start.4 = ((bf16[4,128,2048]{2,1,0:T(8,128)(2,1)}), bf16[4,128,2048]{2,1,0:T(8,128)(2,1)}, u32[]{:S(2)}, u32[]{:S(2)}) async-start(bf16[4,128,2048]{2,1,0:T(8,128)(2,1)} %get-tuple-element.99), calls=%async_computation.4 | async-start | bytes 4194304 | tf_op jit(solution)/shard_map/all_to_all | solution.py:43
  243.9 67.4 %collective-permute-start.18 = (bf16[4,128,2048]{2,1,0:T(8,128)(2,1)}, bf16[4,128,2048]{2,1,0:T(8,128)(2,1)}, u32[]{:S(2)}, u32[]{:S(2)}) collective-permute-start(bf16[4,128,2048]{2,1,0:T(8,128)(2,1)} %bitcast_dynamic-update-slice_fusion.4.cot_ref.left_ref), channel_id=1, source_target_pairs={{0,1},{1,0},{2,3},{3,2},{4,5},{5,4},{6,7},{7,6},{8,9},{9,8},{10,11... | collective-permute-start | bytes 6291464 | tf_op jit(solution)/shard_map/ppermute | solution.py:39
  307.0 30.8 %all-to-all-start.5 = ((bf16[4,128,2048]{2,1,0:T(8,128)(2,1)}), bf16[4,128,2048]{2,1,0:T(8,128)(2,1)S(1)}, u32[]{:S(2)}, u32[]{:S(2)}) async-start(bf16[4,128,2048]{2,1,0:T(8,128)(2,1)} %get-tuple-element.102), calls=%async_computation.5 | async-start | bytes 4194304 | tf_op jit(solution)/shard_map/all_to_all | solution.py:43
  310.6 37.0 %collective-permute-start.21 = (bf16[2,512,1536]{2,1,0:T(8,128)(2,1)}, bf16[2,512,1536]{2,1,0:T(8,128)(2,1)}, u32[]{:S(2)}, u32[]{:S(2)}) collective-permute-start(bf16[2,512,1536]{2,1,0:T(8,128)(2,1)} %get-tuple-element.107.right_ref), channel_id=1, source_target_pairs={{0,1},{1,0},{2,3},{3,2},{4,5},{5,4},{6,7},{7,6},{8,9},{9,8},{10,11... | collective-permute-start | bytes 9437192 | tf_op jit(solution)/shard_map/ppermute | solution.py:39
  311.2 36.5 %collective-permute-start.20 = (bf16[4,128,2048]{2,1,0:T(8,128)(2,1)}, bf16[4,128,2048]{2,1,0:T(8,128)(2,1)}, u32[]{:S(2)}, u32[]{:S(2)}) collective-permute-start(bf16[4,128,2048]{2,1,0:T(8,128)(2,1)} %all-to-all-done.4.x_ref.left_ref), channel_id=1, source_target_pairs={{0,1},{1,0},{2,3},{3,2},{4,5},{5,4},{6,7},{7,6},{8,9},{9,8},{10,11... | collective-permute-start | bytes 6291464 | tf_op jit(solution)/shard_map/ppermute | solution.py:39
  344.0 30.1 %all-to-all-start.6 = ((bf16[4,128,2048]{2,1,0:T(8,128)(2,1)}), bf16[4,128,2048]{2,1,0:T(8,128)(2,1)S(1)}, u32[]{:S(2)}, u32[]{:S(2)}) async-start(bf16[4,128,2048]{2,1,0:T(8,128)(2,1)} %get-tuple-element.106), calls=%async_computation.6 | async-start | bytes 4194304 | tf_op jit(solution)/shard_map/all_to_all | solution.py:43
  347.6 253.0 %reduce-scatter.2.cloned.1.call-start = ((), (), s32[]{:S(2)}) async-start(), calls=%async_computation.14 | async-start | bytes 10027008 | tf_op jit(solution)/shard_map/reduce_scatter | solution.py:630
  399.9 30.3 %all-to-all-start.8 = ((bf16[4,128,2048]{2,1,0:T(8,128)(2,1)}), bf16[4,128,2048]{2,1,0:T(8,128)(2,1)}, u32[]{:S(2)}, u32[]{:S(2)}) async-start(bf16[4,128,2048]{2,1,0:T(8,128)(2,1)} %get-tuple-element.109), calls=%async_computation.8 | async-start | bytes 4194304 | tf_op jit(solution)/shard_map/all_to_all | solution.py:43
  430.3 42.9 %all-to-all-start.9 = ((bf16[16,5,128,128]{3,2,1,0:T(8,128)(2,1)}), bf16[16,5,128,128]{3,2,1,0:T(8,128)(2,1)}, u32[]{:S(2)}, u32[]{:S(2)}) async-start(bf16[16,5,128,128]{3,2,1,0:T(8,128)(2,1)} %shard_map.231), calls=%async_computation.9 | async-start | bytes 5242880 | tf_op jit(solution)/shard_map/all_to_all | solution.py:43
  434.7 69.6 %collective-permute-start.25 = (bf16[4,128,2048]{2,1,0:T(8,128)(2,1)S(1)}, bf16[4,128,2048]{2,1,0:T(8,128)(2,1)}, u32[]{:S(2)}, u32[]{:S(2)}) collective-permute-start(bf16[4,128,2048]{2,1,0:T(8,128)(2,1)S(1)} %copy-done.3), channel_id=1, source_target_pairs={{0,1},{1,0},{2,3},{3,2},{4,5},{5,4},{6,7},{7,6},{8,9},{9,8},{10,11... | collective-permute-start | bytes 6291464 | tf_op jit(solution)/shard_map/ppermute | solution.py:39
  435.1 94.1 %collective-permute-start.23 = (bf16[4,128,2048]{2,1,0:T(8,128)(2,1)}, bf16[4,128,2048]{2,1,0:T(8,128)(2,1)}, u32[]{:S(2)}, u32[]{:S(2)}) collective-permute-start(bf16[4,128,2048]{2,1,0:T(8,128)(2,1)} %get-tuple-element.130.left_ref), channel_id=1, source_target_pairs={{0,1},{1,0},{2,3},{3,2},{4,5},{5,4},{6,7},{7,6},{8,9},{9,8},{10,11... | collective-permute-start | bytes 6291464 | tf_op jit(solution)/shard_map/ppermute | solution.py:39
  474.2 10.8 %collective-permute-start.22 = (bf16[2,2,2,128,128]{4,3,2,1,0:T(8,128)(2,1)S(1)}, bf16[2,2,2,128,128]{4,3,2,1,0:T(8,128)(2,1)S(1)}, u32[]{:S(2)}, u32[]{:S(2)}) collective-permute-start(bf16[2,2,2,128,128]{4,3,2,1,0:T(8,128)(2,1)S(1)} %slice_bitcast_fusion.1), channel_id=1, source_target_pairs={{64,0},{65,1},{66,2},{67,3},{68,4},{69,5},{70,6},{71,7},{72,8},{73... | collective-permute-start | bytes 786440 | tf_op jit(solution)/shard_map/ppermute | solution.py:1008
  489.4 39.7 %collective-permute-start.24 = (bf16[2,512,768]{2,1,0:T(8,128)(2,1)}, bf16[2,512,768]{2,1,0:T(8,128)(2,1)}, u32[]{:S(2)}, u32[]{:S(2)}) collective-permute-start(bf16[2,512,768]{2,1,0:T(8,128)(2,1)} %get-tuple-element.132.g_ref.right_ref), channel_id=1, source_target_pairs={{0,1},{1,0},{2,3},{3,2},{4,5},{5,4},{6,7},{7,6},{8,9},{9,8},{10,11... | collective-permute-start | bytes 4718600 | tf_op jit(solution)/shard_map/ppermute | solution.py:39
  490.3 14.0 %collective-permute-start.26 = (bf16[2,512,256]{2,1,0:T(8,128)(2,1)S(1)}, bf16[2,512,256]{2,1,0:T(8,128)(2,1)S(1)}, u32[]{:S(2)}, u32[]{:S(2)}) collective-permute-start(bf16[2,512,256]{2,1,0:T(8,128)(2,1)S(1)} %reshape.369.right_ref), channel_id=1, source_target_pairs={{0,1},{1,0},{2,3},{3,2},{4,5},{5,4},{6,7},{7,6},{8,9},{9,8},{10,11... | collective-permute-start | bytes 1572872 | tf_op jit(solution)/shard_map/ppermute | solution.py:39
  499.2 70.1 %all-to-all-start.10 = ((bf16[4,128,2048]{2,1,0:T(8,128)(2,1)}), bf16[4,128,2048]{2,1,0:T(8,128)(2,1)}, u32[]{:S(2)}, u32[]{:S(2)}) async-start(bf16[4,128,2048]{2,1,0:T(8,128)(2,1)} %get-tuple-element.116), calls=%async_computation.10 | async-start | bytes 4194304 | tf_op jit(solution)/shard_map/all_to_all | solution.py:43
  512.1 13.6 %collective-permute-start.28 = (bf16[4,128,256]{2,1,0:T(8,128)(2,1)}, bf16[4,128,256]{2,1,0:T(8,128)(2,1)S(1)}, u32[]{:S(2)}, u32[]{:S(2)}) collective-permute-start(bf16[4,128,256]{2,1,0:T(8,128)(2,1)} %get-tuple-element.123), channel_id=1, source_target_pairs={{0,12},{4,0},{8,4},{12,8},{1,13},{5,1},{9,5},{13,9},{2,14},{6,2},{... | collective-permute-start | bytes 786440 | tf_op jit(solution)/shard_map/ppermute | solution.py:66
  514.2 12.2 %collective-permute-start.29 = (bf16[4,128,256]{2,1,0:T(8,128)(2,1)}, bf16[4,128,256]{2,1,0:T(8,128)(2,1)S(1)}, u32[]{:S(2)}, u32[]{:S(2)}) collective-permute-start(bf16[4,128,256]{2,1,0:T(8,128)(2,1)} %get-tuple-element.124), channel_id=1, source_target_pairs={{0,8},{4,12},{8,0},{12,4},{1,9},{5,13},{9,1},{13,5},{2,10},{6,14},... | collective-permute-start | bytes 786440 | tf_op jit(solution)/shard_map/ppermute | solution.py:66
  539.0 14.4 %collective-permute-start.33 = (bf16[4,128,384]{2,1,0:T(8,128)(2,1)}, bf16[4,128,384]{2,1,0:T(8,128)(2,1)S(1)}, u32[]{:S(2)}, u32[]{:S(2)}) collective-permute-start(bf16[4,128,384]{2,1,0:T(8,128)(2,1)} %get-tuple-element.140), channel_id=1, source_target_pairs={{0,4},{4,8},{8,12},{12,0},{1,5},{5,9},{9,13},{13,1},{2,6},{6,10},{... | collective-permute-start | bytes 1179656 | tf_op jit(solution)/shard_map/ppermute | solution.py:66
  540.5 18.5 %collective-permute-start.34 = (bf16[4,128,384]{2,1,0:T(8,128)(2,1)}, bf16[4,128,384]{2,1,0:T(8,128)(2,1)S(1)}, u32[]{:S(2)}, u32[]{:S(2)}) collective-permute-start(bf16[4,128,384]{2,1,0:T(8,128)(2,1)} %get-tuple-element.141), channel_id=1, source_target_pairs={{0,12},{4,0},{8,4},{12,8},{1,13},{5,1},{9,5},{13,9},{2,14},{6,2},{... | collective-permute-start | bytes 1179656 | tf_op jit(solution)/shard_map/ppermute | solution.py:66
  542.6 18.2 %collective-permute-start.35 = (bf16[4,128,384]{2,1,0:T(8,128)(2,1)}, bf16[4,128,384]{2,1,0:T(8,128)(2,1)S(1)}, u32[]{:S(2)}, u32[]{:S(2)}) collective-permute-start(bf16[4,128,384]{2,1,0:T(8,128)(2,1)} %get-tuple-element.142), channel_id=1, source_target_pairs={{0,8},{4,12},{8,0},{12,4},{1,9},{5,13},{9,1},{13,5},{2,10},{6,14},... | collective-permute-start | bytes 1179656 | tf_op jit(solution)/shard_map/ppermute | solution.py:66
  543.9 20.7 %collective-permute-start.30 = (bf16[4,128,384]{2,1,0:T(8,128)(2,1)}, bf16[4,128,384]{2,1,0:T(8,128)(2,1)S(1)}, u32[]{:S(2)}, u32[]{:S(2)}) collective-permute-start(bf16[4,128,384]{2,1,0:T(8,128)(2,1)} %get-tuple-element.135), channel_id=1, source_target_pairs={{0,2},{2,64},{64,66},{66,0},{1,3},{3,65},{65,67},{67,1},{4,6},{6,6... | collective-permute-start | bytes 1179656 | tf_op jit(solution)/shard_map/ppermute | solution.py:66
  545.6 20.7 %collective-permute-start.31 = (bf16[4,128,384]{2,1,0:T(8,128)(2,1)}, bf16[4,128,384]{2,1,0:T(8,128)(2,1)S(1)}, u32[]{:S(2)}, u32[]{:S(2)}) collective-permute-start(bf16[4,128,384]{2,1,0:T(8,128)(2,1)} %get-tuple-element.136), channel_id=1, source_target_pairs={{0,66},{2,0},{64,2},{66,64},{1,67},{3,1},{65,3},{67,65},{4,70},{6,... | collective-permute-start | bytes 1179656 | tf_op jit(solution)/shard_map/ppermute | solution.py:66
  553.4 12.9 %collective-permute-start.32 = (bf16[4,128,384]{2,1,0:T(8,128)(2,1)}, bf16[4,128,384]{2,1,0:T(8,128)(2,1)S(1)}, u32[]{:S(2)}, u32[]{:S(2)}) collective-permute-start(bf16[4,128,384]{2,1,0:T(8,128)(2,1)} %get-tuple-element.137), channel_id=1, source_target_pairs={{0,64},{2,66},{64,0},{66,2},{1,65},{3,67},{65,1},{67,3},{4,68},{6,... | collective-permute-start | bytes 1179656 | tf_op jit(solution)/shard_map/ppermute | solution.py:66
  559.0 24.1 %collective-permute-start.42 = (bf16[128,256]{1,0:T(8,128)(2,1)S(1)}, bf16[128,256]{1,0:T(8,128)(2,1)S(1)}, u32[]{:S(2)}, u32[]{:S(2)}) collective-permute-start(bf16[128,256]{1,0:T(8,128)(2,1)S(1)} %copy-done.43), channel_id=1, source_target_pairs={{0,2},{2,64},{64,66},{66,0},{1,3},{3,65},{65,67},{67,1},{4,6},{6,6... | collective-permute-start | bytes 196616 | tf_op jit(solution)/shard_map/ppermute | solution.py:66
  560.8 22.3 %collective-permute-start.43 = (bf16[128,256]{1,0:T(8,128)(2,1)S(1)}, bf16[128,256]{1,0:T(8,128)(2,1)S(1)}, u32[]{:S(2)}, u32[]{:S(2)}) collective-permute-start(bf16[128,256]{1,0:T(8,128)(2,1)S(1)} %copy-done.42), channel_id=1, source_target_pairs={{0,66},{2,0},{64,2},{66,64},{1,67},{3,1},{65,3},{67,65},{4,70},{6,... | collective-permute-start | bytes 196616 | tf_op jit(solution)/shard_map/ppermute | solution.py:66
  564.5 18.6 %collective-permute-start.44 = (bf16[128,256]{1,0:T(8,128)(2,1)S(1)}, bf16[128,256]{1,0:T(8,128)(2,1)S(1)}, u32[]{:S(2)}, u32[]{:S(2)}) collective-permute-start(bf16[128,256]{1,0:T(8,128)(2,1)S(1)} %copy-done.41), channel_id=1, source_target_pairs={{0,64},{2,66},{64,0},{66,2},{1,65},{3,67},{65,1},{67,3},{4,68},{6,... | collective-permute-start | bytes 196616 | tf_op jit(solution)/shard_map/ppermute | solution.py:66
  566.3 25.4 %collective-permute-start.39 = (bf16[128,384]{1,0:T(8,128)(2,1)}, bf16[128,384]{1,0:T(8,128)(2,1)S(1)}, u32[]{:S(2)}, u32[]{:S(2)}) collective-permute-start(bf16[128,384]{1,0:T(8,128)(2,1)} %get-tuple-element.155), channel_id=1, source_target_pairs={{0,2},{2,64},{64,66},{66,0},{1,3},{3,65},{65,67},{67,1},{4,6},{6,6... | collective-permute-start | bytes 294920 | tf_op jit(solution)/shard_map/ppermute | solution.py:66
  570.1 21.4 %all-to-all-start.11 = ((f32[128,1,128]{2,1,0:T(1,128)}), f32[128,1,128]{2,1,0:T(1,128)S(1)}, u32[]{:S(2)}, u32[]{:S(2)}) async-start(f32[128,1,128]{2,1,0:T(1,128)} %copy.74), calls=%async_computation.11 | async-start | bytes 131072 | tf_op jit(solution)/shard_map/all_to_all | solution.py:43
  583.2 11.8 %collective-permute-start.40 = (bf16[128,384]{1,0:T(8,128)(2,1)S(1)}, bf16[128,384]{1,0:T(8,128)(2,1)S(1)}, u32[]{:S(2)}, u32[]{:S(2)}) collective-permute-start(bf16[128,384]{1,0:T(8,128)(2,1)S(1)} %copy-done.37), channel_id=1, source_target_pairs={{0,66},{2,0},{64,2},{66,64},{1,67},{3,1},{65,3},{67,65},{4,70},{6,... | collective-permute-start | bytes 294920 | tf_op jit(solution)/shard_map/ppermute | solution.py:66
  (54 other events, 424.9 us)
Sparse Core Ops, SparseCore 0:
  72.4 142.6 all-gather.1
  374.2 106.8 reduce-scatter.1
